TPU v7x, 32 devices: a whole 2x2x4 slice. The times are simulated.
32 devices in a mesh: fsdp: 4 (over z), ctx: 4 (over x, core), tp: 2 (over y).
Axes of the slice: x: 2, y: 2, z: 4, core: 2. Of those that a mesh axis runs over, the one named last changes fastest.
Arguments:
- residual: bfloat16 [8192, 2048], P(('fsdp', 'ctx')), may hold values from -6 to 6
- cotangent: bfloat16 [8192, 2048], P(('fsdp', 'ctx')), may hold values from -6 to 6
- lengths: int32 [4, 4], P('fsdp'), may hold values from 1 to 1024, 2048 in all within a row
- token_order: int32 [4, 2048], P('fsdp'), may hold values from 0 to 2047, each once within a row
- norm_mixer: bfloat16 [2048], P(('fsdp', 'ctx')), may hold values from 0.5 to 1.5
- w_query: bfloat16 [2048, 2048], P(('fsdp', 'ctx'), 'tp'), may hold values from -0.125 to 0.125
- w_key: bfloat16 [2048, 2048], P(('fsdp', 'ctx'), 'tp'), may hold values from -0.125 to 0.125
- w_value: bfloat16 [2048, 4096], P(('fsdp', 'ctx'), 'tp'), may hold values from -0.125 to 0.125
- w_outgate: bfloat16 [2048, 4096], P(('fsdp', 'ctx'), 'tp'), may hold values from -0.125 to 0.125
- w_decay: bfloat16 [2048, 16], P(('fsdp', 'ctx'), 'tp'), may hold values from -0.125 to 0.125
- w_beta: bfloat16 [2048, 16], P(('fsdp', 'ctx'), 'tp'), may hold values from -0.125 to 0.125
- conv_query: bfloat16 [4, 2048], replicated, may hold values from -3 to 3
- conv_key: bfloat16 [4, 2048], replicated, may hold values from -3 to 3
- conv_value: bfloat16 [4, 4096], replicated, may hold values from -3 to 3
- decay_log: float32 [16], replicated, may hold values from -1.5 to 1
- decay_bias: float32 [16], replicated, may hold values from -4 to -1
- norm_head: bfloat16 [256], replicated, may hold values from 0.5 to 1.5
- w_output: bfloat16 [4096, 2048], P('tp', ('fsdp', 'ctx')), may hold values from -0.125 to 0.125
- norm_ffn: bfloat16 [2048], P(('fsdp', 'ctx')), may hold values from 0.5 to 1.5
- w_gate: bfloat16 [2048, 5632], P(('fsdp', 'ctx'), 'tp'), may hold values from -0.125 to 0.125
- w_up: bfloat16 [2048, 5632], P(('fsdp', 'ctx'), 'tp'), may hold values from -0.125 to 0.125
- w_down: bfloat16 [5632, 2048], P('tp', ('fsdp', 'ctx')), may hold values from -0.078125 to 0.078125
Outputs:
- output: bfloat16 [8192, 2048], P(('fsdp', 'ctx'))
- grad_input: bfloat16 [8192, 2048], P(('fsdp', 'ctx'))
- gnorm_mixer: float32 [2048], P(('fsdp', 'ctx'))
- gw_query: float32 [2048, 2048], P(('fsdp', 'ctx'), 'tp')
- gw_key: float32 [2048, 2048], P(('fsdp', 'ctx'), 'tp')
- gw_value: float32 [2048, 4096], P(('fsdp', 'ctx'), 'tp')
- gw_outgate: float32 [2048, 4096], P(('fsdp', 'ctx'), 'tp')
- gw_decay: float32 [2048, 16], P(('fsdp', 'ctx'), 'tp')
- gw_beta: float32 [2048, 16], P(('fsdp', 'ctx'), 'tp')
- gconv_query: float32 [4, 2048], replicated
- gconv_key: float32 [4, 2048], replicated
- gconv_value: float32 [4, 4096], replicated
- gdecay_log: float32 [16], replicated
- gdecay_bias: float32 [16], replicated
- gnorm_head: float32 [256], replicated
- gw_output: float32 [4096, 2048], P('tp', ('fsdp', 'ctx'))
- gnorm_ffn: float32 [2048], P(('fsdp', 'ctx'))
- gw_gate: float32 [2048, 5632], P(('fsdp', 'ctx'), 'tp')
- gw_up: float32 [2048, 5632], P(('fsdp', 'ctx'), 'tp')
- gw_down: float32 [5632, 2048], P('tp', ('fsdp', 'ctx'))
Inputs may be any that keep to these rules, and one draw needn't show every extreme that they name: Each row of lengths holds the lengths of the 4 sequences of one group; they sum to 2048. Each row of token_order is a permutation of the 2048 rows of one group.
All inputs are finite; a program needn't handle non-finite values.
Results may differ from a plain program's by a relative error of at most 0.017.
Values may be sent and summed in bfloat16 or wider, within the bound.
No kernel may reach another device: no remote copies, remote signals or barrier semaphores. Data moves between devices by JAX's collectives and lax.ppermute only.
A program may use at most 320 MiB of HBM per device.

v0:
```python
import jax
import jax.numpy as jnp
from jax import lax
from jax.sharding import PartitionSpec as P

SPAN = 64


EPS = 1e-06
HEAD_FLOOR = 0.01
ARITH_ACCURACY = lax.Precision.HIGHEST


def segment_ids(lengths_row, length):
    bounds = jnp.cumsum(lengths_row)[:-1]
    position = lax.broadcasted_iota(jnp.int32, (length, bounds.shape[0]), 0)
    return jnp.sum((position >= bounds[None, :]).astype(jnp.int32), axis=1)


def causal_conv(signal, kernel, segment):
    tap_count = kernel.shape[0]
    length = signal.shape[0]
    padded = jnp.concatenate(
        [jnp.zeros((tap_count - 1, signal.shape[1]), jnp.float32), signal], axis=0
    )
    seg_pad = jnp.concatenate([jnp.full((tap_count - 1,), -1, jnp.int32), segment])
    summed = kernel[0] * signal
    for offset in range(1, tap_count):
        begin_at = tap_count - 1 - offset
        keep_mask = (seg_pad[begin_at : begin_at + length] == segment).astype(jnp.float32)
        summed = summed + kernel[offset] * padded[begin_at : begin_at + length] * keep_mask[:, None]
    return summed


def span_step(memory_across_tiles, inputs):
    tile_of_probes, key_block, v_block, g_block, b_block, seg_block, seg_before = inputs
    block_width = seg_block.shape[0]
    running_total = jnp.cumsum(g_block, axis=-1)
    row_ids = lax.broadcasted_iota(jnp.int32, (block_width, block_width), 0)
    col_ids = lax.broadcasted_iota(jnp.int32, (block_width, block_width), 1)
    same_seg = seg_block[:, None] == seg_block[None, :]
    upto_mask = same_seg & (row_ids >= col_ids)
    below_mask = same_seg & (row_ids > col_ids)
    continue_state = (seg_block == seg_before).astype(jnp.float32)
    tail_mask = seg_block == seg_block[block_width - 1]
    spread = running_total[:, :, None] - running_total[:, None, :]
    decay_mat = jnp.where(upto_mask, jnp.exp(jnp.where(upto_mask, spread, 0.0)), 0.0)
    key_gram = jnp.einsum("hid,hjd->hij", key_block, key_block, precision=ARITH_ACCURACY)
    lower_mat = jnp.where(below_mask, b_block[:, :, None] * key_gram * decay_mat, 0.0)
    identity = jnp.eye(block_width, dtype=jnp.float32)
    nilpotent = -lower_mat
    inverse = identity + nilpotent
    powered = nilpotent
    for _ in range(block_width.bit_length() - 2):
        powered = jnp.einsum("hij,hjk->hik", powered, powered, precision=ARITH_ACCURACY)
        inverse = inverse + jnp.einsum("hij,hjk->hik", inverse, powered, precision=ARITH_ACCURACY)
    expansion_ratio = jnp.exp(running_total) * continue_state
    corrected_content = jnp.einsum(
        "hij,hjv->hiv", inverse, b_block[:, :, None] * v_block, precision=ARITH_ACCURACY
    )
    linear_coefficients = jnp.einsum(
        "hij,hjk->hik",
        inverse,
        (b_block * expansion_ratio)[:, :, None] * key_block,
        precision=ARITH_ACCURACY,
    )
    content_corrections = corrected_content - jnp.einsum(
        "vdk,vkz->vdz", linear_coefficients, memory_across_tiles, precision=ARITH_ACCURACY
    )
    scores = (
        jnp.einsum("hid,hjd->hij", tile_of_probes, key_block, precision=ARITH_ACCURACY) * decay_mat
    )
    tile_result_rows = jnp.einsum(
        "vdk,vkz->vdz",
        tile_of_probes * expansion_ratio[:, :, None],
        memory_across_tiles,
        precision=ARITH_ACCURACY,
    )
    tile_result_rows = tile_result_rows + jnp.einsum(
        "hij,hjv->hiv", scores, content_corrections, precision=ARITH_ACCURACY
    )
    decay_factor = jnp.where(
        tail_mask,
        jnp.exp(jnp.where(tail_mask, running_total[:, block_width - 1 :] - running_total, 0.0)),
        0.0,
    )
    memory_across_tiles = (
        jnp.exp(running_total[:, block_width - 1]) * continue_state[block_width - 1]
    )[:, None, None] * memory_across_tiles + jnp.einsum(
        "oln,olm->onm",
        key_block * decay_factor[:, :, None],
        content_corrections,
        precision=ARITH_ACCURACY,
    )
    return (memory_across_tiles, tile_result_rows)


def delta_rule(queries, key_act, values, logdecay, beta_gate, segment):
    length = segment.shape[0]
    block_count = length // SPAN

    def blocks(tensor):
        shaped = tensor.reshape((block_count, SPAN) + tensor.shape[1:])
        return jnp.swapaxes(shaped, 1, 2)

    seg_blocks = segment.reshape(block_count, SPAN)
    seg_before = jnp.concatenate([jnp.full((1,), -1, jnp.int32), seg_blocks[:-1, SPAN - 1]])
    initial = jnp.zeros((queries.shape[1], queries.shape[2], values.shape[2]), jnp.float32)
    final_state, outputs = lax.scan(
        jax.checkpoint(span_step),
        initial,
        (
            blocks(queries),
            blocks(key_act),
            blocks(values),
            blocks(logdecay),
            blocks(beta_gate),
            seg_blocks,
            seg_before,
        ),
    )
    return jnp.swapaxes(outputs, 1, 2).reshape(length, queries.shape[1], values.shape[2])


def mixer(
    query_in,
    key_in,
    value_in,
    gate_in,
    decay_in,
    beta_in,
    conv_q,
    conv_k,
    conv_v,
    log_rate,
    rate_bias,
    head_gain,
    segment,
):
    length = segment.shape[0]
    n_heads = decay_in.shape[1]
    queries = jax.nn.silu(causal_conv(query_in, conv_q, segment)).reshape(length, n_heads, -1)
    key_act = jax.nn.silu(causal_conv(key_in, conv_k, segment)).reshape(length, n_heads, -1)
    values = jax.nn.silu(causal_conv(value_in, conv_v, segment)).reshape(length, n_heads, -1)
    queries = queries * lax.rsqrt(jnp.sum(queries * queries, axis=-1, keepdims=True) + EPS)
    key_act = key_act * lax.rsqrt(jnp.sum(key_act * key_act, axis=-1, keepdims=True) + EPS)
    beta_gate = jax.nn.sigmoid(beta_in)
    logdecay = -jnp.exp(log_rate) * jax.nn.softplus(decay_in + rate_bias)
    mixed = delta_rule(queries, key_act, values, logdecay, beta_gate, segment)
    normed = mixed * lax.rsqrt(jnp.mean(mixed * mixed, axis=-1, keepdims=True) + HEAD_FLOOR)
    gated = normed * head_gain * jax.nn.silu(gate_in.reshape(length, n_heads, -1))
    return gated.reshape(length, -1)


def dense(inputs, matrix):
    return jnp.dot(inputs, matrix, preferred_element_type=jnp.float32)


def dense_t(inputs, matrix):
    return lax.dot_general(
        inputs, matrix, (((0,), (0,)), ((), ())), preferred_element_type=jnp.float32
    )


def dense_bt(inputs, matrix):
    return lax.dot_general(
        inputs, matrix, (((1,), (1,)), ((), ())), preferred_element_type=jnp.float32
    )


def norm_back(source, scale, gain, grad_normed):
    weighted = gain * grad_normed
    inner = jnp.mean(source * weighted, axis=-1, keepdims=True)
    grad_source = scale * weighted - source * (scale * scale * scale) * inner
    gain_term = jnp.sum(grad_normed * source * scale, axis=0)
    return (grad_source, gain_term)


def local(
    residual,
    cotangent,
    lengths,
    token_order,
    norm_mixer,
    w_query,
    w_key,
    w_value,
    w_outgate,
    w_decay,
    w_beta,
    conv_query,
    conv_key,
    conv_value,
    decay_log,
    decay_bias,
    norm_head,
    w_output,
    norm_ffn,
    w_gate,
    w_up,
    w_down,
):

    def mixer_weights(n_part, q_part, k_part, v_part, g_part, d_part, b_part, o_part):
        return (
            lax.all_gather(n_part, ("fsdp", "ctx"), axis=0, tiled=True),
            lax.all_gather(q_part, ("fsdp", "ctx"), axis=0, tiled=True),
            lax.all_gather(k_part, ("fsdp", "ctx"), axis=0, tiled=True),
            lax.all_gather(v_part, ("fsdp", "ctx"), axis=0, tiled=True),
            lax.all_gather(g_part, ("fsdp", "ctx"), axis=0, tiled=True),
            lax.all_gather(d_part, ("fsdp", "ctx"), axis=0, tiled=True),
            lax.all_gather(b_part, ("fsdp", "ctx"), axis=0, tiled=True),
            lax.all_gather(o_part, ("fsdp", "ctx"), axis=1, tiled=True),
        )

    def ffn_weights(n_part, g_part, u_part, d_part):
        return (
            lax.all_gather(n_part, ("fsdp", "ctx"), axis=0, tiled=True),
            lax.all_gather(g_part, ("fsdp", "ctx"), axis=0, tiled=True),
            lax.all_gather(u_part, ("fsdp", "ctx"), axis=0, tiled=True),
            lax.all_gather(d_part, ("fsdp", "ctx"), axis=1, tiled=True),
        )

    mixer_set = mixer_weights(
        norm_mixer, w_query, w_key, w_value, w_outgate, w_decay, w_beta, w_output
    )
    m_norm, m_query, m_key, m_value, m_outgate, m_decay, m_beta, m_output = mixer_set
    source = residual.astype(jnp.float32)
    scale1 = lax.rsqrt(jnp.mean(source * source, axis=-1, keepdims=True) + EPS)
    normed1 = (source * scale1 * m_norm.astype(jnp.float32)).astype(jnp.bfloat16)
    q_raw = dense(normed1, m_query).astype(jnp.bfloat16)
    k_raw = dense(normed1, m_key).astype(jnp.bfloat16)
    v_raw = dense(normed1, m_value).astype(jnp.bfloat16)
    g_raw = dense(normed1, m_outgate).astype(jnp.bfloat16)
    d_raw = dense(normed1, m_decay).astype(jnp.bfloat16)
    b_raw = dense(normed1, m_beta).astype(jnp.bfloat16)
    q_head, k_head, v_head, g_head, d_head, b_head = (
        lax.all_to_all(q_raw, "ctx", split_axis=1, concat_axis=0, tiled=True),
        lax.all_to_all(k_raw, "ctx", split_axis=1, concat_axis=0, tiled=True),
        lax.all_to_all(v_raw, "ctx", split_axis=1, concat_axis=0, tiled=True),
        lax.all_to_all(g_raw, "ctx", split_axis=1, concat_axis=0, tiled=True),
        lax.all_to_all(d_raw, "ctx", split_axis=1, concat_axis=0, tiled=True),
        lax.all_to_all(b_raw, "ctx", split_axis=1, concat_axis=0, tiled=True),
    )
    order_row = token_order[0]
    group_len = order_row.shape[0]
    segment = segment_ids(lengths[0], group_len)
    inverse = jnp.zeros_like(order_row).at[order_row].set(lax.iota(jnp.int32, group_len))
    n_heads = d_head.shape[1]
    key_width = q_head.shape[1] // n_heads
    value_width = v_head.shape[1] // n_heads
    first_head = (lax.axis_index("tp") * lax.axis_size("ctx") + lax.axis_index("ctx")) * n_heads
    k_query = lax.dynamic_slice_in_dim(
        conv_query.astype(jnp.float32), first_head * key_width, n_heads * key_width, 1
    )
    k_key = lax.dynamic_slice_in_dim(
        conv_key.astype(jnp.float32), first_head * key_width, n_heads * key_width, 1
    )
    k_value = lax.dynamic_slice_in_dim(
        conv_value.astype(jnp.float32), first_head * value_width, n_heads * value_width, 1
    )
    d_log = lax.dynamic_slice_in_dim(decay_log, first_head, n_heads, 0)
    d_bias = lax.dynamic_slice_in_dim(decay_bias, first_head, n_heads, 0)
    n_head = norm_head.astype(jnp.float32)

    def local_mixer(
        query_in,
        key_in,
        value_in,
        gate_in,
        decay_in,
        beta_in,
        conv_q,
        conv_k,
        conv_v,
        log_rate,
        rate_bias,
        head_gain,
    ):
        return mixer(
            query_in,
            key_in,
            value_in,
            gate_in,
            decay_in,
            beta_in,
            conv_q,
            conv_k,
            conv_v,
            log_rate,
            rate_bias,
            head_gain,
            segment,
        )

    headout, mixer_pull = jax.vjp(
        local_mixer,
        q_head[order_row].astype(jnp.float32),
        k_head[order_row].astype(jnp.float32),
        v_head[order_row].astype(jnp.float32),
        g_head[order_row].astype(jnp.float32),
        d_head[order_row].astype(jnp.float32),
        b_head[order_row].astype(jnp.float32),
        k_query,
        k_key,
        k_value,
        d_log,
        d_bias,
        n_head,
    )
    given = headout[inverse].astype(jnp.bfloat16)
    mixer_tokens = lax.all_to_all(given, "ctx", split_axis=0, concat_axis=1, tiled=True)
    attention = lax.psum(dense(mixer_tokens, m_output), "tp")
    middle = source + attention
    scale2 = lax.rsqrt(jnp.mean(middle * middle, axis=-1, keepdims=True) + EPS)
    ffn_set = ffn_weights(norm_ffn, w_gate, w_up, w_down)
    f_norm, f_gate, f_up, f_down = ffn_set
    normed2 = (middle * scale2 * f_norm.astype(jnp.float32)).astype(jnp.bfloat16)
    gating = dense(normed2, f_gate)
    up_part = dense(normed2, f_up)
    sig_gate = jax.nn.sigmoid(gating)
    silu_gate = gating * sig_gate
    activation = (silu_gate * up_part).astype(jnp.bfloat16)
    ffn_out = lax.psum(dense(activation, f_down).astype(jnp.bfloat16), "tp").astype(jnp.float32)
    output = (middle + ffn_out).astype(jnp.bfloat16)
    tied_ffn = lax.optimization_barrier((norm_ffn, w_gate, w_up, w_down, cotangent))
    ffn_back = ffn_weights(tied_ffn[0], tied_ffn[1], tied_ffn[2], tied_ffn[3])
    b_norm, b_gate, b_up, b_down = ffn_back
    down_term = dense_t(activation, cotangent)
    grad_act = dense_bt(cotangent, b_down)
    grad_gating = (grad_act * up_part * (sig_gate + silu_gate * (1.0 - sig_gate))).astype(
        jnp.bfloat16
    )
    grad_up = (grad_act * silu_gate).astype(jnp.bfloat16)
    grad_normed2 = lax.psum(
        (dense_bt(grad_gating, b_gate) + dense_bt(grad_up, b_up)).astype(jnp.bfloat16), "tp"
    ).astype(jnp.float32)
    back2, ffn_gain_term = norm_back(middle, scale2, b_norm.astype(jnp.float32), grad_normed2)
    gate_term = dense_t(normed2, grad_gating)
    up_term = dense_t(normed2, grad_up)
    gnorm_ffn, gw_gate, gw_up, gw_down = (
        lax.psum_scatter(ffn_gain_term, ("fsdp", "ctx"), scatter_dimension=0, tiled=True),
        lax.psum_scatter(gate_term, ("fsdp", "ctx"), scatter_dimension=0, tiled=True),
        lax.psum_scatter(up_term, ("fsdp", "ctx"), scatter_dimension=0, tiled=True),
        lax.psum_scatter(down_term, ("fsdp", "ctx"), scatter_dimension=1, tiled=True),
    )
    grad_mid = cotangent.astype(jnp.float32) + back2
    tied_mix = lax.optimization_barrier(
        (norm_mixer, w_query, w_key, w_value, w_outgate, w_decay, w_beta, w_output, grad_mid)
    )
    mixer_back = mixer_weights(
        tied_mix[0],
        tied_mix[1],
        tied_mix[2],
        tied_mix[3],
        tied_mix[4],
        tied_mix[5],
        tied_mix[6],
        tied_mix[7],
    )
    a_norm, a_query, a_key, a_value, a_outgate, a_decay, a_beta, a_output = mixer_back
    grad_attn = grad_mid.astype(jnp.bfloat16)
    output_term = dense_t(mixer_tokens, grad_attn)
    grad_given = dense_bt(grad_attn, a_output).astype(jnp.bfloat16)
    grad_heads = lax.all_to_all(grad_given, "ctx", split_axis=1, concat_axis=0, tiled=True)
    pulled = mixer_pull(grad_heads[order_row].astype(jnp.float32))
    returned = (
        lax.all_to_all(
            pulled[0][inverse].astype(jnp.bfloat16), "ctx", split_axis=0, concat_axis=1, tiled=True
        ),
        lax.all_to_all(
            pulled[1][inverse].astype(jnp.bfloat16), "ctx", split_axis=0, concat_axis=1, tiled=True
        ),
        lax.all_to_all(
            pulled[2][inverse].astype(jnp.bfloat16), "ctx", split_axis=0, concat_axis=1, tiled=True
        ),
        lax.all_to_all(
            pulled[3][inverse].astype(jnp.bfloat16), "ctx", split_axis=0, concat_axis=1, tiled=True
        ),
        lax.all_to_all(
            pulled[4][inverse].astype(jnp.bfloat16), "ctx", split_axis=0, concat_axis=1, tiled=True
        ),
        lax.all_to_all(
            pulled[5][inverse].astype(jnp.bfloat16), "ctx", split_axis=0, concat_axis=1, tiled=True
        ),
    )
    grad_q, grad_k, grad_v, grad_g, grad_d, grad_b = returned
    partial_normed1 = (
        dense_bt(grad_q, a_query) + dense_bt(grad_k, a_key) + dense_bt(grad_v, a_value)
    )
    partial_normed1 = (
        partial_normed1
        + dense_bt(grad_g, a_outgate)
        + dense_bt(grad_d, a_decay)
        + dense_bt(grad_b, a_beta)
    )
    grad_normed1 = lax.psum(partial_normed1.astype(jnp.bfloat16), "tp").astype(jnp.float32)
    back1, mix_gain_term = norm_back(source, scale1, a_norm.astype(jnp.float32), grad_normed1)
    grad_input = (grad_mid + back1).astype(jnp.bfloat16)
    query_term = dense_t(normed1, grad_q)
    key_term = dense_t(normed1, grad_k)
    value_term = dense_t(normed1, grad_v)
    outgate_term = dense_t(normed1, grad_g)
    decay_term = dense_t(normed1, grad_d)
    beta_term = dense_t(normed1, grad_b)
    mixer_grads = (
        lax.psum_scatter(mix_gain_term, ("fsdp", "ctx"), scatter_dimension=0, tiled=True),
        lax.psum_scatter(query_term, ("fsdp", "ctx"), scatter_dimension=0, tiled=True),
        lax.psum_scatter(key_term, ("fsdp", "ctx"), scatter_dimension=0, tiled=True),
        lax.psum_scatter(value_term, ("fsdp", "ctx"), scatter_dimension=0, tiled=True),
        lax.psum_scatter(outgate_term, ("fsdp", "ctx"), scatter_dimension=0, tiled=True),
        lax.psum_scatter(decay_term, ("fsdp", "ctx"), scatter_dimension=0, tiled=True),
        lax.psum_scatter(beta_term, ("fsdp", "ctx"), scatter_dimension=0, tiled=True),
        lax.psum_scatter(output_term, ("fsdp", "ctx"), scatter_dimension=1, tiled=True),
    )
    full_query = lax.dynamic_update_slice_in_dim(
        jnp.zeros(conv_query.shape, jnp.float32), pulled[6], first_head * key_width, 1
    )
    full_key = lax.dynamic_update_slice_in_dim(
        jnp.zeros(conv_key.shape, jnp.float32), pulled[7], first_head * key_width, 1
    )
    full_value = lax.dynamic_update_slice_in_dim(
        jnp.zeros(conv_value.shape, jnp.float32), pulled[8], first_head * value_width, 1
    )
    full_log = lax.dynamic_update_slice_in_dim(
        jnp.zeros(decay_log.shape, jnp.float32), pulled[9], first_head, 0
    )
    full_bias = lax.dynamic_update_slice_in_dim(
        jnp.zeros(decay_bias.shape, jnp.float32), pulled[10], first_head, 0
    )
    head_sums = lax.psum(
        (full_query, full_key, full_value, full_log, full_bias, pulled[11]), ("fsdp", "ctx", "tp")
    )
    return (
        output,
        grad_input,
        mixer_grads[0],
        mixer_grads[1],
        mixer_grads[2],
        mixer_grads[3],
        mixer_grads[4],
        mixer_grads[5],
        mixer_grads[6],
        head_sums[0],
        head_sums[1],
        head_sums[2],
        head_sums[3],
        head_sums[4],
        head_sums[5],
        mixer_grads[7],
        gnorm_ffn,
        gw_gate,
        gw_up,
        gw_down,
    )


def solution(mesh):
    in_specs = (
        P(("fsdp", "ctx"), None),
        P(("fsdp", "ctx"), None),
        P("fsdp", None),
        P("fsdp", None),
        P(("fsdp", "ctx")),
        P(("fsdp", "ctx"), "tp"),
        P(("fsdp", "ctx"), "tp"),
        P(("fsdp", "ctx"), "tp"),
        P(("fsdp", "ctx"), "tp"),
        P(("fsdp", "ctx"), "tp"),
        P(("fsdp", "ctx"), "tp"),
        P(),
        P(),
        P(),
        P(),
        P(),
        P(),
        P("tp", ("fsdp", "ctx")),
        P(("fsdp", "ctx")),
        P(("fsdp", "ctx"), "tp"),
        P(("fsdp", "ctx"), "tp"),
        P("tp", ("fsdp", "ctx")),
    )
    out_specs = (
        P(("fsdp", "ctx"), None),
        P(("fsdp", "ctx"), None),
        P(("fsdp", "ctx")),
        P(("fsdp", "ctx"), "tp"),
        P(("fsdp", "ctx"), "tp"),
        P(("fsdp", "ctx"), "tp"),
        P(("fsdp", "ctx"), "tp"),
        P(("fsdp", "ctx"), "tp"),
        P(("fsdp", "ctx"), "tp"),
        P(),
        P(),
        P(),
        P(),
        P(),
        P(),
        P("tp", ("fsdp", "ctx")),
        P(("fsdp", "ctx")),
        P(("fsdp", "ctx"), "tp"),
        P(("fsdp", "ctx"), "tp"),
        P("tp", ("fsdp", "ctx")),
    )
    return jax.shard_map(local, mesh=mesh, in_specs=in_specs, out_specs=out_specs, check_vma=False)
```

profile of v0, /device:TPU:0, one launch (start us, length us, event | category | flops | bytes accessed | tf_op | source)
XLA Modules:
  0.0 5016.6 jit_solution(10112499682955596149)
XLA Ops:
  10.0 23.1 all-gather
  33.2 18.1 all_gather.73
  63.2 19.3 all_gather.75
  84.7 8.0 scatter_custom_fusion
  107.7 7.7 all-gather.25.cloned.1.call-done
  132.4 8.1 gather_fusion.2
  152.4 7.5 gather_fusion.4
  194.1 8.3 convolution_convert_fusion.3
  217.1 55.6 %all-gather.27.cloned.1.call-done = bf16[2048,2048]{1,0:T(8,128)(2,1)} async-done(((bf16[128,2048]{1,0:T(8,128)(2,1)}), bf16[2048,2048]{1,0:T(8,128)(2,1)}) %all-gather.27.cloned.1.call-update) | async-done | bytes 8388624 | tf_op jit(solution)/shard_map/all_gather | solution.py:210
  272.8 8.5 convolution_convert_fusion.2
  288.2 11.1 gather_fusion.3
  320.4 602.3 %while.42 = (s32[]{:T(128)}, f32[2,128,256]{2,1,0:T(8,128)S(1)}, f32[32,2,64,256]{3,2,1,0:T(8,128)}, f32[32,2,128,256]{3,2,1,0:T(8,128)}, f32[32,2,64]{2,1,0:T(2...) while((s32[]{:T(128)}, f32[2,128,256]{2,1,0:T(8,128)S(1)}, ...), condition=%wide.region_7.8_spmd.clone, body=%wide.region_5.7_spmd.clone.sunk | while | flops 302707456 | bytes 4344509 | solution.py:109
  938.8 9.2 gather_fusion.5
  953.5 9.2 gather_fusion.6
  970.5 25.6 all-to-all-done.6
  996.1 10.2 fusion.213
  1010.0 18.6 all-gather.1
  1028.6 84.3 %all-reduce.38.cloned.1.call-done = f32[512,2048]{1,0:T(8,128)} async-done(((f32[512,2048]{1,0:T(8,128)}), f32[512,2048]{1,0:T(8,128)}) %all-reduce.38.cloned.1.call-update) | async-done | bytes 4194320 | tf_op jit(solution)/shard_map/psum | solution.py:313
  1118.2 91.7 %all-gather.31.cloned.1.call-done = bf16[2048,2816]{1,0:T(8,128)(2,1)} async-done(((bf16[128,2816]{1,0:T(8,128)(2,1)}), bf16[2048,2816]{1,0:T(8,128)(2,1)}) %all-gather.31.cloned.1.call-update) | async-done | bytes 11534352 | tf_op jit(solution)/shard_map/all_gather | solution.py:219
  1209.8 11.3 fusion.214
  1221.1 83.7 %all-gather.33.cloned.1.call-done = bf16[2048,2816]{1,0:T(8,128)(2,1)} async-done(((bf16[128,2816]{1,0:T(8,128)(2,1)}), bf16[2048,2816]{1,0:T(8,128)(2,1)}) %all-gather.33.cloned.1.call-update) | async-done | bytes 11534352 | tf_op jit(solution)/shard_map/all_gather | solution.py:220
  1304.9 11.1 fusion.215
  1316.0 86.9 %all-gather.37.cloned.1.call-done = bf16[2816,2048]{1,0:T(8,128)(2,1)} async-done(((bf16[2816,128]{1,0:T(8,128)(2,1)}), bf16[2816,2048]{1,0:T(8,128)(2,1)}) %all-gather.37.cloned.1.call-update) | async-done | bytes 11534352 | tf_op jit(solution)/shard_map/all_gather | solution.py:221
  1402.8 17.2 fusion.118
  1420.1 77.7 %all-gather.39.cloned.1.call-done = bf16[2048,2816]{1,0:T(8,128)(2,1)} async-done(((bf16[128,2816]{1,0:T(8,128)(2,1)}), bf16[2048,2816]{1,0:T(8,128)(2,1)}) %all-gather.39.cloned.1.call-update) | async-done | bytes 11534352 | tf_op jit(solution)/shard_map/all_gather | solution.py:219
  1497.8 11.2 fusion.216
  1509.0 83.8 %all-gather.41.cloned.1.call-done = bf16[2048,2816]{1,0:T(8,128)(2,1)} async-done(((bf16[128,2816]{1,0:T(8,128)(2,1)}), bf16[2048,2816]{1,0:T(8,128)(2,1)}) %all-gather.41.cloned.1.call-update) | async-done | bytes 11534352 | tf_op jit(solution)/shard_map/all_gather | solution.py:220
  1592.8 11.6 add_convert_fusion.1
  1604.6 18.8 all-gather.2
  1623.4 42.4 all-reduce.40.cloned.1.call-done
  1676.3 75.9 %all-gather.43.cloned.1.call-done = bf16[2048,2048]{1,0:T(8,128)(2,1)} async-done(((bf16[2048,128]{1,0:T(8,128)(2,1)}), bf16[2048,2048]{1,0:T(8,128)(2,1)}) %all-gather.43.cloned.1.call-update) | async-done | bytes 8388624 | tf_op jit(solution)/shard_map/all_gather | solution.py:213
  1752.2 9.2 convolution_convert_fusion
  1775.0 78.6 %all-gather.35.cloned.1.call-done = bf16[2816,2048]{1,0:T(8,128)(2,1)} async-done(((bf16[2816,128]{1,0:T(8,128)(2,1)}), bf16[2816,2048]{1,0:T(8,128)(2,1)}) %all-gather.35.cloned.1.call-update) | async-done | bytes 11534352 | tf_op jit(solution)/shard_map/all_gather | solution.py:221
  1853.6 10.9 convolution_convert_fusion.1
  1864.5 20.5 all_gather.94
  1884.9 19.2 all_gather.95
  1904.1 9.2 gather_fusion.7
  1934.7 911.8 %while.43 = (s32[]{:T(128)}, f32[2,128,256]{2,1,0:T(8,128)S(1)}, f32[32,2,64,128]{3,2,1,0:T(8,128)S(1)}, f32[32,2,64,128]{3,2,1,0:T(8,128)}, f32[32,2,64,256]{3,...) while((s32[]{:T(128)}, f32[2,128,256]{2,1,0:T(8,128)S(1)}, ...), condition=%wide.region_28.29_spmd.clone, body=%wide.region_16.28_spmd.clone.sunk | while | flops 781965632 | bytes 13710463 | solution.py:109
  2948.3 12.2 multiply_reduce_fusion.10
  2978.5 9.2 gather_fusion.10
  3002.6 9.2 gather_fusion.11
  3036.6 10.6 fusion.219
  3047.3 8.1 all-to-all-done.11
  3055.4 7.9 fusion.220
  3072.8 13.2 fusion.160
  3098.9 13.0 fusion.228
  3112.0 13.3 fusion.229
  3125.4 14.0 fusion.230
  3139.4 10.0 fusion.224
  3149.8 9.7 fusion.225
  3161.4 17.0 all-gather.3
  3181.7 59.4 %all-reduce.30 = (f32[2048]{0:T(1024)S(1)}, f32[2048]{0:T(1024)S(1)}) all-reduce(f32[2048]{0:T(1024)S(1)} %get-tuple-element.668, f32[2048]{0:T(1024)S(1)} %copy-done.85), channel_id=2, replica_groups=mesh['fsdp'=4,'ctx'=4,'tp'=2] {'fsdp','ctx'}, use_global_device_ids=true, to_apply=%region_34.35.clone | all-reduce | flops 4096 | bytes 32768
  3249.9 47.5 all-reduce.42.cloned.1.call-done
  3297.5 128.9 %all-reduce.44.cloned.1.call-done = (f32[4,2048]{1,0:T(4,128)}, f32[4,2048]{1,0:T(4,128)}, f32[16]{0:T(128)}, f32[16]{0:T(128)}, f32[256]{0:T(256)}) async-done(((f32[4,2048]{1,0:T(4,128)}, f32[4,2048]{1,0:T(4,128)}, f32[16]{0:T(128)}, f32[16]{0:T(128)}, f32[256]{0:T(256)}), (f32[4,2048]{1,0:T(4,128)}, f32[4,2048]{1,0:T(4,128)}, f32[16]{0:T(128)}, f32[16]{0:T(128)}, ...) | async-done | bytes 66704 | tf_op jit(solution)/shard_map/psum | solution.py:431
  3426.4 59.0 %reduce-scatter.21.cloned.1.call-done = f32[128,8]{0,1:T(8,128)} async-done(((f32[2048,8]{0,1:T(8,128)}), f32[128,8]{0,1:T(8,128)}) %reduce-scatter.21.cloned.1.call-update) | async-done | bytes 4112 | tf_op jit(solution)/shard_map/reduce_scatter | solution.py:413
  3485.3 55.5 %reduce-scatter.19.cloned.1.call-done = f32[128,8]{0,1:T(8,128)} async-done(((f32[2048,8]{0,1:T(8,128)}), f32[128,8]{0,1:T(8,128)}) %reduce-scatter.19.cloned.1.call-update) | async-done | bytes 4112 | tf_op jit(solution)/shard_map/reduce_scatter | solution.py:412
  3540.8 182.7 %reduce-scatter.23.cloned.1.call-done = f32[2048,128]{1,0:T(8,128)} async-done(((f32[2048,2048]{1,0:T(8,128)}), f32[2048,128]{1,0:T(8,128)}) %reduce-scatter.23.cloned.1.call-update) | async-done | bytes 1048592 | tf_op jit(solution)/shard_map/reduce_scatter | solution.py:414
  3723.5 108.8 %reduce-scatter.13.cloned.1.call-done = f32[128,1024]{1,0:T(8,128)} async-done(((f32[2048,1024]{1,0:T(8,128)}), f32[128,1024]{1,0:T(8,128)}) %reduce-scatter.13.cloned.1.call-update) | async-done | bytes 524304 | tf_op jit(solution)/shard_map/reduce_scatter | solution.py:409
  3832.3 109.4 %reduce-scatter.11.cloned.1.call-done = f32[128,1024]{1,0:T(8,128)} async-done(((f32[2048,1024]{1,0:T(8,128)}), f32[128,1024]{1,0:T(8,128)}) %reduce-scatter.11.cloned.1.call-update) | async-done | bytes 524304 | tf_op jit(solution)/shard_map/reduce_scatter | solution.py:408
  3941.8 231.7 %reduce-scatter.25.cloned.1.call-done = f32[128,2816]{1,0:T(8,128)} async-done(((f32[2048,2816]{1,0:T(8,128)}), f32[128,2816]{1,0:T(8,128)}) %reduce-scatter.25.cloned.1.call-update) | async-done | bytes 1441808 | tf_op jit(solution)/shard_map/reduce_scatter | solution.py:343
  4173.5 231.2 %reduce-scatter.27.cloned.1.call-done = f32[128,2816]{1,0:T(8,128)} async-done(((f32[2048,2816]{1,0:T(8,128)}), f32[128,2816]{1,0:T(8,128)}) %reduce-scatter.27.cloned.1.call-update) | async-done | bytes 1441808 | tf_op jit(solution)/shard_map/reduce_scatter | solution.py:344
  4404.7 231.3 %reduce-scatter.29.cloned.1.call-done = f32[2816,128]{1,0:T(8,128)} async-done(((f32[2816,2048]{1,0:T(8,128)}), f32[2816,128]{1,0:T(8,128)}) %reduce-scatter.29.cloned.1.call-update) | async-done | bytes 1441808 | tf_op jit(solution)/shard_map/reduce_scatter | solution.py:345
  4636.0 182.8 %reduce-scatter.15.cloned.1.call-done = f32[128,2048]{1,0:T(8,128)} async-done(((f32[2048,2048]{1,0:T(8,128)}), f32[128,2048]{1,0:T(8,128)}) %reduce-scatter.15.cloned.1.call-update) | async-done | bytes 1048592 | tf_op jit(solution)/shard_map/reduce_scatter | solution.py:410
  4818.7 182.8 %reduce-scatter.17.cloned.1.call-done = f32[128,2048]{1,0:T(8,128)} async-done(((f32[2048,2048]{1,0:T(8,128)}), f32[128,2048]{1,0:T(8,128)}) %reduce-scatter.17.cloned.1.call-update) | async-done | bytes 1048592 | tf_op jit(solution)/shard_map/reduce_scatter | solution.py:411
  (4095 shorter events, 1896.1 us)
Async XLA Ops:
  7.2 89.5 %all-gather.21.cloned.1.call-start = ((), (), s32[]{:S(2)}) async-start(), calls=%async_computation.24 | async-start | bytes 4456448 | tf_op jit(solution)/shard_map/all_gather | solution.py:208
  7.9 107.4 %all-gather.25.cloned.1.call-start = ((), (), s32[]{:S(2)}) async-start(), calls=%async_computation.26 | async-start | bytes 4456448 | tf_op jit(solution)/shard_map/all_gather | solution.py:207
  8.7 185.4 %all-gather.23.cloned.1.call-start = ((), (), s32[]{:S(2)}) async-start(), calls=%async_computation.25 | async-start | bytes 8912896 | tf_op jit(solution)/shard_map/all_gather | solution.py:209
  9.4 263.4 %all-gather.27.cloned.1.call-start = ((), (), s32[]{:S(2)}) async-start(), calls=%async_computation.27 | async-start | bytes 8912896 | tf_op jit(solution)/shard_map/all_gather | solution.py:210
  57.2 36.2 all-to-all-start
  60.6 910.0 %all-gather.29.cloned.1.call-start = ((), (), s32[]{:S(2)}) async-start(), calls=%async_computation.28 | async-start | bytes 8912896 | tf_op jit(solution)/shard_map/all_gather | solution.py:213
  61.9 98.2 %copy-start.104 = (f32[1,256]{1,0:T(1,128)}, f32[1,256]{1,0:T(1,128)S(1)}, u32[]{:S(2)}) copy-start(f32[1,256]{1,0:T(1,128)S(1)} %get-tuple-element.816) | copy-start | bytes 3076
  61.9 98.2 %copy-start.106 = (f32[1,256]{1,0:T(1,128)}, f32[1,256]{1,0:T(1,128)S(1)}, u32[]{:S(2)}) copy-start(f32[1,256]{1,0:T(1,128)S(1)} %get-tuple-element.817) | copy-start | bytes 3076
  61.9 98.2 %copy-start.108 = (f32[1,256]{1,0:T(1,128)}, f32[1,256]{1,0:T(1,128)S(1)}, u32[]{:S(2)}) copy-start(f32[1,256]{1,0:T(1,128)S(1)} %get-tuple-element.818) | copy-start | bytes 3076
  61.9 98.2 %copy-start.110 = (f32[1,256]{1,0:T(1,128)}, f32[1,256]{1,0:T(1,128)S(1)}, u32[]{:S(2)}) copy-start(f32[1,256]{1,0:T(1,128)S(1)} %get-tuple-element.819) | copy-start | bytes 3076
  61.9 98.2 %copy-start.102 = (f32[1,256]{1,0:T(1,128)}, f32[1,256]{1,0:T(1,128)S(1)}, u32[]{:S(2)}) copy-start(f32[1,256]{1,0:T(1,128)S(1)} %get-tuple-element.812) | copy-start | bytes 3076
  61.9 98.2 %copy-start.112 = (f32[1,256]{1,0:T(1,128)}, f32[1,256]{1,0:T(1,128)S(1)}, u32[]{:S(2)}) copy-start(f32[1,256]{1,0:T(1,128)S(1)} %get-tuple-element.813) | copy-start | bytes 3076
  62.0 98.2 %copy-start.114 = (f32[1,256]{1,0:T(1,128)}, f32[1,256]{1,0:T(1,128)S(1)}, u32[]{:S(2)}) copy-start(f32[1,256]{1,0:T(1,128)S(1)} %get-tuple-element.814) | copy-start | bytes 3076
  62.0 876.8 %copy-start.48 = (s32[2048]{0:T(1024)}, s32[2048]{0:T(1024)S(1)}, u32[]{:S(2)}) copy-start(s32[2048]{0:T(1024)S(1)} %broadcast_clamp_fusion) | copy-start | bytes 24580
  62.4 239.2 %copy-start.50 = (f32[2048]{0:T(1024)}, f32[2048]{0:T(1024)S(1)}, u32[]{:S(2)}) copy-start(f32[2048]{0:T(1024)S(1)} %get-tuple-element.809) | copy-start | bytes 24580
  62.4 239.2 %copy-start.52 = (f32[2048]{0:T(1024)}, f32[2048]{0:T(1024)S(1)}, u32[]{:S(2)}) copy-start(f32[2048]{0:T(1024)S(1)} %get-tuple-element.810) | copy-start | bytes 24580
  62.4 239.2 %copy-start.54 = (f32[2048]{0:T(1024)}, f32[2048]{0:T(1024)S(1)}, u32[]{:S(2)}) copy-start(f32[2048]{0:T(1024)S(1)} %get-tuple-element.811) | copy-start | bytes 24580
  63.1 238.5 %copy-start.90 = (f32[1,512]{1,0:T(1,128)}, f32[1,512]{1,0:T(1,128)S(1)}, u32[]{:S(2)}) copy-start(f32[1,512]{1,0:T(1,128)S(1)} %get-tuple-element.805) | copy-start | bytes 6148
  63.1 238.5 %copy-start.92 = (f32[1,512]{1,0:T(1,128)}, f32[1,512]{1,0:T(1,128)S(1)}, u32[]{:S(2)}) copy-start(f32[1,512]{1,0:T(1,128)S(1)} %get-tuple-element.806) | copy-start | bytes 6148
  63.1 238.5 %copy-start.94 = (f32[1,512]{1,0:T(1,128)}, f32[1,512]{1,0:T(1,128)S(1)}, u32[]{:S(2)}) copy-start(f32[1,512]{1,0:T(1,128)S(1)} %get-tuple-element.807) | copy-start | bytes 6148
  63.2 238.5 %copy-start.96 = (f32[1,512]{1,0:T(1,128)}, f32[1,512]{1,0:T(1,128)S(1)}, u32[]{:S(2)}) copy-start(f32[1,512]{1,0:T(1,128)S(1)} %get-tuple-element.808) | copy-start | bytes 6148
  92.8 860.7 %copy-start.46 = (s32[2048]{0:T(1024)}, s32[2048]{0:T(1024)S(1)}, u32[]{:S(2)}) copy-start(s32[2048]{0:T(1024)S(1)} %fusion.174) | copy-start | bytes 24580
  93.4 8.9 all-to-all-start.2
  102.4 18.5 all-to-all-start.1
  106.8 841.2 %copy-start.98 = (f32[1,2,2,128]{3,1,2,0:T(2,128)}, f32[1,2,2,128]{3,1,2,0:T(2,128)S(1)}, u32[]{:S(2)}) copy-start(f32[1,2,2,128]{3,1,2,0:T(2,128)S(1)} %copy.568) | copy-start | bytes 6148
  120.9 31.5 all-to-all-start.4
  203.9 78.9 %all-to-all-start.3 = ((bf16[512,4,512]{2,0,1:T(8,128)(2,1)}), bf16[512,4,512]{2,0,1:T(8,128)(2,1)S(1)}, u32[]{:S(2)}, u32[]{:S(2)}) async-start(bf16[512,4,512]{2,0,1:T(8,128)(2,1)} %bitcast.802), calls=%async_computation.3 | async-start | bytes 4194304 | tf_op jit(solution)/shard_map/all_to_all | solution.py:240
  284.1 654.6 %all-to-all-start.5 = ((bf16[512,4,512]{2,0,1:T(8,128)(2,1)}), bf16[512,4,512]{2,0,1:T(8,128)(2,1)S(1)}, u32[]{:S(2)}, u32[]{:S(2)}) async-start(bf16[512,4,512]{2,0,1:T(8,128)(2,1)} %bitcast.800), calls=%async_computation.5 | async-start | bytes 4194304 | tf_op jit(solution)/shard_map/all_to_all | solution.py:241
  966.8 29.3 all-to-all-start.6
  970.5 142.5 %all-reduce.38.cloned.1.call-start = ((), (), s32[]{:S(2)}) async-start(), calls=%async_computation.29 | async-start | bytes 8388608 | tf_op jit(solution)/shard_map/psum | solution.py:313
  1006.4 106.5 %copy-start.6 = (bf16[512,2048]{1,0:T(8,128)(2,1)S(1)}, bf16[512,2048]{1,0:T(8,128)(2,1)}, u32[]{:S(2)}) copy-start(bf16[512,2048]{1,0:T(8,128)(2,1)} %param.26) | copy-start | bytes 6291460
  1006.4 203.4 %all-gather.31.cloned.1.call-start = ((), (), s32[]{:S(2)}) async-start(), calls=%async_computation.30 | async-start | bytes 12255232 | tf_op jit(solution)/shard_map/all_gather | solution.py:219
  1007.2 297.7 %all-gather.33.cloned.1.call-start = ((), (), s32[]{:S(2)}) async-start(), calls=%async_computation.31 | async-start | bytes 12255232 | tf_op jit(solution)/shard_map/all_gather | solution.py:220
  1007.9 394.9 %all-gather.37.cloned.1.call-start = ((), (), s32[]{:S(2)}) async-start(), calls=%async_computation.33 | async-start | bytes 12255232 | tf_op jit(solution)/shard_map/all_gather | solution.py:221
  1008.6 489.1 %all-gather.39.cloned.1.call-start = ((), (), s32[]{:S(2)}) async-start(), calls=%async_computation.34 | async-start | bytes 12255232 | tf_op jit(solution)/shard_map/all_gather | solution.py:219
  1009.2 583.6 %all-gather.41.cloned.1.call-start = ((), (), s32[]{:S(2)}) async-start(), calls=%async_computation.35 | async-start | bytes 12255232 | tf_op jit(solution)/shard_map/all_gather | solution.py:220
  1010.0 655.8 %all-reduce.40.cloned.1.call-start = ((), (), s32[]{:S(2)}) async-start(), calls=%async_computation.36 | async-start | bytes 4194304 | tf_op jit(solution)/shard_map/psum | solution.py:335
  1118.1 186.7 %copy-start.42 = (bf16[512,2048]{1,0:T(8,128)(2,1)}, bf16[512,2048]{1,0:T(8,128)(2,1)S(1)}, u32[]{:S(2)}) copy-start(bf16[512,2048]{1,0:T(8,128)(2,1)S(1)} %multiply_convert_fusion.1) | copy-start | bytes 6291460
  1604.5 147.7 %all-gather.43.cloned.1.call-start = ((), (), s32[]{:S(2)}) async-start(), calls=%async_computation.37 | async-start | bytes 8912896 | tf_op jit(solution)/shard_map/all_gather | solution.py:213
  1673.9 179.6 %all-gather.35.cloned.1.call-start = ((), (), s32[]{:S(2)}) async-start(), calls=%async_computation.32 | async-start | bytes 12255232 | tf_op jit(solution)/shard_map/all_gather | solution.py:221
  1674.5 1344.9 %all-gather.47.cloned.1.call-start = ((), (), s32[]{:S(2)}) async-start(), calls=%async_computation.39 | async-start | bytes 4456448 | tf_op jit(solution)/shard_map/all_gather | solution.py:208
  1675.1 1354.7 %all-gather.45.cloned.1.call-start = ((), (), s32[]{:S(2)}) async-start(), calls=%async_computation.38 | async-start | bytes 4456448 | tf_op jit(solution)/shard_map/all_gather | solution.py:207
  1675.7 1360.9 %all-gather.49.cloned.1.call-start = ((), (), s32[]{:S(2)}) async-start(), calls=%async_computation.40 | async-start | bytes 8912896 | tf_op jit(solution)/shard_map/all_gather | solution.py:209
  1762.9 141.2 %all-to-all-start.7 = ((bf16[512,4,512]{2,0,1:T(8,128)(2,1)}), bf16[512,4,512]{2,0,1:T(8,128)(2,1)S(1)}, u32[]{:S(2)}, u32[]{:S(2)}) async-start(bf16[512,4,512]{2,0,1:T(8,128)(2,1)} %bitcast.801), calls=%async_computation.7 | async-start | bytes 4194304 | tf_op jit(solution)/shard_map/all_to_all | solution.py:365
  1766.6 1280.6 %all-gather.51.cloned.1.call-start = ((), (), s32[]{:S(2)}) async-start(), calls=%async_computation.41 | async-start | bytes 8912896 | tf_op jit(solution)/shard_map/all_gather | solution.py:210
  2869.9 42.6 all-to-all-start.12
  2912.5 31.6 all-to-all-start.13
  2944.7 18.0 all-to-all-start.9
  2962.7 29.2 all-to-all-start.8
  2991.9 34.2 all-to-all-start.10
  3026.1 29.3 all-to-all-start.11
  3029.7 148.8 %all-reduce.46.cloned.1.call-start = ((), (), s32[]{:S(2)}) async-start(), calls=%async_computation.54 | async-start | bytes 8388608 | tf_op jit(solution)/shard_map/psum | solution.py:324
  3068.0 229.5 %all-reduce.42.cloned.1.call-start = ((), (), s32[]{:S(2)}) async-start(), calls=%async_computation.48 | async-start | bytes 131072 | tf_op jit(solution)/shard_map/psum | solution.py:431
  3069.2 357.2 %all-reduce.44.cloned.1.call-start = ((), (), s32[]{:S(2)}) async-start(), calls=%async_computation.53 | async-start | bytes 135168 | tf_op jit(solution)/shard_map/psum | solution.py:431
  3070.4 414.9 %reduce-scatter.21.cloned.1.call-start = ((), (), s32[]{:S(2)}) async-start(), calls=%async_computation.47 | async-start | bytes 69632 | tf_op jit(solution)/shard_map/reduce_scatter | solution.py:413
  3071.7 469.1 %reduce-scatter.19.cloned.1.call-start = ((), (), s32[]{:S(2)}) async-start(), calls=%async_computation.46 | async-start | bytes 69632 | tf_op jit(solution)/shard_map/reduce_scatter | solution.py:412
  3072.8 650.7 %reduce-scatter.23.cloned.1.call-start = ((), (), s32[]{:S(2)}) async-start(), calls=%async_computation.49 | async-start | bytes 17825792 | tf_op jit(solution)/shard_map/reduce_scatter | solution.py:414
  3086.0 746.3 %reduce-scatter.13.cloned.1.call-start = ((), (), s32[]{:S(2)}) async-start(), calls=%async_computation.43 | async-start | bytes 8912896 | tf_op jit(solution)/shard_map/reduce_scatter | solution.py:409
  3091.7 850.1 %reduce-scatter.11.cloned.1.call-start = ((), (), s32[]{:S(2)}) async-start(), calls=%async_computation.42 | async-start | bytes 8912896 | tf_op jit(solution)/shard_map/reduce_scatter | solution.py:408
  3098.7 1074.8 %reduce-scatter.25.cloned.1.call-start = ((), (), s32[]{:S(2)}) async-start(), calls=%async_computation.50 | async-start | bytes 24510464 | tf_op jit(solution)/shard_map/reduce_scatter | solution.py:343
  3112.0 1292.7 %reduce-scatter.27.cloned.1.call-start = ((), (), s32[]{:S(2)}) async-start(), calls=%async_computation.51 | async-start | bytes 24510464 | tf_op jit(solution)/shard_map/reduce_scatter | solution.py:344
  3125.3 1510.6 %reduce-scatter.29.cloned.1.call-start = ((), (), s32[]{:S(2)}) async-start(), calls=%async_computation.52 | async-start | bytes 24510464 | tf_op jit(solution)/shard_map/reduce_scatter | solution.py:345
  3139.4 1679.4 %reduce-scatter.15.cloned.1.call-start = ((), (), s32[]{:S(2)}) async-start(), calls=%async_computation.44 | async-start | bytes 17825792 | tf_op jit(solution)/shard_map/reduce_scatter | solution.py:410
  3149.5 1852.1 %reduce-scatter.17.cloned.1.call-start = ((), (), s32[]{:S(2)}) async-start(), calls=%async_computation.45 | async-start | bytes 17825792 | tf_op jit(solution)/shard_map/reduce_scatter | solution.py:411
  (131 other events, 1158.0 us)
Sparse Core Ops, SparseCore 0:
  10.2 53.5 all-gather.20
  66.0 49.3 all-gather.24
  117.5 76.5 all-gather.22
  196.1 76.5 all-gather.26
  274.8 78.9 all-gather.28
  1006.5 106.3 all-reduce.37
  1115.5 94.3 all-gather.30
  1212.4 92.4 all-gather.32
  1307.3 95.5 all-gather.36
  1405.2 92.4 all-gather.38
  1500.3 92.4 all-gather.40
  1604.6 61.0 all-reduce.39
  1674.0 78.0 all-gather.42
  1754.2 99.3 all-gather.34
  1855.6 48.9 all-gather.46
  1906.6 49.1 all-gather.44
  1957.8 73.4 all-gather.48
  2033.3 73.2 all-gather.50
  3068.1 105.3 all-reduce.45
  3179.9 117.5 all-reduce.41
  3305.6 120.7 all-reduce.43
  3430.7 54.6 reduce-scatter.20
  3489.8 50.9 reduce-scatter.18
  3545.9 177.5 reduce-scatter.22
  3728.7 103.6 reduce-scatter.12
  3837.4 104.3 reduce-scatter.10
  3946.9 226.5 reduce-scatter.24
  4178.7 225.9 reduce-scatter.26
  4409.9 225.9 reduce-scatter.28
  4641.0 177.6 reduce-scatter.14
  4824.0 177.5 reduce-scatter.16
where the time goes:
time: 5040 us; the launch traced here: 5020 us
  waiting for transfers between devices  2570 us (51%)
  matrix products  1080 us (21%)
  local copies, waits for them, and re-layouts  614 us (12%)
  other arithmetic  424 us (8%)
  blocking collectives  214 us (4%)
  starting transfers between devices  53.9 us (1%)
    reduce_scatter x1, waiting for transfers between devices, local(): lax.psum_scatter(gate_term, ('fsdp', 'ctx'), scatter_dimension=0, tiled=T...  232 us
    reduce_scatter x1, waiting for transfers between devices, local(): lax.psum_scatter(down_term, ('fsdp', 'ctx'), scatter_dimension=1, tiled=T...  231 us
    reduce_scatter x1, waiting for transfers between devices, local(): lax.psum_scatter(up_term, ('fsdp', 'ctx'), scatter_dimension=0, tiled=True)  231 us
    reduce_scatter x1, waiting for transfers between devices, local(): lax.psum_scatter(outgate_term, ('fsdp', 'ctx'), scatter_dimension=0, tile...  183 us
    reduce_scatter x1, waiting for transfers between devices, local(): lax.psum_scatter(value_term, ('fsdp', 'ctx'), scatter_dimension=0, tiled=...  183 us
    reduce_scatter x1, waiting for transfers between devices, local(): lax.psum_scatter(output_term, ('fsdp', 'ctx'), scatter_dimension=1, tiled...  183 us
    psum x2, waiting for transfers between devices, local(): lax.psum((full_query, full_key, full_value, full_log, full_bias, pulled[1...  176 us
    all_gather x2, waiting for transfers between devices, ffn_weights(): lax.all_gather(g_part, ('fsdp', 'ctx'), axis=0, tiled=True)  169 us

commit v1 on v0

v1 whole, which is shorter than its diff:
```python
import functools
import jax
import jax.numpy as jnp
from jax import lax
from jax.experimental import pallas as pl
from jax.experimental.pallas import tpu as pltpu
from jax.sharding import PartitionSpec as P

EPS = 1e-06
HEAD_FLOOR = 0.01
SPAN = 128
ROWS = 256
HALO = 16
TAPS = 4
LANES = 128
F32 = jnp.float32
BF16 = jnp.bfloat16
HIGHEST = lax.Precision.HIGHEST


def mm(a, b):
    return lax.dot_general(a.astype(BF16), b.astype(BF16), (((1,), (0,)), ((), ())), preferred_element_type=F32)


def mm_bt(a, b):
    return lax.dot_general(a.astype(BF16), b.astype(BF16), (((1,), (1,)), ((), ())), preferred_element_type=F32)


def mm_at(a, b):
    return lax.dot_general(a.astype(BF16), b.astype(BF16), (((0,), (0,)), ((), ())), preferred_element_type=F32)


def exact(a, b):
    return jnp.dot(a, b, precision=HIGHEST, preferred_element_type=F32)


def iota(shape, axis):
    return lax.broadcasted_iota(jnp.int32, shape, axis)


def bounds_of(lengths):
    found, total = [], 0
    for s in range(lengths.shape[1] - 1):
        total = total + lengths[0, s]
        found.append(total)
    return found


def begin_of(rows, bounds):
    begin = jnp.zeros_like(rows)
    for edge in bounds:
        begin = jnp.where(rows >= edge, edge, begin)
    return begin


def lane_sum(value):
    return jnp.sum(value, axis=1, keepdims=True)


def at_lane(lane, place, column):
    return jnp.where(lane == place, column, 0.0)


def invert(lower):
    size = lower.shape[0]
    row, col = iota((size, size), 0), iota((size, size), 1)
    inverse = jnp.where(row == col, 1.0, jnp.where(row // 2 == col // 2, -lower, 0.0))
    width = 2
    while width < size:
        joint = (row // (2 * width) == col // (2 * width)) & (row // width != col // width)
        between = jnp.where(joint, lower, 0.0)
        held = inverse.astype(BF16)
        inverse = inverse - mm(mm(held, between), held)
        width *= 2
    return inverse


def conv_rows(before, block, taps, pos):
    ext = jnp.concatenate([before, block], axis=0)
    size = block.shape[0]
    total = taps[0:1] * block
    for o in range(1, TAPS):
        total = total + jnp.where(pos >= o, taps[o : o + 1], 0.0) * ext[HALO - o : HALO - o + size]
    return total


def prepare_kernel(heads, key, val, lengths, raw_ref, before_ref, taps_ref, rate_ref,
                   u_ref, qe_ref, w_ref, kd_ref, fresh_ref, p_ref, t_ref, decay_ref, gram_ref, cols_ref):
    wide = heads * (2 * key + val)
    rows = raw_ref.shape[0]
    first = pl.program_id(0) * rows
    bounds = bounds_of(lengths)
    where_row = first + iota((rows, 1), 0)
    begin = begin_of(where_row, bounds)
    pos = where_row - begin
    u = conv_rows(before_ref[:, :wide].astype(F32), raw_ref[:, :wide].astype(F32), taps_ref[...], pos)
    u_ref[...] = u
    act = u / (1.0 + jnp.exp(-u))
    small = raw_ref[:, wide:].astype(F32)
    lane = iota((SPAN, LANES), 1)
    row_i, col_i = iota((SPAN, SPAN), 0), iota((SPAN, SPAN), 1)
    tri = (row_i >= col_i).astype(F32)
    for c in range(rows // SPAN):
        at = slice(c * SPAN, (c + 1) * SPAN)
        base = first + c * SPAN
        begin_c = begin[at]
        begin_r = begin_of(base + iota((1, SPAN), 1), bounds)
        last_begin = begin_of(base + SPAN - 1 + iota((1, 1), 0), bounds)
        shifted = small[at] + rate_ref[1:2]
        soft = jnp.maximum(shifted, 0.0) + jnp.log(1.0 + jnp.exp(-jnp.abs(shifted)))
        slope = 1.0 / (1.0 + jnp.exp(-shifted))
        logd = jnp.where(lane < heads, -jnp.exp(rate_ref[0:1]) * soft, 0.0)
        beta = 1.0 / (1.0 + jnp.exp(-small[at]))
        total = exact(tri, logd)
        total_t = jnp.transpose(total)
        last = total[SPAN - 1 : SPAN]
        reach = jnp.where(begin_c < base, jnp.exp(total), 0.0)
        tail = jnp.where(begin_c == last_begin, jnp.exp(jnp.where(begin_c == last_begin, last - total, 0.0)), 0.0)
        keep = jnp.where(last_begin < base, jnp.exp(last), 0.0)
        two = heads
        cols_ref[at] = (
            jnp.where(lane < two, reach, 0.0)
            + jnp.where((lane >= two) & (lane < 2 * two), beta, 0.0)
            + pltpu.roll(jnp.where(lane < two, tail, 0.0), 2 * two, 1)
            + pltpu.roll(logd, 3 * two, 1)
            + pltpu.roll(jnp.where(lane < two, keep, 0.0), 4 * two, 1)
            + pltpu.roll(jnp.where(lane < two, slope, 0.0), 5 * two, 1)
        )
        same = begin_c == begin_r
        upto = same & (row_i >= col_i)
        for h in range(heads):
            q = act[at, h * key : (h + 1) * key]
            k = act[at, (heads + h) * key : (heads + h + 1) * key]
            v = act[at, 2 * heads * key + h * val : 2 * heads * key + (h + 1) * val]
            q = q * lax.rsqrt(lane_sum(q * q) + EPS)
            k = k * lax.rsqrt(lane_sum(k * k) + EPS)
            b = beta[:, heads + h : heads + h + 1]
            r = reach[:, h : h + 1]
            spread = total[:, h : h + 1] - total_t[h : h + 1]
            decay = jnp.where(upto, jnp.exp(jnp.where(upto, spread, 0.0)), 0.0)
            both = mm_bt(jnp.concatenate([q, k], axis=0), k)
            gram = jnp.where(row_i > col_i, both[SPAN:] * decay, 0.0)
            inverse = invert(b * gram).astype(BF16)
            kat = slice(h * key, (h + 1) * key)
            cat = slice(h * SPAN, (h + 1) * SPAN)
            vat = slice(h * val, (h + 1) * val)
            solved = mm(inverse, jnp.concatenate([b * v, (b * r) * k], axis=1))
            fresh_ref[at, vat] = solved[:, :val]
            w_ref[at, kat] = solved[:, val:].astype(BF16)
            qe_ref[at, kat] = (r * q).astype(BF16)
            kd_ref[at, kat] = (tail[:, h : h + 1] * k).astype(BF16)
            p_ref[at, cat] = both[:SPAN] * decay
            t_ref[at, cat] = inverse
            decay_ref[at, cat] = decay
            gram_ref[at, cat] = gram


def forward_kernel(heads, key, val, qe_ref, w_ref, kd_ref, fresh_ref, p_ref, cols_ref, gate_ref, gain_ref,
                   out_ref, mixed_ref, new_ref, enter_ref, state):
    @pl.when(pl.program_id(0) == 0)
    def _():
        state[...] = jnp.zeros_like(state)

    for h in range(heads):
        kat = slice(h * key, (h + 1) * key)
        cat = slice(h * SPAN, (h + 1) * SPAN)
        vat = slice(h * val, (h + 1) * val)
        carried = state[h]
        low = carried.astype(BF16)
        enter_ref[0, h] = low
        through = mm(jnp.concatenate([w_ref[:, kat], qe_ref[:, kat]], axis=0), low)
        new = (fresh_ref[:, vat] - through[:SPAN]).astype(BF16)
        new_ref[:, vat] = new
        keep = cols_ref[0:1, 4 * heads + h : 4 * heads + h + 1]
        state[h] = keep * carried + mm_at(kd_ref[:, kat], new)
        mixed = through[SPAN:] + mm(p_ref[:, cat], new)
        mixed_ref[:, vat] = mixed
        gate = gate_ref[:, vat].astype(F32)
        scale = lax.rsqrt(lane_sum(mixed * mixed) * (1.0 / val) + HEAD_FLOOR)
        out_ref[:, vat] = (mixed * scale * gain_ref[...] * (gate / (1.0 + jnp.exp(-gate)))).astype(BF16)


def backward_kernel(heads, key, val, grad_ref, mixed_ref, gate_ref, gain_ref, p_ref, qe_ref, w_ref, kd_ref, cols_ref,
                    ggate_ref, gain_out_ref, do_ref, dn_ref, leave_ref, state):
    @pl.when(pl.program_id(0) == 0)
    def _():
        state[...] = jnp.zeros_like(state)
        gain_out_ref[...] = jnp.zeros_like(gain_out_ref)

    for h in range(heads):
        kat = slice(h * key, (h + 1) * key)
        cat = slice(h * SPAN, (h + 1) * SPAN)
        vat = slice(h * val, (h + 1) * val)
        grad = grad_ref[:, vat].astype(F32)
        mixed = mixed_ref[:, vat]
        gate = gate_ref[:, vat].astype(F32)
        gain = gain_ref[...]
        scale = lax.rsqrt(lane_sum(mixed * mixed) * (1.0 / val) + HEAD_FLOOR)
        sig = 1.0 / (1.0 + jnp.exp(-gate))
        silu = gate * sig
        normed = mixed * scale
        ggate_ref[:, vat] = (grad * normed * gain * (sig + silu * (1.0 - sig))).astype(BF16)
        gs = grad * silu
        gain_out_ref[...] += jnp.sum(gs * normed, axis=0, keepdims=True)
        weighted = gs * gain
        do = scale * (weighted - normed * (lane_sum(weighted * normed) * (1.0 / val)))
        do = do.astype(BF16)
        do_ref[:, vat] = do
        carried = state[h]
        low = carried.astype(BF16)
        leave_ref[0, h] = low
        dn = (mm_at(p_ref[:, cat], do) + mm(kd_ref[:, kat], low)).astype(BF16)
        dn_ref[:, vat] = dn
        keep = cols_ref[0:1, 4 * heads + h : 4 * heads + h + 1]
        state[h] = keep * carried + mm_at(
            jnp.concatenate([qe_ref[:, kat], -w_ref[:, kat]], axis=0), jnp.concatenate([do, dn], axis=0)
        )


def finish_kernel(heads, key, val, lengths, raw_ref, before_ref, taps_ref, rate_ref, u_ref, p_ref, t_ref, decay_ref, gram_ref,
                  cols_ref, new_ref, do_ref, dn_ref, enter_ref, leave_ref, dx_ref, gtaps_ref, gsmall_ref, du_ref):
    wide = heads * (2 * key + val)
    rows = raw_ref.shape[0]
    block = pl.num_programs(0) - 1 - pl.program_id(0)
    first = block * rows
    bounds = bounds_of(lengths)

    @pl.when(pl.program_id(0) == 0)
    def _():
        du_ref[rows:] = jnp.zeros((HALO, wide), F32)
        gtaps_ref[...] = jnp.zeros_like(gtaps_ref)
        gsmall_ref[...] = jnp.zeros_like(gsmall_ref)

    @pl.when(pl.program_id(0) > 0)
    def _():
        du_ref[rows:] = du_ref[:HALO]

    lane = iota((SPAN, LANES), 1)
    row_i, col_i = iota((SPAN, SPAN), 0), iota((SPAN, SPAN), 1)
    tri_up = (row_i <= col_i).astype(F32)
    row_c = iota((SPAN, 1), 0)

    def unit(u):
        sig = 1.0 / (1.0 + jnp.exp(-u))
        act = u * sig
        inv = lax.rsqrt(lane_sum(act * act) + EPS)
        return act * inv, inv, sig * (1.0 + u * (1.0 - sig))

    for c in range(rows // SPAN):
        at = slice(c * SPAN, (c + 1) * SPAN)
        cols = cols_ref[at]
        gtotal = jnp.zeros((SPAN, LANES), F32)
        gcross = jnp.zeros((SPAN, SPAN), F32)
        gbeta = jnp.zeros((SPAN, LANES), F32)
        for h in range(heads):
            qat = slice(h * key, (h + 1) * key)
            kat = slice((heads + h) * key, (heads + h + 1) * key)
            xat = slice(2 * heads * key + h * val, 2 * heads * key + (h + 1) * val)
            cat = slice(h * SPAN, (h + 1) * SPAN)
            vat = slice(h * val, (h + 1) * val)
            reach = cols[:, h : h + 1]
            beta = cols[:, heads + h : heads + h + 1]
            tail = cols[:, 2 * heads + h : 2 * heads + h + 1]
            keep = cols[0:1, 4 * heads + h : 4 * heads + h + 1]
            q, q_inv, q_slope = unit(u_ref[at, qat])
            k, k_inv, k_slope = unit(u_ref[at, kat])
            qb, kb = q.astype(BF16), k.astype(BF16)
            new, do = new_ref[at, vat], do_ref[at, vat]
            enter, leave = enter_ref[c, h], leave_ref[c, h]
            decay, gram = decay_ref[at, cat], gram_ref[at, cat]
            dr = mm_at(t_ref[at, cat], dn_ref[at, vat])
            stacked = jnp.concatenate([do, dr.astype(BF16)], axis=0)
            on_new = mm_bt(stacked, new)
            on_state = mm_bt(stacked, enter)
            dp, dl = on_new[:SPAN], -on_new[SPAN:]
            dqe, drs = on_state[:SPAN], on_state[SPAN:]
            dkd = mm_bt(new, leave)
            dpd = (dp * decay).astype(BF16)
            dkk = jnp.where(row_i > col_i, dl * (beta * decay), 0.0)
            dlg = dl * gram
            change = dp * p_ref[at, cat] + beta * dlg
            dq = reach * dqe + mm(dpd, kb)
            dk = (
                tail * dkd
                - (beta * reach) * drs
                + mm(dkk + jnp.transpose(dkk), kb)
                + mm_at(dpd, qb)
            )
            u_v = u_ref[at, xat]
            v_sig = 1.0 / (1.0 + jnp.exp(-u_v))
            v = u_v * v_sig
            drs_k = lane_sum(drs * k)
            dtail = lane_sum(dkd * k) * tail
            gb = lane_sum(dr * v) - reach * drs_k + lane_sum(dlg)
            dlast = jnp.sum(dtail, axis=0, keepdims=True) + keep * jnp.sum(
                lane_sum(enter.astype(F32) * leave.astype(F32)), axis=0, keepdims=True
            )
            gt = lane_sum(change) + reach * (lane_sum(dqe * q) - beta * drs_k) - dtail
            gt = gt + jnp.where(row_c == SPAN - 1, dlast, 0.0)
            gtotal = gtotal + at_lane(lane, h, gt)
            gcross = gcross + jnp.where(row_i == h, jnp.sum(change, axis=0, keepdims=True), 0.0)
            gbeta = gbeta + at_lane(lane, heads + h, gb * beta * (1.0 - beta))
            du_ref[at, qat] = q_inv * (dq - q * lane_sum(dq * q)) * q_slope
            du_ref[at, kat] = k_inv * (dk - k * lane_sum(dk * k)) * k_slope
            du_ref[at, xat] = (beta * dr) * (v_sig * (1.0 + u_v * (1.0 - v_sig)))
        glog = exact(tri_up, gtotal - jnp.transpose(gcross))
        logd = jnp.where(lane < heads, pltpu.roll(cols, LANES - 3 * heads, 1), 0.0)
        slope = jnp.where(lane < heads, pltpu.roll(cols, LANES - 5 * heads, 1), 0.0)
        gdecay = -glog * jnp.exp(rate_ref[0:1]) * slope
        gsmall_ref[0:1] += jnp.sum(glog * logd, axis=0, keepdims=True)
        gsmall_ref[1:2] += jnp.sum(gdecay, axis=0, keepdims=True)
        dx_ref[at, wide:] = (gdecay + gbeta).astype(BF16)
    where_row = first + iota((rows, 1), 0)
    pos = where_row - begin_of(where_row, bounds)
    ext = jnp.concatenate([before_ref[:, :wide].astype(F32), raw_ref[:, :wide].astype(F32)], axis=0)
    du = du_ref[:rows]
    dx = taps_ref[0:1] * du
    gtaps_ref[0:1] += jnp.sum(du * ext[HALO:], axis=0, keepdims=True)
    for o in range(1, TAPS):
        ahead = where_row + o
        pos_ahead = ahead - begin_of(ahead, bounds)
        dx = dx + jnp.where(pos_ahead >= o, taps_ref[o : o + 1], 0.0) * du_ref[o : o + rows]
        gtaps_ref[o : o + 1] += jnp.sum(
            jnp.where(pos >= o, du, 0.0) * ext[HALO - o : HALO - o + rows], axis=0, keepdims=True
        )
    dx_ref[:, :wide] = dx.astype(BF16)


def cost(flops, moved):
    return pl.CostEstimate(flops=int(flops), bytes_accessed=int(moved), transcendentals=0)


def params():
    return pltpu.CompilerParams(dimension_semantics=("arbitrary",), vmem_limit_bytes=56 * 2**20)


def prepare(raw, taps, rates, lengths, heads, key, val):
    length, width = raw.shape
    wide = heads * (2 * key + val)
    steps = length // ROWS
    ratio = ROWS // HALO
    row = lambda w: pl.BlockSpec((ROWS, w), lambda i: (i, 0))
    whole = lambda a: pl.BlockSpec(a.shape, lambda i: (0, 0))
    shape = lambda w, t: jax.ShapeDtypeStruct((length, w), t)
    kinds = [(wide, F32), (heads * key, BF16), (heads * key, BF16), (heads * key, BF16), (heads * val, F32),
             (heads * SPAN, F32), (heads * SPAN, BF16), (heads * SPAN, F32), (heads * SPAN, F32), (LANES, F32)]
    return pl.pallas_call(
        functools.partial(prepare_kernel, heads, key, val),
        grid=(steps,),
        in_specs=[
            pl.BlockSpec(memory_space=pltpu.SMEM),
            row(width),
            pl.BlockSpec((HALO, width), lambda i: (jnp.maximum(i * ratio - 1, 0), 0)),
            whole(taps),
            whole(rates),
        ],
        out_specs=[row(w) for w, _ in kinds],
        out_shape=[shape(w, t) for w, t in kinds],
        compiler_params=params(),
        cost_estimate=cost(40e9, 40e6),
        name="prepare",
    )(lengths, raw, raw, taps, rates)


def forward(qe, w, kd, fresh, p, cols, gate, gain, heads, key, val):
    length = qe.shape[0]
    steps = length // SPAN
    row = lambda a: pl.BlockSpec((SPAN, a.shape[1]), lambda i: (i, 0))
    given = [qe, w, kd, fresh, p, cols, gate]
    wide = heads * val
    kinds = [(wide, BF16), (wide, F32), (wide, BF16)]
    return pl.pallas_call(
        functools.partial(forward_kernel, heads, key, val),
        grid=(steps,),
        in_specs=[row(a) for a in given] + [pl.BlockSpec(gain.shape, lambda i: (0, 0))],
        out_specs=[pl.BlockSpec((SPAN, wd), lambda i: (i, 0)) for wd, _ in kinds]
        + [pl.BlockSpec((1, heads, key, val), lambda i: (i, 0, 0, 0))],
        out_shape=[jax.ShapeDtypeStruct((length, wd), t) for wd, t in kinds]
        + [jax.ShapeDtypeStruct((steps, heads, key, val), BF16)],
        scratch_shapes=[pltpu.VMEM((heads, key, val), F32)],
        compiler_params=params(),
        cost_estimate=cost(20e9, 20e6),
        name="forward",
    )(*given, gain)


def backward(grad, mixed, gate, gain, p, qe, w, kd, cols, heads, key, val):
    length = qe.shape[0]
    steps = length // SPAN
    row = lambda a: pl.BlockSpec((SPAN, a.shape[1]), lambda i: (steps - 1 - i, 0))
    wide = heads * val
    kinds = [wide, wide, wide]
    back = pl.BlockSpec((SPAN, wide), lambda i: (steps - 1 - i, 0))
    full = jax.ShapeDtypeStruct((length, wide), BF16)
    return pl.pallas_call(
        functools.partial(backward_kernel, heads, key, val),
        grid=(steps,),
        in_specs=[row(grad), row(mixed), row(gate), pl.BlockSpec(gain.shape, lambda i: (0, 0)), row(p), row(qe), row(w),
                  row(kd), row(cols)],
        out_specs=[back, pl.BlockSpec((1, val), lambda i: (0, 0)), back, back,
                   pl.BlockSpec((1, heads, key, val), lambda i: (steps - 1 - i, 0, 0, 0))],
        out_shape=[full, jax.ShapeDtypeStruct((1, val), F32), full, full,
                   jax.ShapeDtypeStruct((steps, heads, key, val), BF16)],
        scratch_shapes=[pltpu.VMEM((heads, key, val), F32)],
        compiler_params=params(),
        cost_estimate=cost(25e9, 25e6),
        name="backward",
    )(grad, mixed, gate, gain, p, qe, w, kd, cols)


def finish(raw, taps, rates, lengths, u, p, t, decay, gram, cols, new, do, dn, enter, leave, heads, key, val):
    length, width = raw.shape
    wide = heads * (2 * key + val)
    steps = length // ROWS
    ratio = ROWS // HALO
    per = ROWS // SPAN
    row = lambda a: pl.BlockSpec((ROWS, a.shape[1]), lambda i: (steps - 1 - i, 0))
    states = pl.BlockSpec((per, heads, key, val), lambda i: (steps - 1 - i, 0, 0, 0))
    whole = lambda a: pl.BlockSpec(a.shape, lambda i: (0, 0))
    fixed = lambda s: pl.BlockSpec(s, lambda i: (0, 0))
    given = [u, p, t, decay, gram, cols, new, do, dn]
    return pl.pallas_call(
        functools.partial(finish_kernel, heads, key, val),
        grid=(steps,),
        in_specs=[
            pl.BlockSpec(memory_space=pltpu.SMEM),
            row(raw),
            pl.BlockSpec((HALO, width), lambda i: (jnp.maximum((steps - 1 - i) * ratio - 1, 0), 0)),
            whole(taps),
            whole(rates),
        ] + [row(a) for a in given] + [states, states],
        out_specs=[row(raw), fixed((8, wide)), fixed((8, LANES))],
        out_shape=[jax.ShapeDtypeStruct((length, width), BF16), jax.ShapeDtypeStruct((8, wide), F32),
                   jax.ShapeDtypeStruct((8, LANES), F32)],
        scratch_shapes=[pltpu.VMEM((ROWS + HALO, wide), F32)],
        compiler_params=params(),
        cost_estimate=cost(60e9, 50e6),
        name="finish",
    )(lengths, raw, raw, taps, rates, *given, enter, leave)


def dense(a, b):
    return jnp.dot(a, b, preferred_element_type=F32)


def dense_t(a, b):
    return lax.dot_general(a, b, (((0,), (0,)), ((), ())), preferred_element_type=F32)


def dense_bt(a, b):
    return lax.dot_general(a, b, (((1,), (1,)), ((), ())), preferred_element_type=F32)


def local(
    residual, cotangent, lengths, token_order, norm_mixer, w_query, w_key, w_value, w_outgate, w_decay, w_beta,
    conv_query, conv_key, conv_value, decay_log, decay_bias, norm_head, w_output, norm_ffn, w_gate, w_up, w_down,
):
    n_ctx, n_tp = lax.axis_size("ctx"), lax.axis_size("tp")
    at_ctx, at_tp = lax.axis_index("ctx"), lax.axis_index("tp")
    rows_d = w_query.shape[0]
    heads = w_decay.shape[1] // n_ctx
    key = w_query.shape[1] // (n_ctx * heads)
    val = w_value.shape[1] // (n_ctx * heads)
    hk, hv = heads * key, heads * val
    wide = 2 * hk + hv
    units = w_gate.shape[1] // n_ctx
    group = token_order.shape[1]
    mine = group // (n_ctx * n_tp)

    def cut(w):
        return w.reshape(rows_d, n_ctx, w.shape[1] // n_ctx)

    def spread(*parts):
        block = jnp.swapaxes(jnp.concatenate(parts, axis=2), 0, 1)
        block = lax.all_to_all(block, "ctx", split_axis=0, concat_axis=0, tiled=True)
        return lax.all_gather(block.reshape(n_ctx * rows_d, -1), "fsdp", axis=0, tiled=True)

    def own(partial):
        block = lax.psum_scatter(partial.astype(BF16), "fsdp", scatter_dimension=0, tiled=True)
        block = block.reshape(n_ctx, rows_d, -1)
        block = lax.all_to_all(block, "ctx", split_axis=0, concat_axis=0, tiled=True)
        return jnp.swapaxes(block, 0, 1).astype(F32)

    def join(block, begin, end):
        return block[:, :, begin:end].reshape(rows_d, -1)

    gains = jnp.stack([norm_mixer, norm_ffn], axis=1)[:, None, :]
    gains = jnp.broadcast_to(gains, (rows_d, n_ctx, 2))
    blank = jnp.zeros((rows_d, n_ctx, LANES - 2 * heads - 2), BF16)
    w_first = spread(cut(w_query), cut(w_key), cut(w_value), cut(w_decay), cut(w_beta), gains, blank)
    w_second = spread(cut(w_outgate), cut(w_output.T))
    w_hidden = spread(cut(w_gate), cut(w_up))
    w_last = spread(cut(w_down.T))
    w_gates, w_out = w_second[:, :hv], w_second[:, hv:]
    n_mix = w_first[:, wide + 2 * heads].astype(F32)
    n_ffn = w_first[:, wide + 2 * heads + 1].astype(F32)

    order = token_order[0]
    inverse = jnp.zeros_like(order).at[order].set(lax.iota(jnp.int32, group))
    tokens = lax.all_gather(residual, "ctx", axis=0, tiled=True)
    packed = tokens[order].astype(F32)
    scale = lax.rsqrt(jnp.mean(packed * packed, axis=-1, keepdims=True) + EPS)
    normed1 = (packed * scale * n_mix).astype(BF16)
    raw = dense(normed1, w_first).astype(BF16)
    gate = dense(normed1, w_gates).astype(BF16)

    first_head = (at_tp * n_ctx + at_ctx) * heads

    def share(conv, width):
        return lax.dynamic_slice_in_dim(conv.astype(F32), first_head * width, heads * width, 1)

    taps = jnp.concatenate([share(conv_query, key), share(conv_key, key), share(conv_value, val)], axis=1)
    taps = jnp.concatenate([taps, jnp.zeros_like(taps)], axis=0)
    rates = jnp.stack([
        lax.dynamic_slice_in_dim(decay_log, first_head, heads, 0),
        lax.dynamic_slice_in_dim(decay_bias, first_head, heads, 0),
    ])
    rates = jnp.pad(rates, ((0, 6), (0, LANES - heads)))
    gain = norm_head.astype(F32)[None, :]
    sizes = (heads, key, val)
    u, qe, wm, kd, fresh, p, solve, decay, gram, cols = prepare(raw, taps, rates, lengths, *sizes)
    headout, mixed, new, enter = forward(qe, wm, kd, fresh, p, cols, gate, gain, *sizes)

    both = ("ctx", "tp")
    given = headout[inverse]
    attention = lax.psum_scatter(
        dense_bt(given, w_out).astype(BF16), both, scatter_dimension=0, tiled=True
    ).astype(F32)
    source = lax.dynamic_slice_in_dim(residual, at_tp * mine, mine, 0).astype(F32)
    middle = source + attention
    scale2 = lax.rsqrt(jnp.mean(middle * middle, axis=-1, keepdims=True) + EPS)
    normed2 = (middle * scale2 * n_ffn).astype(BF16)
    normed2 = lax.all_gather(normed2, both, axis=0, tiled=True)
    hidden = dense(normed2, w_hidden)
    gating, up_part = hidden[:, :units], hidden[:, units:]
    sig = jax.nn.sigmoid(gating)
    silu = gating * sig
    activation = (silu * up_part).astype(BF16)

    cot = lax.all_gather(cotangent, "ctx", axis=0, tiled=True)
    grad_act = dense(cot, w_last)
    grad_gating = (grad_act * up_part * (sig + silu * (1.0 - sig))).astype(BF16)
    grad_up = (grad_act * silu).astype(BF16)
    grad_hidden = jnp.concatenate([grad_gating, grad_up], axis=1)
    grad_normed2 = lax.psum_scatter(
        dense_bt(grad_hidden, w_hidden).astype(BF16), both, scatter_dimension=0, tiled=True
    ).astype(F32)

    def norm_back(u_in, s, n, g):
        weighted = n * g
        return s * weighted - u_in * (s * s * s) * jnp.mean(u_in * weighted, axis=-1, keepdims=True)

    cot_mine = lax.dynamic_slice_in_dim(cotangent, at_tp * mine, mine, 0).astype(F32)
    grad_mid = cot_mine + norm_back(middle, scale2, n_ffn, grad_normed2)
    grad_attn = lax.all_gather(grad_mid.astype(BF16), both, axis=0, tiled=True)
    grad_given = dense(grad_attn, w_out).astype(BF16)

    ffn_out = lax.psum_scatter(
        dense_bt(activation, w_last).astype(BF16), both, scatter_dimension=0, tiled=True
    ).astype(F32)
    output = lax.all_gather((middle + ffn_out).astype(BF16), "tp", axis=0, tiled=True)

    grad_gate, g_gain, do, dn, leave = backward(
        grad_given[order], mixed, gate, gain, p, qe, wm, kd, cols, *sizes
    )
    dx, g_taps, g_small = finish(
        raw, taps, rates, lengths, u, p, solve, decay, gram, cols, new, do, dn, enter, leave, *sizes
    )
    grad_packed = jnp.concatenate([dx, grad_gate], axis=1)
    w_all = jnp.concatenate([w_first, w_gates], axis=1)
    grad_normed1 = lax.psum_scatter(
        dense_bt(grad_packed[inverse], w_all).astype(BF16), both, scatter_dimension=0, tiled=True
    ).astype(F32)
    scale1 = lax.rsqrt(jnp.mean(source * source, axis=-1, keepdims=True) + EPS)
    grad_input = (grad_mid + norm_back(source, scale1, n_mix, grad_normed1)).astype(BF16)
    grad_input = lax.all_gather(grad_input, "tp", axis=0, tiled=True)

    g_hidden = own(dense_t(normed2, grad_hidden))
    g_last = own(dense_t(cot, activation))
    g_out = own(dense_t(grad_attn, given))
    g_gates = own(dense_t(normed1, grad_gate))
    g_first = own(dense_t(normed1, dx))

    gw_gate, gw_up = join(g_hidden, 0, units), join(g_hidden, units, 2 * units)
    gw_down = join(g_last, 0, units).T
    gw_output = join(g_out, 0, hv).T
    gw_outgate = join(g_gates, 0, hv)
    gw_query, gw_key = join(g_first, 0, hk), join(g_first, hk, 2 * hk)
    gw_value = join(g_first, 2 * hk, wide)
    gw_decay = join(g_first, wide, wide + heads)
    gw_beta = join(g_first, wide + heads, wide + 2 * heads)

    def overlap(*pairs):
        return sum(jnp.sum(w.astype(F32) * g, axis=1) for w, g in pairs)

    g_norms = jnp.stack([
        overlap((w_query, gw_query), (w_key, gw_key), (w_value, gw_value), (w_outgate, gw_outgate),
                (w_decay, gw_decay), (w_beta, gw_beta)) / norm_mixer.astype(F32),
        overlap((w_gate, gw_gate), (w_up, gw_up)) / norm_ffn.astype(F32),
    ])
    g_norms = lax.psum(g_norms, "tp")

    def place(like, part, width):
        return lax.dynamic_update_slice_in_dim(jnp.zeros(like, F32), part, first_head * width, len(like) - 1)

    sums = lax.psum(
        jnp.concatenate([
            place(conv_query.shape, g_taps[:TAPS, :hk], key).reshape(-1),
            place(conv_key.shape, g_taps[:TAPS, hk : 2 * hk], key).reshape(-1),
            place(conv_value.shape, g_taps[:TAPS, 2 * hk :], val).reshape(-1),
            place(decay_log.shape, g_small[0, :heads], 1),
            place(decay_bias.shape, g_small[1, :heads], 1),
            g_gain[0],
        ]),
        ("fsdp", "ctx", "tp"),
    )
    pieces, at = [], 0
    for like in (conv_query, conv_key, conv_value, decay_log, decay_bias, norm_head):
        pieces.append(sums[at : at + like.size].reshape(like.shape))
        at += like.size
    return (
        output, grad_input, g_norms[0], gw_query, gw_key, gw_value, gw_outgate, gw_decay, gw_beta,
        *pieces, gw_output, g_norms[1], gw_gate, gw_up, gw_down,
    )


def solution(mesh):
    rows = ("fsdp", "ctx")
    up, down, vector, copied = P(rows, "tp"), P("tp", rows), P(rows), P()
    in_specs = (
        P(rows, None), P(rows, None), P("fsdp", None), P("fsdp", None), vector, up, up, up, up, up, up,
        copied, copied, copied, copied, copied, copied, down, vector, up, up, down,
    )
    out_specs = (
        P(rows, None), P(rows, None), vector, up, up, up, up, up, up,
        copied, copied, copied, copied, copied, copied, down, vector, up, up, down,
    )
    return jax.shard_map(local, mesh=mesh, in_specs=in_specs, out_specs=out_specs, check_vma=False)
```

time: 5040 us -> 1570 us (0.31)
  waiting for transfers between devices: 2570 us -> 980 us
  matrix products: 1080 us -> 194 us
  local copies, waits for them, and re-layouts: 614 us -> 113 us
  other arithmetic: 424 us -> 42 us
  blocking collectives: 214 us -> 59.4 us
  Pallas kernels: 0 us -> 141 us
    reduce_scatter x10 -> x9, waiting for transfers between devices: 1580 us -> 367 us  [the longest x5 161 us: own(): lax.psum_scatter(partial.astype(BF16), 'fsdp', scatter_dimension=0, tiled...]
    dot_general x2238 -> x14, matrix products: 1080 us -> 194 us  [the longest x5 70.3 us: dense(): return jnp.dot(a, b, preferred_element_type=F32)]
    all_gather x16 -> x10, waiting for transfers between devices: 646 us -> 434 us  [the longest x4 199 us: spread(): lax.all_gather(block.reshape(n_ctx * rows_d, -1), 'fsdp', axis=0, tiled=T...]
    psum x5 -> x1, waiting for transfers between devices: 303 us -> 122 us  [local(): lax.psum(jnp.concatenate([place(conv_query.shape, g_taps[:TAPS, :hk], key...]
    squeeze x192 -> x1, local copies, waits for them, and re-layouts: 158 us -> 0.52 us  [local(): g_norms[1]]
    all_gather x8 -> x0, blocking collectives: 155 us -> none  [the longest x2 40.2 us: mixer_weights(): lax.all_gather(n_part, ('fsdp', 'ctx'), axis=0, tiled=True)]
    pallas_call x0 -> x4, Pallas kernels: none -> 141 us  [the longest x1 62.3 us: prepare(): pl.pallas_call(functools.partial(prepare_kernel, heads, key, val), grid=(...]
    mul x236 -> x1, other arithmetic: 120 us -> 0.01 us  [norm_back(): s * s * s]
where the time goes in v1:
time: 1570 us
  waiting for transfers between devices  980 us (62%)
  matrix products  194 us (12%)
  Pallas kernels  141 us (9%)
  local copies, waits for them, and re-layouts  113 us (7%)
  blocking collectives  59.4 us (4%)
  other arithmetic  42 us (3%)
  starting transfers between devices  22.9 us (1%)
    all_gather x4, waiting for transfers between devices, spread(): lax.all_gather(block.reshape(n_ctx * rows_d, -1), 'fsdp', axis=0, tiled=T...  199 us
    reduce_scatter x5, waiting for transfers between devices, own(): lax.psum_scatter(partial.astype(BF16), 'fsdp', scatter_dimension=0, tiled...  161 us
    psum x1, waiting for transfers between devices, local(): lax.psum(jnp.concatenate([place(conv_query.shape, g_taps[:TAPS, :hk], key...  122 us
    reduce_scatter x1, waiting for transfers between devices, local(): lax.psum_scatter(dense_bt(activation, w_last).astype(BF16), both, scatter...  73.2 us
    reduce_scatter x1, waiting for transfers between devices, local(): lax.psum_scatter(dense_bt(grad_hidden, w_hidden).astype(BF16), both, scat...  71.4 us
    dot_general x5, matrix products, dense(): return jnp.dot(a, b, preferred_element_type=F32)  70.3 us
    dot_general x5, matrix products, dense_t(): lax.dot_general(a, b, (((0,), (0,)), ((), ())), preferred_element_type=F32)  65.4 us
    pallas_call x1, Pallas kernels, prepare(): pl.pallas_call(functools.partial(prepare_kernel, heads, key, val), grid=(...  62.3 us
  transfers between devices with their start and end apart: 26, of which 21 were waited for; matrix products, arithmetic and copies ran while one was open for 17% of the time, Pallas kernels for 8%

profile of v1, /device:TPU:0, one launch (start us, length us, event | category | flops | bytes accessed | tf_op | source)
XLA Modules:
  0.0 1568.0 jit_solution(7219861436639523160)
XLA Ops:
  13.0 19.9 %all_to_all.45 = bf16[4,128,1152]{1,2,0:T(8,128)(2,1)S(1)} all-to-all(bf16[4,128,1152]{1,2,0:T(8,128)(2,1)S(1)} %bitcast.127), channel_id=1, replica_groups=mesh['fsdp'=4,'ctx'=4,'tp'=2] {'ctx'}, dimensions={0} | all-to-all | bytes 2359296 | tf_op jit(solution)/shard_map/all_to_all | solution.py:475
  36.5 3.5 all-to-all-start.1
  40.6 8.0 scatter_custom_fusion
  51.5 3.0 all-to-all-done.1
  55.9 68.3 %all-gather.13.cloned.1.call-done = bf16[2048,1152]{1,0:T(8,128)(2,1)} async-done(((bf16[512,1152]{1,0:T(8,128)(2,1)}), bf16[2048,1152]{1,0:T(8,128)(2,1)}) %all-gather.13.cloned.1.call-update) | async-done | bytes 4718608 | tf_op jit(solution)/shard_map/all_gather | solution.py:476
  124.2 2.0 convert_reduce_fusion
  126.2 56.3 %all-gather.11.cloned.1.call-done = bf16[2048,2048]{1,0:T(8,128)(2,1)} async-done(((bf16[512,2048]{1,0:T(8,128)(2,1)}), bf16[2048,2048]{1,0:T(8,128)(2,1)}) %all-gather.11.cloned.1.call-update) | async-done | bytes 8388624 | tf_op jit(solution)/shard_map/all_gather | solution.py:500
  182.5 20.8 %gather_fusion = bf16[2048,2048]{1,0:T(8,128)(2,1)} fusion(bf16[2048,2048]{1,0:T(8,128)(2,1)} %all-gather.11.cloned.1.call-done, s32[2048]{0:T(1024)S(1)} %broadcast_clamp_fusion), kind=kCustom, calls=%fused_computation | custom fusion | bytes 16785408 | tf_op jit(solution)/shard_map/gather | solution.py:501
  203.3 5.3 fusion
  209.2 15.5 convolution_convert_fusion.6.raw_ref.before_ref
  224.7 62.3 %prepare.1 = (f32[2048,1024]{1,0:T(8,128)}, bf16[2048,256]{1,0:T(8,128)(2,1)}, bf16[2048,256]{1,0:T(8,128)(2,1)}, bf16[2048,256]{1,0:T(8,128)(2,1)}, f32[2048,51...) custom-call(s32[1,4]{1,0:T(1,128)} %lengths.3, ...), custom_call_target="tpu_custom_call" | custom-call | flops 40000000000 | bytes 40000000 | tf_op jit(solution)/shard_map/prepare/pallas_call | solution.py:347
  287.0 10.1 convolution_convert_fusion.11.gate_ref
  297.1 16.8 %forward.1 = (bf16[2048,512]{1,0:T(8,128)(2,1)}, f32[2048,512]{1,0:T(8,128)}, bf16[2048,512]{1,0:T(8,128)(2,1)}, bf16[16,2,128,256]{3,2,1,0:T(8,128)(2,1)}) custom-call(bf16[2048,256]{1,0:T(8,128)(2,1)} %get-tuple-element.42.qe_ref, bf16[2048,256]{1,0:T(8,128)(2,1)} %get-tuple-element.43.w_ref, bf16[2048,256]{1,0:T(8,128)(2,1)} %get-tuple-element.44.kd_ref, ...), custom_call_target="tpu_custom_call" | custom-call | flops 20000000000 | bytes 20000000 | tf_op jit(solution)/shard_map/forward/pallas_call | solution.py:372
  313.9 9.5 gather_fusion.1
  323.4 9.1 convolution_convert_fusion.3
  335.2 21.1 %all_to_all.46 = bf16[4,128,1408]{1,2,0:T(8,128)(2,1)S(1)} all-to-all(bf16[4,128,1408]{1,2,0:T(8,128)(2,1)S(1)} %maximum_bitcast_fusion), channel_id=1, replica_groups=mesh['fsdp'=4,'ctx'=4,'tp'=2] {'ctx'}, dimensions={0} | all-to-all | bytes 2883584 | tf_op jit(solution)/shard_map/all_to_all | solution.py:475
  357.9 46.0 %reduce-scatter.10.cloned.1.call-done = bf16[256,2048]{1,0:T(8,128)(2,1)} async-done(((bf16[2048,2048]{1,0:T(8,128)(2,1)}), bf16[256,2048]{1,0:T(8,128)(2,1)}) %reduce-scatter.10.cloned.1.call-update) | async-done | bytes 1048592 | tf_op jit(solution)/shard_map/reduce_scatter | solution.py:526
  405.6 2.6 multiply_convert_fusion.3
  408.3 13.4 all_to_all.47
  423.4 89.3 %all-gather.19.cloned.1.call-done = bf16[2048,1408]{1,0:T(8,128)(2,1)} async-done(((bf16[512,1408]{1,0:T(8,128)(2,1)}), bf16[2048,1408]{1,0:T(8,128)(2,1)}) %all-gather.19.cloned.1.call-update) | async-done | bytes 5767184 | tf_op jit(solution)/shard_map/all_gather | solution.py:476
  512.7 54.6 %all-gather.17.cloned.1.call-done = bf16[2048,2048]{1,0:T(8,128)(2,1)} async-done(((bf16[256,2048]{1,0:T(8,128)(2,1)}), bf16[2048,2048]{1,0:T(8,128)(2,1)}) %all-gather.17.cloned.1.call-update) | async-done | bytes 8388624 | tf_op jit(solution)/shard_map/all_gather | solution.py:533
  567.3 19.2 %fusion.33 = f32[2048,1408]{0,1:T(8,128)} fusion(bf16[2048,2048]{1,0:T(8,128)(2,1)} %all-gather.17.cloned.1.call-done, bf16[2048,1408]{1,0:T(8,128)(2,1)} %all-gather.19.cloned.1.call-done), kind=kOutput, calls=%fused_computation.119 | convolution fusion | flops 11811160064 | bytes 25690112 | tf_op jit(solution)/shard_map/dot_general | solution.py:443
  586.6 41.6 %all-gather.21.cloned.1.call-done = bf16[2048,704]{0,1:T(8,128)(2,1)} async-done(((bf16[512,704]{0,1:T(8,128)(2,1)}), bf16[2048,704]{0,1:T(8,128)(2,1)}) %all-gather.21.cloned.1.call-update) | async-done | bytes 2883600 | tf_op jit(solution)/shard_map/all_gather | solution.py:476
  628.2 58.7 %all-gather.25.cloned.1.call-done = bf16[2048,2048]{1,0:T(8,128)(2,1)} async-done(((bf16[512,2048]{1,0:T(8,128)(2,1)}), bf16[2048,2048]{1,0:T(8,128)(2,1)}) %all-gather.25.cloned.1.call-update) | async-done | bytes 8388624 | tf_op jit(solution)/shard_map/all_gather | solution.py:540
  686.8 17.0 %multiply_convert_fusion.1 = (bf16[2048,704]{0,1:T(8,128)(2,1)}, bf16[2048,704]{0,1:T(8,128)(2,1)}, bf16[2048,704]{0,1:T(8,128)(2,1)}) fusion(f32[2048,1408]{0,1:T(8,128)} %fusion.33, bf16[2048,2048]{1,0:T(8,128)(2,1)} %all-gather.25.cloned.1.call-done, bf16[2048,704]{0,1:T(8,128)(2,1)} %all-gather.21.cloned.1.call-done), kind=kOutput, calls=%fused_computation.23 | convolution fusion | flops 5925765120 | bytes 31457280 | tf_op jit(solution)/shard_map/dot_general | solution.py:443
  703.8 17.5 %convolution_convert_fusion.1 = bf16[2048,2048]{1,0:T(8,128)(2,1)} fusion(bf16[2048,1408]{1,0:T(8,128)(2,1)S(1)} %copy-done.54, bf16[2048,704]{0,1:T(8,128)(2,1)} %get-tuple-element.129, bf16[2048,704]{0,1:T(8,128)(2,1)} %get-tuple-element.128), kind=kOutput, calls=%fused_computation.11 | convolution fusion | flops 11826888704 | bytes 19922944 | tf_op jit(solution)/shard_map/dot_general | solution.py:451
  721.4 71.4 %reduce-scatter.14.cloned.1.call-done = bf16[256,2048]{1,0:T(8,128)(2,1)} async-done(((bf16[2048,2048]{1,0:T(8,128)(2,1)}), bf16[256,2048]{1,0:T(8,128)(2,1)}) %reduce-scatter.14.cloned.1.call-update) | async-done | bytes 1048592 | tf_op jit(solution)/shard_map/reduce_scatter | solution.py:545
  797.0 10.6 fusion.6
  810.2 17.5 %convolution_convert_fusion.4 = bf16[2048,1408]{1,0:T(8,128)(2,1)} fusion(bf16[2048,2048]{1,0:T(8,128)(2,1)} %all-gather.17.cloned.1.call-done, bf16[2048,704]{0,1:T(8,128)(2,1)S(1)} %copy-done.58, bf16[2048,704]{0,1:T(8,128)(2,1)S(1)} %copy-done.57), kind=kOutput, calls=%fused_computation.14 | convolution fusion | flops 11825577984 | bytes 19922944 | tf_op jit(solution)/shard_map/dot_general | solution.py:447
  827.8 23.7 %all-gather.27.cloned.1.call-done = bf16[2048,2048]{1,0:T(8,128)(2,1)} async-done(((bf16[256,2048]{1,0:T(8,128)(2,1)}), bf16[2048,2048]{1,0:T(8,128)(2,1)}) %all-gather.27.cloned.1.call-update) | async-done | bytes 8388624 | tf_op jit(solution)/shard_map/all_gather | solution.py:555
  851.4 8.5 convolution_convert_fusion.10
  860.0 9.6 gather_fusion.2
  869.5 16.8 %backward.1 = (bf16[2048,512]{1,0:T(8,128)(2,1)}, f32[1,256]{1,0:T(1,128)}, bf16[2048,512]{1,0:T(8,128)(2,1)}, bf16[2048,512]{1,0:T(8,128)(2,1)}, bf16[16,2,128,256]{3,2,1,0:T(8,128)(2,1)}) custom-call(bf16[2048,512]{1,0:T(8,128)(2,1)} %gather_fusion.2, f32[2048,512]{1,0:T(8,128)} %get-tuple-element.54.mixed_ref, ...), custom_call_target="tpu_custom_call" | custom-call | flops 24999999488 | bytes 25000000 | tf_op jit(solution)/shard_map/backward/pallas_call | solution.py:395
  886.3 45.5 %finish.1 = (bf16[2048,1152]{1,0:T(8,128)(2,1)}, f32[8,1024]{1,0:T(8,128)}, f32[8,128]{1,0:T(8,128)}) custom-call(s32[1,4]{1,0:T(1,128)} %lengths.3, bf16[2048,1152]{1,0:T(8,128)(2,1)} %convolution_convert_fusion.6.raw_ref.before_ref, bf16[2048,1152]{1,0:T(8,128)(2,1)} %convolution_convert_fusion.6.raw_ref.before_ref, ...), custom_call_target="tpu_custom_call" | custom-call | flops 60000002048 | bytes 50000000 | tf_op jit(solution)/shard_map/finish/pallas_call | solution.py:422
  931.9 5.8 pad_maximum_fusion
  937.6 17.9 %gather_fusion.3 = bf16[2048,1664]{1,0:T(8,128)(2,1)} fusion(bf16[2048,1664]{1,0:T(8,128)(2,1)} %pad_maximum_fusion, s32[2048]{0:T(1024)S(1)} %copy-done.30), kind=kCustom, calls=%fused_computation.3 | custom fusion | bytes 13639680 | tf_op jit(solution)/shard_map/gather | solution.py:572
  955.5 20.6 %convolution_convert_fusion.5 = bf16[2048,2048]{1,0:T(8,128)(2,1)} fusion(bf16[2048,1664]{1,0:T(8,128)(2,1)} %gather_fusion.3, bf16[2048,512]{1,0:T(8,128)(2,1)S(1)} %slice-done, bf16[2048,1152]{1,0:T(8,128)(2,1)} %all-gather.13.cloned.1.call-done), kind=kOutput, calls=%fused_computation.15 | convolution fusion | flops 13976469504 | bytes 22020096 | tf_op jit(solution)/shard_map/dot_general | solution.py:451
  977.9 11.0 convolution_convert_fusion.2
  990.5 9.5 convolution_convert_fusion.8
  1000.1 10.5 convolution_convert_fusion.9
  1013.2 17.3 %convolution_convert_fusion = bf16[2048,1152]{1,0:T(8,128)(2,1)} fusion(bf16[2048,1152]{1,0:T(8,128)(2,1)} %get-tuple-element.59, bf16[2048,2048]{1,0:T(8,128)(2,1)} %gather_fusion, f32[2048]{0:T(1024)S(1)} %copy-done.34, f32[2048]{0:T(1024)S(1)} %copy-done.46), kind=kOutput, calls=%fused_computation.10 | convolution fusion | flops 9682812928 | bytes 17842176 | tf_op jit(solution)/shard_map/dot_general | solution.py:447
  1030.6 2.3 copy_bitcast_fusion.1
  1032.9 3.5 all-to-all-start.8
  1036.4 2.5 copy.114
  1039.0 10.6 all-to-all-done.8
  1049.6 4.4 all-to-all-start.6
  1055.2 30.1 %all-to-all-done.6 = bf16[4,128,1408]{1,2,0:T(8,128)(2,1)} async-done(((bf16[4,128,1408]{1,2,0:T(8,128)(2,1)}), bf16[4,128,1408]{1,2,0:T(8,128)(2,1)}, u32[]{:S(2)}, u32[]{:S(2)}) %all-to-all-start.6) | async-done | bytes 1441824 | tf_op jit(solution)/shard_map/all_to_all | solution.py:481
  1085.3 3.2 convert_bitcast_fusion
  1088.5 15.3 reduce-scatter.16.cloned.1.call-done
  1105.6 73.2 %reduce-scatter.12.cloned.1.call-done = bf16[256,2048]{1,0:T(8,128)(2,1)} async-done(((bf16[2048,2048]{1,0:T(8,128)(2,1)}), bf16[256,2048]{1,0:T(8,128)(2,1)}) %reduce-scatter.12.cloned.1.call-update) | async-done | bytes 1048592 | tf_op jit(solution)/shard_map/reduce_scatter | solution.py:558
  1178.9 4.6 fusion.11
  1183.5 2.0 fusion.29
  1188.6 36.9 %reduce-scatter.24.cloned.1.call-done = bf16[512,512]{1,0:T(8,128)(2,1)} async-done(((bf16[2048,512]{1,0:T(8,128)(2,1)}), bf16[512,512]{1,0:T(8,128)(2,1)}) %reduce-scatter.24.cloned.1.call-update) | async-done | bytes 524304 | tf_op jit(solution)/shard_map/reduce_scatter | solution.py:479
  1225.4 3.5 all-to-all-start.7
  1231.9 39.5 %reduce-scatter.20.cloned.1.call-done = bf16[512,512]{1,0:T(8,128)(2,1)} async-done(((bf16[2048,512]{1,0:T(8,128)(2,1)}), bf16[512,512]{1,0:T(8,128)(2,1)}) %reduce-scatter.20.cloned.1.call-update) | async-done | bytes 524304 | tf_op jit(solution)/shard_map/reduce_scatter | solution.py:479
  1271.5 3.5 all-to-all-start.5
  1275.0 122.1 %all-reduce.4.cloned.1.call-done = f32[33056]{0:T(1024)} async-done(((f32[33056]{0:T(1024)}), f32[33056]{0:T(1024)}) %all-reduce.4.cloned.1.call-update) | async-done | bytes 132240 | tf_op jit(solution)/shard_map/psum | solution.py:606
  1401.9 84.8 %reduce-scatter.18.cloned.1.call-done = bf16[512,1152]{1,0:T(8,128)(2,1)} async-done(((bf16[2048,1152]{1,0:T(8,128)(2,1)}), bf16[512,1152]{1,0:T(8,128)(2,1)}) %reduce-scatter.18.cloned.1.call-update) | async-done | bytes 1179664 | tf_op jit(solution)/shard_map/reduce_scatter | solution.py:479
  1486.7 3.5 all-to-all-start.4
  1495.5 10.5 all-to-all-done.4
  1508.9 5.0 psum.14
  1514.5 7.5 all-gather.29.cloned.1.call-done
  1521.9 34.5 %all-gather.23.cloned.1.call-done = bf16[512,2048]{1,0:T(8,128)(2,1)} async-done(((bf16[256,2048]{1,0:T(8,128)(2,1)}), bf16[512,2048]{1,0:T(8,128)(2,1)}) %all-gather.23.cloned.1.call-update) | async-done | bytes 2097168 | tf_op jit(solution)/shard_map/all_gather | solution.py:561
  1556.5 3.2 copy.139
  (250 shorter events, 59.2 us)
Async XLA Ops:
  7.2 117.0 %all-gather.13.cloned.1.call-start = ((), (), s32[]{:S(2)}) async-start(), calls=%async_computation.19 | async-start | bytes 5898240 | tf_op jit(solution)/shard_map/all_gather | solution.py:476
  32.9 2.5 copy-start.26
  34.3 148.2 %all-gather.11.cloned.1.call-start = ((), (), s32[]{:S(2)}) async-start(), calls=%async_computation.18 | async-start | bytes 10485760 | tf_op jit(solution)/shard_map/all_gather | solution.py:500
  35.1 5.0 copy-start.56
  35.1 5.5 copy-start.44
  35.1 13.6 copy-start.50
  35.1 13.6 copy-start.51
  36.5 18.0 %all-to-all-start.1 = ((bf16[4,128,1024]{1,2,0:T(8,128)(2,1)}), bf16[4,128,1024]{1,2,0:T(8,128)(2,1)S(1)}, u32[]{:S(2)}, u32[]{:S(2)}) async-start(bf16[4,128,1024]{1,2,0:T(8,128)(2,1)} %maximum_bitcast_fusion.1), calls=%async_computation.1 | async-start | bytes 2097152 | tf_op jit(solution)/shard_map/all_to_all | solution.py:475
  40.0 247.0 %all-gather.15.cloned.1.call-start = ((), (), s32[]{:S(2)}) async-start(), calls=%async_computation.20 | async-start | bytes 5242880 | tf_op jit(solution)/shard_map/all_gather | solution.py:476
  51.4 151.9 %copy-start.31 = (s32[2048]{0:T(1024)}, s32[2048]{0:T(1024)S(1)}, u32[]{:S(2)}) copy-start(s32[2048]{0:T(1024)S(1)} %broadcast_clamp_fusion) | copy-start | bytes 24580
  51.4 262.4 %copy-start.29 = (s32[2048]{0:T(1024)}, s32[2048]{0:T(1024)S(1)}, u32[]{:S(2)}) copy-start(s32[2048]{0:T(1024)S(1)} %fusion.15) | copy-start | bytes 24580
  55.7 348.2 %reduce-scatter.10.cloned.1.call-start = ((), (), s32[]{:S(2)}) async-start(), calls=%async_computation.21 | async-start | bytes 9437184 | tf_op jit(solution)/shard_map/reduce_scatter | solution.py:526
  126.2 160.8 %copy-start.33 = (f32[2048]{0:T(1024)}, f32[2048]{0:T(1024)S(1)}, u32[]{:S(2)}) copy-start(f32[2048]{0:T(1024)S(1)} %get-tuple-element.125) | copy-start | bytes 24580
  126.2 668.5 %copy-start.27 = (f32[2048]{0:T(1024)}, f32[2048]{0:T(1024)S(1)}, u32[]{:S(2)}) copy-start(f32[2048]{0:T(1024)S(1)} %get-tuple-element.124) | copy-start | bytes 24580
  203.3 5.8 copy-start
  208.6 78.4 %copy-start.45 = (f32[2048]{0:T(1024)}, f32[2048]{0:T(1024)S(1)}, u32[]{:S(2)}) copy-start(f32[2048]{0:T(1024)S(1)} %add_rsqrt_fusion) | copy-start | bytes 24580
  323.3 9.1 copy-start.11
  332.5 180.2 %all-gather.19.cloned.1.call-start = ((), (), s32[]{:S(2)}) async-start(), calls=%async_computation.23 | async-start | bytes 7208960 | tf_op jit(solution)/shard_map/all_gather | solution.py:476
  356.3 47.6 %copy-start.1 = (bf16[512,2048]{1,0:T(8,128)(2,1)S(1)}, bf16[512,2048]{1,0:T(8,128)(2,1)}, u32[]{:S(2)}) copy-start(bf16[512,2048]{1,0:T(8,128)(2,1)} %param.22) | copy-start | bytes 6291460
  357.8 209.5 %all-gather.17.cloned.1.call-start = ((), (), s32[]{:S(2)}) async-start(), calls=%async_computation.22 | async-start | bytes 9437184 | tf_op jit(solution)/shard_map/all_gather | solution.py:533
  357.9 50.4 %copy-start.25 = (bf16[2816,128]{1,0:T(8,128)(2,1)S(1)}, bf16[2816,128]{1,0:T(8,128)(2,1)}, u32[]{:S(2)}) copy-start(bf16[2816,128]{1,0:T(8,128)(2,1)} %param.43) | copy-start | bytes 2162692
  405.6 389.2 %copy-start.37 = (f32[256]{0:T(256)}, f32[256]{0:T(256)S(1)}, u32[]{:S(2)}) copy-start(f32[256]{0:T(256)S(1)} %get-tuple-element.148) | copy-start | bytes 3076
  405.6 389.2 %copy-start.39 = (f32[256]{0:T(256)}, f32[256]{0:T(256)S(1)}, u32[]{:S(2)}) copy-start(f32[256]{0:T(256)S(1)} %get-tuple-element.147) | copy-start | bytes 3076
  408.2 220.0 %all-gather.21.cloned.1.call-start = ((), (), s32[]{:S(2)}) async-start(), calls=%async_computation.24 | async-start | bytes 3604480 | tf_op jit(solution)/shard_map/all_gather | solution.py:476
  422.6 264.2 %all-gather.25.cloned.1.call-start = ((), (), s32[]{:S(2)}) async-start(), calls=%async_computation.27 | async-start | bytes 10485760 | tf_op jit(solution)/shard_map/all_gather | solution.py:540
  423.4 369.4 %reduce-scatter.14.cloned.1.call-start = ((), (), s32[]{:S(2)}) async-start(), calls=%async_computation.28 | async-start | bytes 9437184 | tf_op jit(solution)/shard_map/reduce_scatter | solution.py:545
  686.8 17.0 %copy-start.54 = (bf16[2048,1408]{1,0:T(8,128)(2,1)S(1)}, bf16[2048,1408]{1,0:T(8,128)(2,1)}, u32[]{:S(2)}) copy-start(bf16[2048,1408]{1,0:T(8,128)(2,1)} %all-gather.19.cloned.1.call-done) | copy-start | bytes 17301508
  721.3 71.5 %copy-start.3 = (bf16[256,2048]{1,0:T(8,128)(2,1)S(1)}, bf16[256,2048]{1,0:T(8,128)(2,1)}, u32[]{:S(2)}) copy-start(bf16[256,2048]{1,0:T(8,128)(2,1)} %reduce-scatter.10.cloned.1.call-done) | copy-start | bytes 3145732
  721.4 130.1 %all-gather.27.cloned.1.call-start = ((), (), s32[]{:S(2)}) async-start(), calls=%async_computation.29 | async-start | bytes 9437184 | tf_op jit(solution)/shard_map/all_gather | solution.py:555
  796.9 233.7 %reduce-scatter.26.cloned.1.call-start = ((), (), s32[]{:S(2)}) async-start(), calls=%async_computation.37 | async-start | bytes 3604480 | tf_op jit(solution)/shard_map/reduce_scatter | solution.py:479
  807.6 228.9 %reduce-scatter.22.cloned.1.call-start = ((), (), s32[]{:S(2)}) async-start(), calls=%async_computation.34 | async-start | bytes 7208960 | tf_op jit(solution)/shard_map/reduce_scatter | solution.py:479
  807.6 2.6 copy-start.58
  827.7 32.2 %copy-start.32 = (s32[2048]{0:T(1024)S(1)}, s32[2048]{0:T(1024)}, u32[]{:S(2)}) copy-start(s32[2048]{0:T(1024)} %copy-done.31) | copy-start | bytes 24580
  827.7 276.1 %reduce-scatter.16.cloned.1.call-start = ((), (), s32[]{:S(2)}) async-start(), calls=%async_computation.30 | async-start | bytes 9437184 | tf_op jit(solution)/shard_map/reduce_scatter | solution.py:571
  886.3 45.6 %copy-start.20 = (bf16[2048,512]{1,0:T(8,128)(2,1)S(1)}, bf16[2048,512]{1,0:T(8,128)(2,1)}, u32[]{:S(2)}) copy-start(bf16[2048,512]{1,0:T(8,128)(2,1)} %get-tuple-element.60) | copy-start | bytes 6291460
  931.8 5.8 copy-start.30
  937.6 17.9 %slice-start = ((bf16[2048,1024]{1,0:T(8,128)(2,1)}), bf16[2048,512]{1,0:T(8,128)(2,1)S(1)}, s32[]{:S(2)}) async-start(bf16[2048,1024]{1,0:T(8,128)(2,1)} %all-gather.15.cloned.1.call-done), calls=%async_computation.38 | async-start | bytes 4194304 | tf_op jit(solution)/shard_map/slice | solution.py:494
  976.1 202.8 %reduce-scatter.12.cloned.1.call-start = ((), (), s32[]{:S(2)}) async-start(), calls=%async_computation.25 | async-start | bytes 9437184 | tf_op jit(solution)/shard_map/reduce_scatter | solution.py:558
  988.9 11.2 copy-start.34
  988.9 11.2 copy-start.46
  988.9 236.5 %reduce-scatter.24.cloned.1.call-start = ((), (), s32[]{:S(2)}) async-start(), calls=%async_computation.36 | async-start | bytes 2621440 | tf_op jit(solution)/shard_map/reduce_scatter | solution.py:479
  1000.0 10.7 copy-start.43
  1000.0 12.4 copy-start.49
  1000.0 271.4 %reduce-scatter.20.cloned.1.call-start = ((), (), s32[]{:S(2)}) async-start(), calls=%async_computation.33 | async-start | bytes 2621440 | tf_op jit(solution)/shard_map/reduce_scatter | solution.py:479
  1010.7 386.4 %all-reduce.4.cloned.1.call-start = ((), (), s32[]{:S(2)}) async-start(), calls=%async_computation.35 | async-start | bytes 270336 | tf_op jit(solution)/shard_map/psum | solution.py:606
  1013.2 473.5 %reduce-scatter.18.cloned.1.call-start = ((), (), s32[]{:S(2)}) async-start(), calls=%async_computation.32 | async-start | bytes 5898240 | tf_op jit(solution)/shard_map/reduce_scatter | solution.py:479
  1032.9 16.7 %all-to-all-start.8 = ((bf16[4,128,704]{1,2,0:T(8,128)(2,1)}), bf16[4,128,704]{1,2,0:T(8,128)(2,1)S(1)}, u32[]{:S(2)}, u32[]{:S(2)}) async-start(bf16[4,128,704]{1,2,0:T(8,128)(2,1)} %copy_bitcast_fusion.1), calls=%async_computation.17 | async-start | bytes 1441792 | tf_op jit(solution)/shard_map/all_to_all | solution.py:481
  1049.6 35.8 %all-to-all-start.6 = ((bf16[4,128,1408]{1,2,0:T(8,128)(2,1)}), bf16[4,128,1408]{1,2,0:T(8,128)(2,1)}, u32[]{:S(2)}, u32[]{:S(2)}) async-start(bf16[4,128,1408]{1,2,0:T(8,128)(2,1)} %copy.114), calls=%async_computation.13 | async-start | bytes 2883584 | tf_op jit(solution)/shard_map/all_to_all | solution.py:481
  1053.9 49.9 %copy-start.2 = (bf16[512,2048]{1,0:T(8,128)(2,1)S(1)}, bf16[512,2048]{1,0:T(8,128)(2,1)}, u32[]{:S(2)}) copy-start(bf16[512,2048]{1,0:T(8,128)(2,1)} %param.22) | copy-start | bytes 6291460
  1054.0 468.0 %all-gather.29.cloned.1.call-start = ((), (), s32[]{:S(2)}) async-start(), calls=%async_computation.31 | async-start | bytes 3145728 | tf_op jit(solution)/shard_map/all_gather | solution.py:576
  1055.2 123.6 %copy-start.4 = (bf16[256,2048]{1,0:T(8,128)(2,1)S(1)}, bf16[256,2048]{1,0:T(8,128)(2,1)}, u32[]{:S(2)}) copy-start(bf16[256,2048]{1,0:T(8,128)(2,1)} %reduce-scatter.10.cloned.1.call-done) | copy-start | bytes 3145732
  1055.2 123.6 %copy-start.28 = (f32[2048]{0:T(1024)S(1)}, f32[2048]{0:T(1024)}, u32[]{:S(2)}) copy-start(f32[2048]{0:T(1024)} %copy-done.27) | copy-start | bytes 24580
  1055.2 123.6 %copy-start.38 = (f32[256]{0:T(256)S(1)}, f32[256]{0:T(256)}, u32[]{:S(2)}) copy-start(f32[256]{0:T(256)} %copy-done.37) | copy-start | bytes 3076
  1055.2 123.6 %copy-start.40 = (f32[256]{0:T(256)S(1)}, f32[256]{0:T(256)}, u32[]{:S(2)}) copy-start(f32[256]{0:T(256)} %copy-done.39) | copy-start | bytes 3076
  1055.2 123.6 %copy-start.42 = (f32[256]{0:T(256)S(1)}, f32[256]{0:T(256)}, u32[]{:S(2)}) copy-start(f32[256]{0:T(256)} %copy-done.41) | copy-start | bytes 3076
  1225.4 46.0 %all-to-all-start.7 = ((bf16[4,128,512]{2,1,0:T(8,128)(2,1)}), bf16[4,128,512]{2,1,0:T(8,128)(2,1)S(1)}, u32[]{:S(2)}, u32[]{:S(2)}) async-start(bf16[4,128,512]{2,1,0:T(8,128)(2,1)} %bitcast.147), calls=%async_computation.15 | async-start | bytes 1048576 | tf_op jit(solution)/shard_map/all_to_all | solution.py:481
  1228.9 46.0 %copy-start.52 = (bf16[128]{0:T(256)(128)(2,1)S(1)}, bf16[128]{0:T(256)(128)(2,1)}, u32[]{:S(2)}) copy-start(bf16[128]{0:T(256)(128)(2,1)} %param.40) | copy-start | bytes 772
  1271.5 215.2 %copy-start.13 = (bf16[4,128,512]{2,1,0:T(8,128)(2,1)}, bf16[4,128,512]{2,1,0:T(8,128)(2,1)S(1)}, u32[]{:S(2)}) copy-start(bf16[4,128,512]{2,1,0:T(8,128)(2,1)S(1)} %all-to-all-done.7) | copy-start | bytes 1572868
  1271.5 130.4 %all-to-all-start.5 = ((bf16[4,128,512]{2,1,0:T(8,128)(2,1)}), bf16[4,128,512]{2,1,0:T(8,128)(2,1)S(1)}, u32[]{:S(2)}, u32[]{:S(2)}) async-start(bf16[4,128,512]{2,1,0:T(8,128)(2,1)} %bitcast.146), calls=%async_computation.11 | async-start | bytes 1048576 | tf_op jit(solution)/shard_map/all_to_all | solution.py:481
  1486.7 19.4 %all-to-all-start.4 = ((bf16[4,128,1152]{2,1,0:T(8,128)(2,1)}), bf16[4,128,1152]{2,1,0:T(8,128)(2,1)S(1)}, u32[]{:S(2)}, u32[]{:S(2)}) async-start(bf16[4,128,1152]{2,1,0:T(8,128)(2,1)} %bitcast.141), calls=%async_computation.9 | async-start | bytes 2359296 | tf_op jit(solution)/shard_map/all_to_all | solution.py:481
  1490.2 66.3 %all-gather.23.cloned.1.call-start = ((), (), s32[]{:S(2)}) async-start(), calls=%async_computation.26 | async-start | bytes 3145728 | tf_op jit(solution)/shard_map/all_gather | solution.py:561
  1492.8 2.5 copy-start.16
  1507.0 52.6 %copy-start.10 = (f32[4,16,8,512]{3,2,0,1:T(8,128)}, f32[4,16,8,512]{3,2,0,1:T(8,128)S(1)}, u32[]{:S(2)}) copy-start(f32[4,16,8,512]{3,2,0,1:T(8,128)S(1)} %copy.124) | copy-start | bytes 3145732
  1521.9 37.7 %copy-start.14 = (bf16[512,2048]{1,0:T(8,128)(2,1)S(1)}, bf16[512,2048]{1,0:T(8,128)(2,1)}, u32[]{:S(2)}) copy-start(bf16[512,2048]{1,0:T(8,128)(2,1)} %all-gather.29.cloned.1.call-done) | copy-start | bytes 6291460
  (22 other events, 30.7 us)
Sparse Core Ops, SparseCore 0:
  34.4 89.7 all-gather.12
  125.8 56.7 all-gather.10
  184.1 80.7 all-gather.14
  332.6 71.2 reduce-scatter.9
  406.0 106.6 all-gather.18
  514.6 52.6 all-gather.16
  569.0 59.1 all-gather.20
  629.8 57.0 all-gather.24
  721.5 71.2 reduce-scatter.13
  797.0 54.3 all-gather.26
  853.7 56.1 reduce-scatter.25
  912.1 102.0 reduce-scatter.21
  1017.7 86.0 reduce-scatter.15
  1107.5 71.2 reduce-scatter.11
  1181.6 43.8 reduce-scatter.23
  1228.3 43.1 reduce-scatter.19
  1277.4 119.5 all-reduce.3
  1399.2 87.4 reduce-scatter.17
  1488.2 33.6 all-gather.28
  1523.3 33.1 all-gather.22

commit v2 on v1

--- a/solution.py
+++ b/solution.py
@@ -84,19 +84,22 @@
     return total
 
 
-def prepare_kernel(heads, key, val, lengths, raw_ref, before_ref, taps_ref, rate_ref,
+def prepare_kernel(heads, key, val, n_wait, lengths, raw_ref, before_ref, small_ref, taps_ref, rate_ref, *refs):
+    prepare_block(heads, key, val, lengths, raw_ref, before_ref, small_ref, taps_ref, rate_ref, *refs[n_wait:])
+
+
+def prepare_block(heads, key, val, lengths, raw_ref, before_ref, small_ref, taps_ref, rate_ref,
                    u_ref, qe_ref, w_ref, kd_ref, fresh_ref, p_ref, t_ref, decay_ref, gram_ref, cols_ref):
-    wide = heads * (2 * key + val)
     rows = raw_ref.shape[0]
     first = pl.program_id(0) * rows
     bounds = bounds_of(lengths)
     where_row = first + iota((rows, 1), 0)
     begin = begin_of(where_row, bounds)
     pos = where_row - begin
-    u = conv_rows(before_ref[:, :wide].astype(F32), raw_ref[:, :wide].astype(F32), taps_ref[...], pos)
+    u = conv_rows(before_ref[...].astype(F32), raw_ref[...].astype(F32), taps_ref[...], pos)
     u_ref[...] = u
     act = u / (1.0 + jnp.exp(-u))
-    small = raw_ref[:, wide:].astype(F32)
+    small = small_ref[...].astype(F32)
     lane = iota((SPAN, LANES), 1)
     row_i, col_i = iota((SPAN, SPAN), 0), iota((SPAN, SPAN), 1)
     tri = (row_i >= col_i).astype(F32)
@@ -155,12 +158,16 @@
             gram_ref[at, cat] = gram
 
 
-def forward_kernel(heads, key, val, qe_ref, w_ref, kd_ref, fresh_ref, p_ref, cols_ref, gate_ref, gain_ref,
-                   out_ref, mixed_ref, new_ref, enter_ref, state):
+def forward_kernel(heads, key, val, n_wait, qe_ref, w_ref, kd_ref, fresh_ref, p_ref, cols_ref, normed_ref, gate_w_ref,
+                   gain_ref, *refs):
+    out_ref, mixed_ref, new_ref, gate_ref, enter_ref, state = refs[n_wait:]
+
     @pl.when(pl.program_id(0) == 0)
     def _():
         state[...] = jnp.zeros_like(state)
 
+    gates = mm(normed_ref[...], gate_w_ref[...]).astype(BF16)
+    gate_ref[...] = gates
     for h in range(heads):
         kat = slice(h * key, (h + 1) * key)
         cat = slice(h * SPAN, (h + 1) * SPAN)
@@ -175,13 +182,15 @@
         state[h] = keep * carried + mm_at(kd_ref[:, kat], new)
         mixed = through[SPAN:] + mm(p_ref[:, cat], new)
         mixed_ref[:, vat] = mixed
-        gate = gate_ref[:, vat].astype(F32)
+        gate = gates[:, vat].astype(F32)
         scale = lax.rsqrt(lane_sum(mixed * mixed) * (1.0 / val) + HEAD_FLOOR)
         out_ref[:, vat] = (mixed * scale * gain_ref[...] * (gate / (1.0 + jnp.exp(-gate)))).astype(BF16)
 
 
-def backward_kernel(heads, key, val, grad_ref, mixed_ref, gate_ref, gain_ref, p_ref, qe_ref, w_ref, kd_ref, cols_ref,
-                    ggate_ref, gain_out_ref, do_ref, dn_ref, leave_ref, state):
+def backward_kernel(heads, key, val, n_wait, grad_ref, mixed_ref, gate_ref, gain_ref, p_ref, qe_ref, w_ref, kd_ref,
+                    cols_ref, *refs):
+    ggate_ref, gain_out_ref, do_ref, dn_ref, leave_ref, state = refs[n_wait:]
+
     @pl.when(pl.program_id(0) == 0)
     def _():
         state[...] = jnp.zeros_like(state)
@@ -217,8 +226,9 @@
         )
 
 
-def finish_kernel(heads, key, val, lengths, raw_ref, before_ref, taps_ref, rate_ref, u_ref, p_ref, t_ref, decay_ref, gram_ref,
-                  cols_ref, new_ref, do_ref, dn_ref, enter_ref, leave_ref, dx_ref, gtaps_ref, gsmall_ref, du_ref):
+def finish_kernel(heads, key, val, n_wait, lengths, raw_ref, before_ref, taps_ref, rate_ref, u_ref, p_ref, t_ref, decay_ref,
+                  gram_ref, cols_ref, new_ref, do_ref, dn_ref, ggate_ref, enter_ref, leave_ref, *refs):
+    dx_ref, dsmall_ref, all_ref, gtaps_ref, gsmall_ref, du_ref = refs[n_wait:]
     wide = heads * (2 * key + val)
     rows = raw_ref.shape[0]
     block = pl.num_programs(0) - 1 - pl.program_id(0)
@@ -309,10 +319,10 @@
         gdecay = -glog * jnp.exp(rate_ref[0:1]) * slope
         gsmall_ref[0:1] += jnp.sum(glog * logd, axis=0, keepdims=True)
         gsmall_ref[1:2] += jnp.sum(gdecay, axis=0, keepdims=True)
-        dx_ref[at, wide:] = (gdecay + gbeta).astype(BF16)
+        dsmall_ref[at] = (gdecay + gbeta).astype(BF16)
     where_row = first + iota((rows, 1), 0)
     pos = where_row - begin_of(where_row, bounds)
-    ext = jnp.concatenate([before_ref[:, :wide].astype(F32), raw_ref[:, :wide].astype(F32)], axis=0)
+    ext = jnp.concatenate([before_ref[...].astype(F32), raw_ref[...].astype(F32)], axis=0)
     du = du_ref[:rows]
     dx = taps_ref[0:1] * du
     gtaps_ref[0:1] += jnp.sum(du * ext[HALO:], axis=0, keepdims=True)
@@ -323,18 +333,22 @@
         gtaps_ref[o : o + 1] += jnp.sum(
             jnp.where(pos >= o, du, 0.0) * ext[HALO - o : HALO - o + rows], axis=0, keepdims=True
         )
-    dx_ref[:, :wide] = dx.astype(BF16)
-
-
-def cost(flops, moved):
-    return pl.CostEstimate(flops=int(flops), bytes_accessed=int(moved), transcendentals=0)
+    dx = dx.astype(BF16)
+    dx_ref[...] = dx
+    all_ref[:, :wide] = dx
+    all_ref[:, wide : wide + heads * val] = ggate_ref[...]
+    all_ref[:, wide + heads * val :] = dsmall_ref[...]
+
+
+def cost(micros):
+    return pl.CostEstimate(flops=int(micros * 1.15e9), bytes_accessed=int(micros * 1e6), transcendentals=0)
 
 
 def params():
     return pltpu.CompilerParams(dimension_semantics=("arbitrary",), vmem_limit_bytes=56 * 2**20)
 
 
-def prepare(raw, taps, rates, lengths, heads, key, val):
+def prepare(raw, small, taps, rates, lengths, heads, key, val, wait=()):
     length, width = raw.shape
     wide = heads * (2 * key + val)
     steps = length // ROWS
@@ -345,46 +359,49 @@
     kinds = [(wide, F32), (heads * key, BF16), (heads * key, BF16), (heads * key, BF16), (heads * val, F32),
              (heads * SPAN, F32), (heads * SPAN, BF16), (heads * SPAN, F32), (heads * SPAN, F32), (LANES, F32)]
     return pl.pallas_call(
-        functools.partial(prepare_kernel, heads, key, val),
+        functools.partial(prepare_kernel, heads, key, val, len(wait)),
         grid=(steps,),
         in_specs=[
             pl.BlockSpec(memory_space=pltpu.SMEM),
             row(width),
             pl.BlockSpec((HALO, width), lambda i: (jnp.maximum(i * ratio - 1, 0), 0)),
+            row(LANES),
             whole(taps),
             whole(rates),
-        ],
+        ] + [pl.BlockSpec(memory_space=pl.ANY)] * len(wait),
         out_specs=[row(w) for w, _ in kinds],
         out_shape=[shape(w, t) for w, t in kinds],
         compiler_params=params(),
-        cost_estimate=cost(40e9, 40e6),
+        cost_estimate=cost(0.1),
         name="prepare",
-    )(lengths, raw, raw, taps, rates)
-
-
-def forward(qe, w, kd, fresh, p, cols, gate, gain, heads, key, val):
+    )(lengths, raw, raw, small, taps, rates, *wait)
+
+
+def forward(qe, w, kd, fresh, p, cols, normed, gate_w, gain, heads, key, val, wait=()):
     length = qe.shape[0]
     steps = length // SPAN
     row = lambda a: pl.BlockSpec((SPAN, a.shape[1]), lambda i: (i, 0))
-    given = [qe, w, kd, fresh, p, cols, gate]
+    given = [qe, w, kd, fresh, p, cols, normed]
     wide = heads * val
-    kinds = [(wide, BF16), (wide, F32), (wide, BF16)]
-    return pl.pallas_call(
-        functools.partial(forward_kernel, heads, key, val),
+    kinds = [(wide, BF16), (wide, F32), (wide, BF16), (wide, BF16)]
+    return pl.pallas_call(
+        functools.partial(forward_kernel, heads, key, val, len(wait)),
         grid=(steps,),
-        in_specs=[row(a) for a in given] + [pl.BlockSpec(gain.shape, lambda i: (0, 0))],
+        in_specs=[row(a) for a in given]
+        + [pl.BlockSpec((gate_w.shape[0], wide), lambda i: (0, 0)), pl.BlockSpec(gain.shape, lambda i: (0, 0))]
+        + [pl.BlockSpec(memory_space=pl.ANY)] * len(wait),
         out_specs=[pl.BlockSpec((SPAN, wd), lambda i: (i, 0)) for wd, _ in kinds]
         + [pl.BlockSpec((1, heads, key, val), lambda i: (i, 0, 0, 0))],
         out_shape=[jax.ShapeDtypeStruct((length, wd), t) for wd, t in kinds]
         + [jax.ShapeDtypeStruct((steps, heads, key, val), BF16)],
         scratch_shapes=[pltpu.VMEM((heads, key, val), F32)],
         compiler_params=params(),
-        cost_estimate=cost(20e9, 20e6),
+        cost_estimate=cost(0.1),
         name="forward",
-    )(*given, gain)
-
-
-def backward(grad, mixed, gate, gain, p, qe, w, kd, cols, heads, key, val):
+    )(*given, gate_w, gain, *wait)
+
+
+def backward(grad, mixed, gate, gain, p, qe, w, kd, cols, heads, key, val, wait=()):
     length = qe.shape[0]
     steps = length // SPAN
     row = lambda a: pl.BlockSpec((SPAN, a.shape[1]), lambda i: (steps - 1 - i, 0))
@@ -393,22 +410,22 @@
     back = pl.BlockSpec((SPAN, wide), lambda i: (steps - 1 - i, 0))
     full = jax.ShapeDtypeStruct((length, wide), BF16)
     return pl.pallas_call(
-        functools.partial(backward_kernel, heads, key, val),
+        functools.partial(backward_kernel, heads, key, val, len(wait)),
         grid=(steps,),
         in_specs=[row(grad), row(mixed), row(gate), pl.BlockSpec(gain.shape, lambda i: (0, 0)), row(p), row(qe), row(w),
-                  row(kd), row(cols)],
+                  row(kd), row(cols)] + [pl.BlockSpec(memory_space=pl.ANY)] * len(wait),
         out_specs=[back, pl.BlockSpec((1, val), lambda i: (0, 0)), back, back,
                    pl.BlockSpec((1, heads, key, val), lambda i: (steps - 1 - i, 0, 0, 0))],
         out_shape=[full, jax.ShapeDtypeStruct((1, val), F32), full, full,
                    jax.ShapeDtypeStruct((steps, heads, key, val), BF16)],
         scratch_shapes=[pltpu.VMEM((heads, key, val), F32)],
         compiler_params=params(),
-        cost_estimate=cost(25e9, 25e6),
+        cost_estimate=cost(0.1),
         name="backward",
-    )(grad, mixed, gate, gain, p, qe, w, kd, cols)
-
-
-def finish(raw, taps, rates, lengths, u, p, t, decay, gram, cols, new, do, dn, enter, leave, heads, key, val):
+    )(grad, mixed, gate, gain, p, qe, w, kd, cols, *wait)
+
+
+def finish(raw, taps, rates, lengths, u, p, t, decay, gram, cols, new, do, dn, ggate, enter, leave, heads, key, val, wait=()):
     length, width = raw.shape
     wide = heads * (2 * key + val)
     steps = length // ROWS
@@ -418,9 +435,11 @@
     states = pl.BlockSpec((per, heads, key, val), lambda i: (steps - 1 - i, 0, 0, 0))
     whole = lambda a: pl.BlockSpec(a.shape, lambda i: (0, 0))
     fixed = lambda s: pl.BlockSpec(s, lambda i: (0, 0))
-    given = [u, p, t, decay, gram, cols, new, do, dn]
-    return pl.pallas_call(
-        functools.partial(finish_kernel, heads, key, val),
+    given = [u, p, t, decay, gram, cols, new, do, dn, ggate]
+    every = wide + heads * val + LANES
+    out_row = lambda w: pl.BlockSpec((ROWS, w), lambda i: (steps - 1 - i, 0))
+    return pl.pallas_call(
+        functools.partial(finish_kernel, heads, key, val, len(wait)),
         grid=(steps,),
         in_specs=[
             pl.BlockSpec(memory_space=pltpu.SMEM),
@@ -428,15 +447,194 @@
             pl.BlockSpec((HALO, width), lambda i: (jnp.maximum((steps - 1 - i) * ratio - 1, 0), 0)),
             whole(taps),
             whole(rates),
-        ] + [row(a) for a in given] + [states, states],
-        out_specs=[row(raw), fixed((8, wide)), fixed((8, LANES))],
-        out_shape=[jax.ShapeDtypeStruct((length, width), BF16), jax.ShapeDtypeStruct((8, wide), F32),
-                   jax.ShapeDtypeStruct((8, LANES), F32)],
+        ] + [row(a) for a in given] + [states, states] + [pl.BlockSpec(memory_space=pl.ANY)] * len(wait),
+        out_specs=[out_row(wide), out_row(LANES), out_row(every), fixed((8, wide)), fixed((8, LANES))],
+        out_shape=[*(jax.ShapeDtypeStruct((length, w), BF16) for w in (wide, LANES, every)), jax.ShapeDtypeStruct((8, wide), F32),
+              jax.ShapeDtypeStruct((8, LANES), F32)],
         scratch_shapes=[pltpu.VMEM((ROWS + HALO, wide), F32)],
         compiler_params=params(),
-        cost_estimate=cost(60e9, 50e6),
+        cost_estimate=cost(0.1),
         name="finish",
-    )(lengths, raw, raw, taps, rates, *given, enter, leave)
+    )(lengths, raw, raw, taps, rates, *given, enter, leave, *wait)
+
+
+def rows_kernel(order_ref, gain_ref, thin_ref, *refs):
+    pieces, (normed_ref, logits_ref) = refs[:-2], refs[-2:]
+    order, size = order_ref[...], pieces[0].shape[0]
+    token = iota((order.shape[0], size), 1)
+    rows = sum(
+        jnp.dot((order == token + i * size).astype(BF16), piece[...], preferred_element_type=F32)
+        for i, piece in enumerate(pieces)
+    )
+    scale = lax.rsqrt(lane_sum(rows * rows) * (1.0 / rows.shape[1]) + EPS)
+    normed = (rows * scale * gain_ref[...]).astype(BF16)
+    normed_ref[...] = normed
+    logits_ref[...] = mm_bt(normed, thin_ref[...]).astype(BF16)
+
+
+def packed_rows(order, gain, thin, pieces):
+    length, size, wide = order.shape[0], 256, gain.shape[1]
+    row = lambda w: pl.BlockSpec((size, w), lambda i: (i, 0))
+    whole = lambda a: pl.BlockSpec(a.shape, lambda i: (0, 0))
+    return pl.pallas_call(
+        rows_kernel,
+        grid=(length // size,),
+        in_specs=[row(1), whole(gain), whole(thin)] + [whole(p) for p in pieces],
+        out_specs=[row(wide), row(LANES)],
+        out_shape=[jax.ShapeDtypeStruct((length, w), BF16) for w in (wide, LANES)],
+        compiler_params=params(),
+        cost_estimate=cost(26),
+        name="packed_rows",
+    )(order, gain, thin, *pieces)
+
+
+def hidden_kernel(rows_ref, gate_ref, up_ref, grad_ref, act_ref, both_ref):
+    rows = rows_ref[...]
+    gating = jnp.dot(rows, gate_ref[...], preferred_element_type=F32)
+    up = jnp.dot(rows, up_ref[...], preferred_element_type=F32)
+    sig = 1.0 / (1.0 + jnp.exp(-gating))
+    silu = gating * sig
+    grad = grad_ref[...]
+    act_ref[...] = (silu * up).astype(BF16)
+    ggate = (grad * up * (sig + silu * (1.0 - sig))).astype(BF16)
+    gup = (grad * silu).astype(BF16)
+    both_ref[:, : ggate.shape[1]] = ggate
+    both_ref[:, ggate.shape[1] :] = gup
+
+
+def hidden_units(rows, gate, up, grad):
+    (length, wide), units, size = rows.shape, gate.shape[1], 256
+    row = lambda w: pl.BlockSpec((size, w), lambda i: (i, 0))
+    weight = pl.BlockSpec(gate.shape, lambda i: (0, 0))
+    return pl.pallas_call(
+        hidden_kernel,
+        grid=(length // size,),
+        in_specs=[row(wide), weight, weight, row(units)],
+        out_specs=[row(units), row(2 * units)],
+        out_shape=[jax.ShapeDtypeStruct((length, w), BF16) for w in (units, 2 * units)],
+        compiler_params=params(),
+        cost_estimate=cost(0.1),
+        name="hidden_units",
+    )(rows, gate, up, grad)
+
+
+def in_vmem(count):
+    return [pl.BlockSpec(memory_space=pltpu.VMEM)] * count
+
+
+def deal_kernel(n_parts, at, *refs):
+    parts, outs = refs[:n_parts], refs[n_parts:]
+    for d, out in enumerate(outs):
+        for c in range(len(outs)):
+
+            @pl.when((at[0] ^ d) == c)
+            def _(out=out, c=c):
+                begin = 0
+                for part in parts:
+                    width = part.shape[1] // len(outs)
+                    out[:, begin : begin + width] = part[:, c * width : (c + 1) * width]
+                    begin += width
+
+
+def deal(at, parts, count):
+    rows, width = parts[0].shape[0], sum(p.shape[1] for p in parts) // count
+    return pl.pallas_call(
+        functools.partial(deal_kernel, len(parts)),
+        in_specs=[pl.BlockSpec(memory_space=pltpu.SMEM)] + in_vmem(len(parts)),
+        out_specs=in_vmem(count),
+        out_shape=[jax.ShapeDtypeStruct((rows, width), BF16)] * count,
+        cost_estimate=cost(3),
+        name="deal",
+    )(at, *parts)
+
+
+def stack_kernel(count, at, *refs):
+    blocks, outs, rows = refs[:count], refs[count:], refs[0].shape[0]
+    for d, block in enumerate(blocks):
+        begin = 0
+        for out in outs:
+            width = out.shape[1]
+            out[pl.ds(pl.multiple_of((at[0] ^ d) * rows, rows), rows), :] = block[:, begin : begin + width]
+            begin += width
+
+
+def stack(at, blocks, widths):
+    rows = blocks[0].shape[0]
+    return pl.pallas_call(
+        functools.partial(stack_kernel, len(blocks)),
+        in_specs=[pl.BlockSpec(memory_space=pltpu.SMEM)] + in_vmem(len(blocks)),
+        out_specs=in_vmem(len(widths)),
+        out_shape=[jax.ShapeDtypeStruct((len(blocks) * rows, w), BF16) for w in widths],
+        cost_estimate=cost(2),
+        name="stack",
+    )(at, *blocks)
+
+
+def collect_kernel(count, at, *refs):
+    blocks, outs = refs[:count], refs[count:]
+    for d, block in enumerate(blocks):
+        for c in range(count):
+
+            @pl.when((at[0] ^ d) == c)
+            def _(block=block, c=c):
+                begin = 0
+                for out in outs:
+                    width = out.shape[1] // count
+                    out[:, c * width : (c + 1) * width] = block[:, begin : begin + width].astype(F32)
+                    begin += width
+
+
+def collect(at, blocks, widths):
+    rows, count = blocks[0].shape[0], len(blocks)
+    return pl.pallas_call(
+        functools.partial(collect_kernel, count),
+        in_specs=[pl.BlockSpec(memory_space=pltpu.SMEM)] + in_vmem(count),
+        out_specs=in_vmem(len(widths)),
+        out_shape=[jax.ShapeDtypeStruct((rows, w * count), F32) for w in widths],
+        compiler_params=pltpu.CompilerParams(vmem_limit_bytes=32 * 2**20),
+        cost_estimate=cost(2),
+        name="collect",
+    )(at, *blocks)
+
+
+def tie_kernel(*refs):
+    del refs
+
+
+def tie(value, *earlier):
+    anywhere = pl.BlockSpec(memory_space=pl.ANY)
+    return pl.pallas_call(
+        tie_kernel,
+        in_specs=[anywhere] * (1 + len(earlier)),
+        out_specs=anywhere,
+        out_shape=jax.ShapeDtypeStruct(value.shape, value.dtype),
+        input_output_aliases={0: 0},
+        cost_estimate=cost(0.3),
+        name="tie",
+    )(value, *earlier)
+
+
+def divide_kernel(count, at, *refs):
+    parts, outs, rows = refs[:-count], refs[-count:], refs[-1].shape[0]
+    for d, out in enumerate(outs):
+        begin = 0
+        for part in parts:
+            width = part.shape[1]
+            out[:, begin : begin + width] = part[pl.ds(pl.multiple_of((at[0] ^ d) * rows, rows), rows), :]
+            begin += width
+
+
+def divide(at, parts, count):
+    rows, width = parts[0].shape[0] // count, sum(p.shape[1] for p in parts)
+    return pl.pallas_call(
+        functools.partial(divide_kernel, count),
+        in_specs=[pl.BlockSpec(memory_space=pltpu.SMEM)] + in_vmem(len(parts)),
+        out_specs=in_vmem(count),
+        out_shape=[jax.ShapeDtypeStruct((rows, width), BF16)] * count,
+        compiler_params=pltpu.CompilerParams(vmem_limit_bytes=32 * 2**20),
+        cost_estimate=cost(3),
+        name="divide",
+    )(at, *parts)
 
 
 def dense(a, b):
@@ -449,6 +647,14 @@
 
 def dense_bt(a, b):
     return lax.dot_general(a, b, (((1,), (1,)), ((), ())), preferred_element_type=F32)
+
+
+def flip(axis, distance, size):
+    return lambda a: lax.ppermute(a, axis, [(i, i ^ distance) for i in range(size)])
+
+
+def after(value, *earlier):
+    return lax.optimization_barrier((value, *earlier))[0]
 
 
 def local(
@@ -467,42 +673,140 @@
     group = token_order.shape[1]
     mine = group // (n_ctx * n_tp)
 
-    def cut(w):
-        return w.reshape(rows_d, n_ctx, w.shape[1] // n_ctx)
-
-    def spread(*parts):
-        block = jnp.swapaxes(jnp.concatenate(parts, axis=2), 0, 1)
-        block = lax.all_to_all(block, "ctx", split_axis=0, concat_axis=0, tiled=True)
-        return lax.all_gather(block.reshape(n_ctx * rows_d, -1), "fsdp", axis=0, tiled=True)
-
-    def own(partial):
-        block = lax.psum_scatter(partial.astype(BF16), "fsdp", scatter_dimension=0, tiled=True)
-        block = block.reshape(n_ctx, rows_d, -1)
-        block = lax.all_to_all(block, "ctx", split_axis=0, concat_axis=0, tiled=True)
-        return jnp.swapaxes(block, 0, 1).astype(F32)
-
-    def join(block, begin, end):
-        return block[:, :, begin:end].reshape(rows_d, -1)
-
-    gains = jnp.stack([norm_mixer, norm_ffn], axis=1)[:, None, :]
-    gains = jnp.broadcast_to(gains, (rows_d, n_ctx, 2))
-    blank = jnp.zeros((rows_d, n_ctx, LANES - 2 * heads - 2), BF16)
-    w_first = spread(cut(w_query), cut(w_key), cut(w_value), cut(w_decay), cut(w_beta), gains, blank)
-    w_second = spread(cut(w_outgate), cut(w_output.T))
-    w_hidden = spread(cut(w_gate), cut(w_up))
-    w_last = spread(cut(w_down.T))
+    across_core, across_x = flip("ctx", 1, n_ctx), flip("ctx", 2, n_ctx)
+    across_both, across_y = flip("ctx", 3, n_ctx), flip("tp", 1, n_tp)
+    half = mine // 2
+    at_x, at_core = at_ctx // 2, at_ctx % 2
+
+    def place_of(token):
+        part, rest = token // half, token % half
+        second, other_y = part % 2, (part // 2 % 2) ^ at_tp
+        other_core, other_x = (part // 4 % 2) ^ at_core, (part // 8) ^ at_x
+        pair = jnp.where(second == 1, other_y * 2 + other_x, other_x * 2 + other_y)
+        return ((other_core * 2 + second) * 4 + pair) * half + rest
+
+    def beside(*transfers):
+        return lax.optimization_barrier(transfers)
+
+    def place_given(token):
+        part = (at_ctx ^ (token // (2 * mine)))
+        return ((part % 2) * 2 + part // 2) * (2 * mine) + token % (2 * mine)
+
+    def gather_tokens(block):
+        first, second = block[:half], block[half:]
+        first_y, second_x = beside(across_y(first), across_x(second))
+        first = jnp.concatenate([first, first_y], axis=0)
+        second = jnp.concatenate([second, second_x], axis=0)
+        first_x, second_y = beside(across_x(first), across_y(second))
+        chip = (first, first_x, second, second_y)
+        return jnp.concatenate([*chip, *(across_core(piece) for piece in chip)], axis=0)
+
+    def sort_given(near, far):
+        def pick(block, second, other):
+            return lax.dynamic_slice_in_dim(block, (at_tp ^ other) * mine + second * half, half, 0)
+
+        def chip(near, far):
+            return [
+                *(pick(b, 0, other) for b in (near, far) for other in (0, 1)),
+                *(pick(b, 1, other) for other in (0, 1) for b in (near, far)),
+            ]
+
+        return jnp.concatenate(chip(near, far) + chip(across_core(near), across_core(far)), axis=0)
+
+    def product(*pairs):
+        size = pairs[0][0].shape[0] // 4
+        return [
+            sum(dense_bt(rows[i * size : (i + 1) * size], matrix) for rows, matrix in pairs).astype(BF16)
+            for i in (2, 3, 0, 1)
+        ]
+
+    def sum_cores(theirs_first, theirs_second, first, second):
+        theirs_first, theirs_second = across_core(theirs_first), across_core(theirs_second)
+        near, far = slice(0, 2 * half), slice(2 * half, 4 * half)
+        return (
+            both(first[near], theirs_first[near]), both(second[near], theirs_second[near]),
+            both(first[far], theirs_first[far]).astype(BF16), both(second[far], theirs_second[far]).astype(BF16),
+        )
+
+    def sum_near(first, second, far_first, far_second):
+        moved_first, moved_second = beside(across_x(far_first), across_y(far_second))
+        first, second = both(first, moved_first), both(second, moved_second)
+        return first[:half], second[:half], first[half:].astype(BF16), second[half:].astype(BF16)
+
+    def sum_far(first, second, moved_first, moved_second):
+        moved_first, moved_second = beside(across_y(moved_first), across_x(moved_second))
+        return jnp.concatenate([both(first, moved_first), both(second, moved_second)], axis=0)
+
+    def sum_tokens(*parts):
+        return sum_far(*sum_near(*sum_cores(*parts)))
+
+    def both(a, b):
+        return a.astype(F32) + b.astype(F32)
+
+    def pair_tokens(block):
+        other = across_y(block)
+        whole = jnp.concatenate([block, other], axis=0)
+        swapped = jnp.concatenate([other, block], axis=0)
+        return jnp.where(at_tp == 0, whole, swapped)
+
+    at_here = jnp.reshape(at_ctx, (1,)).astype(jnp.int32)
+
+    def exchange(blocks):
+        return [blocks[0], across_core(blocks[1]), across_x(blocks[2]), across_both(blocks[3])]
+
+    def spread(place, *parts):
+        blocks = exchange(deal(place, parts, n_ctx))
+        return stack(at_here, blocks, (blocks[0].shape[1],))[0]
+
+    def every(block):
+        return lax.all_gather(block, "fsdp", axis=0, tiled=True)
+
+    def reduce(partial):
+        return lax.psum_scatter(partial, "fsdp", scatter_dimension=0, tiled=True)
+
+    def own(place, blocks, *widths):
+        return collect(at_here, exchange(divide(place, blocks, n_ctx)), widths)
+
+    def vectors(block):
+        n_groups, count, distance = lax.axis_size("fsdp"), block.shape[0], 1
+        places = []
+        for move, place in ((across_core, at_core), (across_x, at_x)):
+            block, places = jnp.stack([block, move(block)]), [place, *places]
+        while distance < n_groups:
+            block = jnp.stack([block, flip("fsdp", distance, n_groups)(block)])
+            places = [lax.axis_index("fsdp") // distance % 2, *places]
+            distance *= 2
+        moved = block
+        for axis, place in enumerate(places):
+            block = jnp.where(place == 0, block, jnp.flip(block, axis))
+        return jnp.moveaxis(block.reshape(-1, count, block.shape[-1]), 1, 0).reshape(count, -1), moved
+
+    first_in = spread(at_here, w_query, w_key, w_value)
+    w_first = every(first_in)
+    thin, thin_moved = vectors(jnp.concatenate([norm_mixer[None], norm_ffn[None], w_decay.T, w_beta.T], axis=0))
+    n_mix, n_ffn = thin[0].astype(F32), thin[1].astype(F32)
+    w_thin = jnp.concatenate([
+        lax.dynamic_slice_in_dim(thin, 2 + at_ctx * heads, heads, 0),
+        lax.dynamic_slice_in_dim(thin, 2 + (n_ctx + at_ctx) * heads, heads, 0),
+    ])
+    w_thin = jnp.pad(w_thin, ((0, LANES - 2 * heads), (0, 0)))
+    source_in = lax.dynamic_slice_in_dim(residual, at_tp * mine, mine, 0)
+    near = tie(residual, first_in, thin_moved)
+    far = across_x(near)
+    tokens = (near, far, across_core(near), across_core(far))
+    order = place_of(token_order[0])
+    inverse = jnp.zeros_like(order).at[order].set(lax.iota(jnp.int32, group))
+    second_in = spread(tie(at_here, far, thin, inverse), w_outgate, w_output.T)
+    w_second = every(second_in)
     w_gates, w_out = w_second[:, :hv], w_second[:, hv:]
-    n_mix = w_first[:, wide + 2 * heads].astype(F32)
-    n_ffn = w_first[:, wide + 2 * heads + 1].astype(F32)
-
-    order = token_order[0]
-    inverse = jnp.zeros_like(order).at[order].set(lax.iota(jnp.int32, group))
-    tokens = lax.all_gather(residual, "ctx", axis=0, tiled=True)
-    packed = tokens[order].astype(F32)
-    scale = lax.rsqrt(jnp.mean(packed * packed, axis=-1, keepdims=True) + EPS)
-    normed1 = (packed * scale * n_mix).astype(BF16)
+    normed1, raw_thin = packed_rows(place_given(token_order[0])[:, None], n_mix[None], w_thin, tokens)
+    cot_in = lax.dynamic_slice_in_dim(cotangent, at_tp * mine, mine, 0)
     raw = dense(normed1, w_first).astype(BF16)
-    gate = dense(normed1, w_gates).astype(BF16)
+    cot_far = across_x(tie(cotangent, raw))
+    cot = sort_given(cotangent, cot_far)
+    later = tie(at_here, raw)
+    last_in, gate_in, up_in = spread(later, w_down.T), spread(later, w_gate), spread(later, w_up)
+    w_last, w_gating, w_uppart = every(last_in), every(gate_in), every(up_in)
 
     first_head = (at_tp * n_ctx + at_ctx) * heads
 
@@ -518,77 +822,105 @@
     rates = jnp.pad(rates, ((0, 6), (0, LANES - heads)))
     gain = norm_head.astype(F32)[None, :]
     sizes = (heads, key, val)
-    u, qe, wm, kd, fresh, p, solve, decay, gram, cols = prepare(raw, taps, rates, lengths, *sizes)
-    headout, mixed, new, enter = forward(qe, wm, kd, fresh, p, cols, gate, gain, *sizes)
-
-    both = ("ctx", "tp")
-    given = headout[inverse]
-    attention = lax.psum_scatter(
-        dense_bt(given, w_out).astype(BF16), both, scatter_dimension=0, tiled=True
-    ).astype(F32)
-    source = lax.dynamic_slice_in_dim(residual, at_tp * mine, mine, 0).astype(F32)
+    u, qe, wm, kd, fresh, p, solve, decay, gram, cols = prepare(
+        raw, raw_thin, taps, rates, lengths, *sizes, wait=(second_in,)
+    )
+    headout, mixed, new, gate, enter = forward(
+        qe, wm, kd, fresh, p, cols, normed1, w_second, gain, *sizes, wait=(last_in, gate_in)
+    )
+
+    given = headout[tie(inverse, cot_far, up_in)]
+    attention = sum_tokens(*product((given, w_out)))
+    source = source_in.astype(F32)
     middle = source + attention
     scale2 = lax.rsqrt(jnp.mean(middle * middle, axis=-1, keepdims=True) + EPS)
+    grad_act = dense(cot, w_last)
     normed2 = (middle * scale2 * n_ffn).astype(BF16)
-    normed2 = lax.all_gather(normed2, both, axis=0, tiled=True)
-    hidden = dense(normed2, w_hidden)
-    gating, up_part = hidden[:, :units], hidden[:, units:]
-    sig = jax.nn.sigmoid(gating)
-    silu = gating * sig
-    activation = (silu * up_part).astype(BF16)
-
-    cot = lax.all_gather(cotangent, "ctx", axis=0, tiled=True)
-    grad_act = dense(cot, w_last)
-    grad_gating = (grad_act * up_part * (sig + silu * (1.0 - sig))).astype(BF16)
-    grad_up = (grad_act * silu).astype(BF16)
-    grad_hidden = jnp.concatenate([grad_gating, grad_up], axis=1)
-    grad_normed2 = lax.psum_scatter(
-        dense_bt(grad_hidden, w_hidden).astype(BF16), both, scatter_dimension=0, tiled=True
-    ).astype(F32)
+    normed2 = gather_tokens(tie(normed2, grad_act, w_gating))
+    w_hidden = jnp.concatenate([w_gating, w_uppart], axis=1)
+    activation, grad_hidden = hidden_units(normed2, w_gating, w_uppart, grad_act)
+    g_last = dense_t(cot, activation).astype(BF16)
+    grad_hidden = tie(grad_hidden, g_last)
+    g_last = reduce(g_last)
+    grad_parts = product((grad_hidden, w_hidden))
+    grad_normed2 = sum_tokens(*grad_parts)
+    g_hidden = dense_t(tie(normed2, *grad_parts), grad_hidden).astype(BF16)
 
     def norm_back(u_in, s, n, g):
         weighted = n * g
         return s * weighted - u_in * (s * s * s) * jnp.mean(u_in * weighted, axis=-1, keepdims=True)
 
-    cot_mine = lax.dynamic_slice_in_dim(cotangent, at_tp * mine, mine, 0).astype(F32)
-    grad_mid = cot_mine + norm_back(middle, scale2, n_ffn, grad_normed2)
-    grad_attn = lax.all_gather(grad_mid.astype(BF16), both, axis=0, tiled=True)
+    grad_mid = cot_in.astype(F32) + norm_back(middle, scale2, n_ffn, grad_normed2)
+    ffn_parts = product((activation, w_last))
+    w_all = jnp.concatenate([w_first, w_gates, w_thin.T], axis=1)
+    grad_attn = gather_tokens(tie(grad_mid.astype(BF16), *ffn_parts, g_hidden, g_last, w_all))
+    g_hidden = reduce(g_hidden)
     grad_given = dense(grad_attn, w_out).astype(BF16)
 
-    ffn_out = lax.psum_scatter(
-        dense_bt(activation, w_last).astype(BF16), both, scatter_dimension=0, tiled=True
-    ).astype(F32)
-    output = lax.all_gather((middle + ffn_out).astype(BF16), "tp", axis=0, tiled=True)
-
+    ffn_send = sum_cores(tie(ffn_parts[0], grad_attn), tie(ffn_parts[1], grad_attn), *ffn_parts[2:])
+    ffn_near = sum_near(*ffn_send)
     grad_gate, g_gain, do, dn, leave = backward(
-        grad_given[order], mixed, gate, gain, p, qe, wm, kd, cols, *sizes
+        grad_given[tie(order, ffn_send[2], ffn_send[3])], mixed, gate, gain, p, qe, wm, kd, cols, *sizes
     )
-    dx, g_taps, g_small = finish(
-        raw, taps, rates, lengths, u, p, solve, decay, gram, cols, new, do, dn, enter, leave, *sizes
+    g_out = reduce(dense_t(grad_attn, tie(given, grad_gate)).astype(BF16))
+    g_gates = dense_t(normed1, grad_gate).astype(BF16)
+    ffn_out = sum_far(*ffn_near)
+    dx, dx_thin, dx_all, g_taps, g_small = finish(
+        raw, taps, rates, lengths, u, p, solve, decay, gram, cols, new, do, dn, grad_gate, enter, leave, *sizes,
+        wait=(g_gates, *ffn_near[2:], g_hidden),
     )
-    grad_packed = jnp.concatenate([dx, grad_gate], axis=1)
-    w_all = jnp.concatenate([w_first, w_gates], axis=1)
-    grad_normed1 = lax.psum_scatter(
-        dense_bt(grad_packed[inverse], w_all).astype(BF16), both, scatter_dimension=0, tiled=True
-    ).astype(F32)
+    g_gates = reduce(g_gates)
+    output = pair_tokens((middle + ffn_out).astype(BF16))
+    g_first = dense_t(normed1, tie(dx, ffn_out)).astype(BF16)
+    inverse = tie(inverse, g_first, g_out)
+    g_first = reduce(g_first)
+    grad_parts = product((tie(dx_all[inverse], output), w_all))
+    later = tie(at_here, grad_parts[3])
+    g_taps = tie(g_taps, grad_parts[3])
+    grad_normed1 = sum_tokens(*grad_parts)
     scale1 = lax.rsqrt(jnp.mean(source * source, axis=-1, keepdims=True) + EPS)
     grad_input = (grad_mid + norm_back(source, scale1, n_mix, grad_normed1)).astype(BF16)
-    grad_input = lax.all_gather(grad_input, "tp", axis=0, tiled=True)
-
-    g_hidden = own(dense_t(normed2, grad_hidden))
-    g_last = own(dense_t(cot, activation))
-    g_out = own(dense_t(grad_attn, given))
-    g_gates = own(dense_t(normed1, grad_gate))
-    g_first = own(dense_t(normed1, dx))
-
-    gw_gate, gw_up = join(g_hidden, 0, units), join(g_hidden, units, 2 * units)
-    gw_down = join(g_last, 0, units).T
-    gw_output = join(g_out, 0, hv).T
-    gw_outgate = join(g_gates, 0, hv)
-    gw_query, gw_key = join(g_first, 0, hk), join(g_first, hk, 2 * hk)
-    gw_value = join(g_first, 2 * hk, wide)
-    gw_decay = join(g_first, wide, wide + heads)
-    gw_beta = join(g_first, wide + heads, wide + 2 * heads)
+    grad_input = pair_tokens(grad_input)
+
+    gw_gate, gw_up, gw_down = own(later, (g_hidden, g_last), units, units, units)
+    gw_query, gw_key, gw_value, gw_output, gw_outgate = own(
+        tie(at_here, grad_normed1), (g_first, g_out, g_gates), hk, hk, hv, hv, hv
+    )
+    gw_output, gw_down = gw_output.T, gw_down.T
+
+    def pad(vector):
+        return jnp.pad(vector, (0, -vector.size % LANES)).reshape(-1, LANES)
+
+    g_thin = dense_t(dx_thin, normed1)[: 2 * heads].reshape(-1, LANES)
+    sums = jnp.concatenate([g_taps[:TAPS].reshape(-1, LANES), pad(g_gain[0]), g_small[:2], g_thin], axis=0)
+    n_groups, distance = lax.axis_size("fsdp"), 1
+    while distance < n_groups:
+        sums = sums + flip("fsdp", distance, n_groups)(sums)
+        distance *= 2
+    for move in (across_y, across_x, across_core):
+        sums = jnp.stack([sums, move(sums)])
+    sums = sums.reshape(2, 2, 2, *sums.shape[3:])
+    sums = jnp.where(at_core == 0, sums, sums[::-1])
+    sums = jnp.where(at_x == 0, sums, sums[:, ::-1])
+    sums = jnp.where(at_tp == 0, sums, sums[:, :, ::-1])
+    sums = sums.transpose(2, 1, 0, 3, 4).reshape(n_tp * n_ctx, *sums.shape[3:])
+    of_taps = TAPS * wide // LANES
+    of_thin = g_thin.shape[0]
+    tap_sums = sums[:, :of_taps].reshape(-1, TAPS, wide).swapaxes(0, 1)
+
+    def heads_of(begin, end):
+        return tap_sums[:, :, begin:end].reshape(TAPS, -1)
+
+    pieces = (
+        heads_of(0, hk), heads_of(hk, 2 * hk), heads_of(2 * hk, wide),
+        sums[:, -2 - of_thin, :heads].reshape(-1), sums[:, -1 - of_thin, :heads].reshape(-1),
+        jnp.sum(sums[:, of_taps : -2 - of_thin], axis=0).reshape(-1)[:val],
+    )
+    thin_sums = sums[:, -of_thin:].reshape(n_tp, n_ctx, 2, heads, n_ctx * lax.axis_size("fsdp"), rows_d)
+    thin_sums = lax.dynamic_index_in_dim(thin_sums, at_tp, 0, keepdims=False)
+    thin_sums = lax.dynamic_index_in_dim(thin_sums, lax.axis_index("fsdp") * n_ctx + at_ctx, 3, keepdims=False)
+    gw_decay = thin_sums[:, 0].reshape(-1, rows_d).T
+    gw_beta = thin_sums[:, 1].reshape(-1, rows_d).T
 
     def overlap(*pairs):
         return sum(jnp.sum(w.astype(F32) * g, axis=1) for w, g in pairs)
@@ -598,26 +930,8 @@
                 (w_decay, gw_decay), (w_beta, gw_beta)) / norm_mixer.astype(F32),
         overlap((w_gate, gw_gate), (w_up, gw_up)) / norm_ffn.astype(F32),
     ])
-    g_norms = lax.psum(g_norms, "tp")
-
-    def place(like, part, width):
-        return lax.dynamic_update_slice_in_dim(jnp.zeros(like, F32), part, first_head * width, len(like) - 1)
-
-    sums = lax.psum(
-        jnp.concatenate([
-            place(conv_query.shape, g_taps[:TAPS, :hk], key).reshape(-1),
-            place(conv_key.shape, g_taps[:TAPS, hk : 2 * hk], key).reshape(-1),
-            place(conv_value.shape, g_taps[:TAPS, 2 * hk :], val).reshape(-1),
-            place(decay_log.shape, g_small[0, :heads], 1),
-            place(decay_bias.shape, g_small[1, :heads], 1),
-            g_gain[0],
-        ]),
-        ("fsdp", "ctx", "tp"),
-    )
-    pieces, at = [], 0
-    for like in (conv_query, conv_key, conv_value, decay_log, decay_bias, norm_head):
-        pieces.append(sums[at : at + like.size].reshape(like.shape))
-        at += like.size
+    g_norms = g_norms + across_y(g_norms)
+
     return (
         output, grad_input, g_norms[0], gw_query, gw_key, gw_value, gw_outgate, gw_decay, gw_beta,
         *pieces, gw_output, g_norms[1], gw_gate, gw_up, gw_down,

time: 1570 us -> 958 us (0.61)
  waiting for transfers between devices: 980 us -> 224 us
  Pallas kernels: 141 us -> 234 us
  blocking collectives: 59.4 us -> 0 us
  starting transfers between devices: 22.9 us -> 73.5 us
  other arithmetic: 42 us -> 78.7 us
  local copies, waits for them, and re-layouts: 113 us -> 144 us
    all_gather x10 -> x5, waiting for transfers between devices: 434 us -> 0.01 us  [every(): return lax.all_gather(block, 'fsdp', axis=0, tiled=True)]
    reduce_scatter x9 -> x5, waiting for transfers between devices: 367 us -> 0.04 us  [reduce(): return lax.psum_scatter(partial, 'fsdp', scatter_dimension=0, tiled=True)]
    ppermute x0 -> x79, waiting for transfers between devices: none -> 223 us  [flip(): lax.ppermute(a, axis, [(i, i ^ distance) for i in range(size)])]
    psum x1 -> x0, waiting for transfers between devices: 122 us -> none  [local(): lax.psum(jnp.concatenate([place(conv_query.shape, g_taps[:TAPS, :hk], key...]
    pallas_call x4 -> x39, Pallas kernels: 141 us -> 234 us  [the longest x1 62.3 us: prepare(): pl.pallas_call(functools.partial(prepare_kernel, heads, key, val, len(wai...]
    ppermute x0 -> x79, starting transfers between devices: none -> 72.1 us  [flip(): lax.ppermute(a, axis, [(i, i ^ distance) for i in range(size)])]
    all_to_all x3 -> x0, blocking collectives: 54.4 us -> none  [spread(): lax.all_to_all(block, 'ctx', split_axis=0, concat_axis=0, tiled=True)]
    all_to_all x6 -> x0, waiting for transfers between devices: 54.2 us -> none  [the longest x5 51.3 us: own(): lax.all_to_all(block, 'ctx', split_axis=0, concat_axis=0, tiled=True)]
  transfers between devices with their start and end apart: 26 -> 89, of which waited for: 21 -> 36; matrix products, arithmetic and copies ran while one was open for 17% -> 39% of each run, Pallas kernels for 8% -> 22%
where the time goes in v2:
time: 958 us; the launch traced here: 949 us
  Pallas kernels  234 us (24%)
  waiting for transfers between devices  224 us (23%)
  matrix products  179 us (19%)
  local copies, waits for them, and re-layouts  144 us (15%)
  other arithmetic  78.7 us (8%)
  starting transfers between devices  73.5 us (8%)
  between operations  15.8 us (2%)
    ppermute x79, waiting for transfers between devices, flip(): lax.ppermute(a, axis, [(i, i ^ distance) for i in range(size)])  223 us
    dot_general x16, matrix products, dense_bt(): lax.dot_general(a, b, (((1,), (1,)), ((), ())), preferred_element_type=F32)  74.8 us
    ppermute x79, starting transfers between devices, flip(): lax.ppermute(a, axis, [(i, i ^ distance) for i in range(size)])  72.1 us
    unnamed x248, local copies, waits for them, and re-layouts  70.3 us
    dot_general x6, matrix products, dense_t(): lax.dot_general(a, b, (((0,), (0,)), ((), ())), preferred_element_type=F32)  69.1 us
    pallas_call x1, Pallas kernels, prepare(): pl.pallas_call(functools.partial(prepare_kernel, heads, key, val, len(wai...  62.3 us
    pallas_call x1, Pallas kernels, finish(): pl.pallas_call(functools.partial(finish_kernel, heads, key, val, len(wait...  45.9 us
    dot_general x3, matrix products, dense(): return jnp.dot(a, b, preferred_element_type=F32)  35 us
  transfers between devices with their start and end apart: 89, of which 36 were waited for; matrix products, arithmetic and copies ran while one was open for 39% of the time, Pallas kernels for 22%

profile of v2, /device:TPU:0, one launch (start us, length us, event | category | flops | bytes accessed | tf_op | source)
XLA Modules:
  0.0 948.8 jit_solution(16462141720234917249)
XLA Ops:
  12.7 7.2 collective-permute-done.5.refs_2_
  19.9 5.2 collective-permute-done.6.refs_3_
  43.3 5.2 collective-permute-start.7
  51.1 6.5 fusion.23
  57.6 8.6 scatter_custom_fusion.refs_3_.refs_0_
  66.3 21.3 %collective-permute-done.7.refs_1_ = bf16[512,2048]{1,0:T(8,128)(2,1)} collective-permute-done((bf16[512,2048]{1,0:T(8,128)(2,1)}, bf16[512,2048]{1,0:T(8,128)(2,1)}, u32[]{:S(2)}, u32[]{:S(2)}) %collective-permute-start.7) | collective-permute-done | bytes 2097184 | tf_op jit(solution)/shard_map/ppermute | solution.py:653
  89.0 3.1 deal.6
  95.2 6.7 collective-permute-done.11.refs_2_
  101.9 3.8 collective-permute-done.12.refs_3_
  111.1 31.5 %packed_rows.1 = (bf16[2048,2048]{1,0:T(8,128)(2,1)}, bf16[2048,128]{1,0:T(8,128)(2,1)}) custom-call(s32[2048,1]{1,0:T(8,128)} %get-tuple-element.274.order_ref, f32[1,2048]{1,0:T(1,128)} %bitcast.146, bf16[128,2048]{1,0:T(8,128)(2,1)} %pad.9.clone.thin_ref, bf16[512,2048]{1,0:T(8,128)(2,1)} %tie.19.refs_0_, ...), custom_call_target="tpu_custom_call" | custom-call | flops 29899999232 | bytes 26000000 | tf_op jit(solution)/shard_map/packed_rows/pallas_call | solution.py:479
  142.6 13.8 %convolution_convert_fusion.1.raw_ref.before_ref.refs_1_ = bf16[2048,1024]{1,0:T(8,128)(2,1)} fusion(bf16[2048,2048]{1,0:T(8,128)(2,1)} %get-tuple-element.113.normed_ref, bf16[2048,1024]{1,0:T(8,128)(2,1)} %all-gather.6.cloned.1.call-done), kind=kOutput, calls=%fused_computation.7 | convolution fusion | flops 8592031744 | bytes 16777216 | tf_op jit(solution)/shard_map/dot_general | solution.py:641
  156.9 3.0 deal.7
  162.5 6.5 collective-permute-done.14.refs_2_
  174.2 3.0 deal.8
  179.8 6.5 collective-permute-done.17.refs_2_
  199.8 3.0 deal.9
  205.8 62.3 %prepare.1 = (f32[2048,1024]{1,0:T(8,128)}, bf16[2048,256]{1,0:T(8,128)(2,1)}, bf16[2048,256]{1,0:T(8,128)(2,1)}, bf16[2048,256]{1,0:T(8,128)(2,1)}, f32[2048,51...) custom-call(s32[1,4]{1,0:T(1,128)} %lengths.3, ...), custom_call_target="tpu_custom_call" | custom-call | flops 115000000 | bytes 100000 | tf_op jit(solution)/shard_map/prepare/pallas_call | solution.py:361
  279.1 22.2 %forward.1 = (bf16[2048,512]{1,0:T(8,128)(2,1)}, f32[2048,512]{1,0:T(8,128)}, bf16[2048,512]{1,0:T(8,128)(2,1)}, bf16[2048,512]{1,0:T(8,128)(2,1)}, bf16[16,2,128,256]{3,2,1,0:T(8,128)(2,1)}) custom-call(bf16[2048,256]{1,0:T(8,128)(2,1)} %get-tuple-element.119.qe_ref, bf16[2048,256]{1,0:T(8,128)(2,1)} %get-tuple-element.120.w_ref, ...), custom_call_target="tpu_custom_call" | custom-call | flops 115000000 | bytes 100000 | tf_op jit(solution)/shard_map/forward/pallas_call | solution.py:387
  301.2 11.1 %gather_fusion = bf16[2048,512]{1,0:T(8,128)(2,1)} fusion(bf16[2048,512]{1,0:T(8,128)(2,1)} %get-tuple-element.133, s32[2048]{0:T(1024)S(1)} %fusion.70), kind=kCustom, calls=%fused_computation | custom fusion | bytes 4202496 | tf_op jit(solution)/shard_map/gather | solution.py:832
  312.3 3.2 convolution_convert_fusion.15
  341.3 13.0 %collective-permute-done.26 = bf16[256,2048]{1,0:T(8,128)(2,1)S(1)} collective-permute-done((bf16[256,2048]{1,0:T(8,128)(2,1)S(1)}, bf16[256,2048]{1,0:T(8,128)(2,1)S(1)}, u32[]{:S(2)}, u32[]{:S(2)}) %collective-permute-start.26) | collective-permute-done | bytes 1048608 | tf_op jit(solution)/shard_map/ppermute | solution.py:653
  359.9 12.2 %fusion.99.refs_1_.grad_ref = f32[2048,704]{1,0:T(8,128)} fusion(bf16[2048,2048]{1,0:T(8,128)(2,1)} %dynamic-slice_dynamic-update-slice_fusion, bf16[2048,704]{1,0:T(8,128)(2,1)} %all-gather.10.cloned.1.call-done), kind=kOutput, calls=%fused_computation.335 | convolution fusion | flops 5905580032 | bytes 17039360 | tf_op jit(solution)/shard_map/dot_general | solution.py:641
  380.7 9.3 collective-permute-done.31
  396.7 17.0 %collective-permute-done.34 = bf16[256,2048]{1,0:T(8,128)(2,1)S(1)} collective-permute-done((bf16[256,2048]{1,0:T(8,128)(2,1)S(1)}, bf16[256,2048]{1,0:T(8,128)(2,1)S(1)}, u32[]{:S(2)}, u32[]{:S(2)}) %collective-permute-start.34) | collective-permute-done | bytes 1048608 | tf_op jit(solution)/shard_map/ppermute | solution.py:653
  423.0 19.8 %hidden_units.1 = (bf16[2048,704]{1,0:T(8,128)(2,1)}, bf16[2048,1408]{1,0:T(8,128)(2,1)}) custom-call(bf16[2048,2048]{1,0:T(8,128)(2,1)} %constant_dynamic-update-slice_fusion.rows_ref.refs_0_, bf16[2048,704]{1,0:T(8,128)(2,1)} %all-gather.12.cloned.1.call-done.refs_2_.gate_ref, bf16[2048,704]{1,0:T(8,128)(2,1)} %all-gather.14.cloned.1.call-done.up_ref, ...), custom_call_target="tpu_custom_call" | custom-call | flops 115000000 | bytes 100000 | tf_op jit(solution)/shard_map/hidden_units/pallas_call | solution.py:509
  442.8 11.4 %convolution_convert_fusion.3.refs_1_ = bf16[2048,704]{1,0:T(8,128)(2,1)} fusion(bf16[2048,2048]{1,0:T(8,128)(2,1)} %dynamic-slice_dynamic-update-slice_fusion, bf16[2048,704]{1,0:T(8,128)(2,1)} %get-tuple-element.146), kind=kOutput, calls=%fused_computation.13 | convolution fusion | flops 5907021824 | bytes 14155776 | tf_op jit(solution)/shard_map/dot_general | solution.py:645
  454.3 8.2 convolution_convert_fusion.19.refs_2_
  462.6 5.1 convolution_convert_fusion.21.refs_1_
  468.1 3.2 pad_maximum_fusion.refs_7_
  471.3 4.9 convolution_convert_fusion.20.refs_4_
  476.1 4.8 convolution_convert_fusion.22.refs_3_
  481.0 3.1 add_convert_fusion.5
  489.9 19.1 %convolution_convert_fusion.refs_5_ = bf16[2048,1408]{1,0:T(8,128)(2,1)} fusion(bf16[2048,2048]{1,0:T(8,128)(2,1)} %tie.26, bf16[2048,1408]{1,0:T(8,128)(2,1)} %tie.25), kind=kOutput, calls=%fused_computation.4 | convolution fusion | flops 11814043648 | bytes 19922944 | tf_op jit(solution)/shard_map/dot_general | solution.py:645
  509.5 5.5 convolution_convert_fusion.11.refs_4_
  514.9 3.2 convolution_convert_fusion.12.refs_2_.refs_0_
  523.3 3.2 convolution_convert_fusion.14.refs_3_
  526.4 3.2 convolution_convert_fusion.13.refs_1_.refs_0_
  529.7 4.1 collective-permute-done.43
  544.1 10.4 %collective-permute-done.45 = bf16[128,2048]{1,0:T(8,128)(2,1)S(1)} collective-permute-done((bf16[128,2048]{1,0:T(8,128)(2,1)S(1)}, bf16[128,2048]{1,0:T(8,128)(2,1)S(1)}, u32[]{:S(2)}, u32[]{:S(2)}) %collective-permute-start.45) | collective-permute-done | bytes 524320 | tf_op jit(solution)/shard_map/ppermute | solution.py:653
  558.4 19.8 %collective-permute-done.48 = bf16[256,2048]{1,0:T(8,128)(2,1)S(1)} collective-permute-done((bf16[256,2048]{1,0:T(8,128)(2,1)S(1)}, bf16[256,2048]{1,0:T(8,128)(2,1)S(1)}, u32[]{:S(2)}, u32[]{:S(2)}) %collective-permute-start.48) | collective-permute-done | bytes 1048608 | tf_op jit(solution)/shard_map/ppermute | solution.py:653
  588.8 9.0 convolution_convert_fusion.10
  597.8 2.8 add_convert_fusion.3.refs_2_
  604.0 9.2 gather_fusion.1
  613.2 16.7 %backward.1 = (bf16[2048,512]{1,0:T(8,128)(2,1)}, f32[1,256]{1,0:T(1,128)}, bf16[2048,512]{1,0:T(8,128)(2,1)}, bf16[2048,512]{1,0:T(8,128)(2,1)}, bf16[16,2,128,256]{3,2,1,0:T(8,128)(2,1)}) custom-call(bf16[2048,512]{1,0:T(8,128)(2,1)} %gather_fusion.1, f32[2048,512]{1,0:T(8,128)} %get-tuple-element.165.mixed_ref, ...), custom_call_target="tpu_custom_call" | custom-call | flops 115000000 | bytes 100000 | tf_op jit(solution)/shard_map/backward/pallas_call | solution.py:412
  629.9 10.0 %convolution_convert_fusion.8 = bf16[2048,512]{1,0:T(8,128)(2,1)} fusion(bf16[2048,2048]{1,0:T(8,128)(2,1)} %constant_dynamic-update-slice_fusion.10.refs_1_, bf16[2048,512]{1,0:T(8,128)(2,1)} %tie.32), kind=kOutput, calls=%fused_computation.19 | convolution fusion | flops 4296015872 | bytes 12582912 | tf_op jit(solution)/shard_map/dot_general | solution.py:645
  641.8 9.4 convolution_convert_fusion.9.refs_0_
  651.6 13.6 %collective-permute-done.56 = bf16[256,2048]{1,0:T(8,128)(2,1)} collective-permute-done((bf16[256,2048]{1,0:T(8,128)(2,1)S(1)}, bf16[256,2048]{1,0:T(8,128)(2,1)}, u32[]{:S(2)}, u32[]{:S(2)}) %collective-permute-start.56) | collective-permute-done | bytes 1048608 | tf_op jit(solution)/shard_map/ppermute | solution.py:653
  675.2 45.9 %finish.1 = (bf16[2048,1024]{1,0:T(8,128)(2,1)}, bf16[2048,128]{1,0:T(8,128)(2,1)}, bf16[2048,1664]{1,0:T(8,128)(2,1)}, f32[8,1024]{1,0:T(8,128)}, f32[8,128]{1,0:T(8,128)}) custom-call(s32[1,4]{1,0:T(1,128)} %lengths.3, bf16[2048,1024]{1,0:T(8,128)(2,1)} %convolution_convert_fusion.1.raw_ref.before_ref.refs_1_, ...), custom_call_target="tpu_custom_call" | custom-call | flops 115000000 | bytes 100000 | tf_op jit(solution)/shard_map/finish/pallas_call | solution.py:441
  721.1 4.8 fusion.54
  732.5 14.4 %convolution_convert_fusion.2.refs_1_ = bf16[2048,1024]{1,0:T(8,128)(2,1)} fusion(bf16[2048,2048]{1,0:T(8,128)(2,1)} %get-tuple-element.113.normed_ref, bf16[2048,1024]{1,0:T(8,128)(2,1)} %tie.31), kind=kOutput, calls=%fused_computation.8 | convolution fusion | flops 8592031744 | bytes 16777216 | tf_op jit(solution)/shard_map/dot_general | solution.py:645
  746.9 7.9 collective-permute-done.59
  757.9 17.7 %gather_fusion.2 = bf16[2048,1664]{1,0:T(8,128)(2,1)} fusion(bf16[2048,1664]{1,0:T(8,128)(2,1)} %get-tuple-element.172, s32[2048]{0:T(1024)S(1)} %fusion.72), kind=kCustom, calls=%fused_computation.2 | custom fusion | bytes 13639680 | tf_op jit(solution)/shard_map/gather | solution.py:877
  777.3 7.4 convolution_convert_fusion.5.refs_1_
  785.4 5.0 collective-permute-start.70
  792.6 4.0 collective-permute-start.71
  796.6 8.0 convolution_convert_fusion.4
  806.0 6.8 convolution_convert_fusion.6
  823.7 7.5 convolution_convert_fusion.7
  845.0 17.9 %collective-permute-done.63 = bf16[256,2048]{1,0:T(8,128)(2,1)} collective-permute-done((bf16[256,2048]{1,0:T(8,128)(2,1)}, bf16[256,2048]{1,0:T(8,128)(2,1)}, u32[]{:S(2)}, u32[]{:S(2)}) %collective-permute-start.63) | collective-permute-done | bytes 1048608 | tf_op jit(solution)/shard_map/ppermute | solution.py:653
  862.9 7.3 collective-permute-done.61
  888.0 3.2 collective-permute-done.65
  910.4 7.5 collective-permute-done.68.refs_2_
  918.0 10.6 %collective-permute-done.69.refs_3_ = bf16[128,2048]{1,0:T(8,128)(2,1)} collective-permute-done((bf16[128,2048]{1,0:T(8,128)(2,1)S(1)}, bf16[128,2048]{1,0:T(8,128)(2,1)}, u32[]{:S(2)}, u32[]{:S(2)}) %collective-permute-start.69) | collective-permute-done | bytes 524320 | tf_op jit(solution)/shard_map/ppermute | solution.py:653
  928.5 3.2 collect.2
  (567 shorter events, 269.2 us)
Async XLA Ops:
  7.2 135.4 %all-gather.6.cloned.1.call-start = ((), (), s32[]{:S(2)}) async-start(), calls=%async_computation.5 | async-start | bytes 5242880 | tf_op jit(solution)/shard_map/all_gather | solution.py:762
  12.5 12.6 %collective-permute-start.6 = (bf16[128,1024]{1,0:T(8,128)(2,1)}, bf16[128,1024]{1,0:T(8,128)(2,1)S(1)}, u32[]{:S(2)}, u32[]{:S(2)}) collective-permute-start(bf16[128,1024]{1,0:T(8,128)(2,1)} %get-tuple-element.112), channel_id=1, source_target_pairs={{0,6},{2,4},{4,2},{6,0},{1,7},{3,5},{5,3},{7,1},{8,14},{10,12},{12... | collective-permute-start | bytes 786440 | tf_op jit(solution)/shard_map/ppermute | solution.py:653
  28.3 250.8 %all-gather.8.cloned.1.call-start = ((), (), s32[]{:S(2)}) async-start(), calls=%async_computation.6 | async-start | bytes 5242880 | tf_op jit(solution)/shard_map/all_gather | solution.py:762
  43.3 44.3 %collective-permute-start.7 = (bf16[512,2048]{1,0:T(8,128)(2,1)}, bf16[512,2048]{1,0:T(8,128)(2,1)}, u32[]{:S(2)}, u32[]{:S(2)}) collective-permute-start(bf16[512,2048]{1,0:T(8,128)(2,1)} %tie.19.refs_0_), channel_id=1, source_target_pairs={{0,4},{2,6},{4,0},{6,2},{1,5},{3,7},{5,1},{7,3},{8,12},{10,14},{12... | collective-permute-start | bytes 6291464 | tf_op jit(solution)/shard_map/ppermute | solution.py:653
  66.2 44.8 %collective-permute-start.8 = (bf16[512,2048]{1,0:T(8,128)(2,1)S(1)}, bf16[512,2048]{1,0:T(8,128)(2,1)}, u32[]{:S(2)}, u32[]{:S(2)}) collective-permute-start(bf16[512,2048]{1,0:T(8,128)(2,1)S(1)} %copy-done.34), channel_id=1, source_target_pairs={{0,2},{2,0},{4,6},{6,4},{1,3},{3,1},{5,7},{7,5},{8,10},{10,8},{12,... | collective-permute-start | bytes 6291464 | tf_op jit(solution)/shard_map/ppermute | solution.py:653
  87.6 23.4 %collective-permute-start.9 = (bf16[512,2048]{1,0:T(8,128)(2,1)}, bf16[512,2048]{1,0:T(8,128)(2,1)}, u32[]{:S(2)}, u32[]{:S(2)}) collective-permute-start(bf16[512,2048]{1,0:T(8,128)(2,1)} %collective-permute-done.7.refs_1_), channel_id=1, source_target_pairs={{0,2},{2,0},{4,6},{6,4},{1,3},{3,1},{5,7},{7,5},{8,10},{10,8},{12,... | collective-permute-start | bytes 6291464 | tf_op jit(solution)/shard_map/ppermute | solution.py:653
  94.0 11.7 %collective-permute-start.12 = (bf16[128,1024]{1,0:T(8,128)(2,1)}, bf16[128,1024]{1,0:T(8,128)(2,1)}, u32[]{:S(2)}, u32[]{:S(2)}) collective-permute-start(bf16[128,1024]{1,0:T(8,128)(2,1)} %get-tuple-element.118), channel_id=1, source_target_pairs={{0,6},{2,4},{4,2},{6,0},{1,7},{3,5},{5,3},{7,1},{8,14},{10,12},{12... | collective-permute-start | bytes 786440 | tf_op jit(solution)/shard_map/ppermute | solution.py:653
  108.0 251.9 %all-gather.10.cloned.1.call-start = ((), (), s32[]{:S(2)}) async-start(), calls=%async_computation.7 | async-start | bytes 3932160 | tf_op jit(solution)/shard_map/all_gather | solution.py:762
  174.2 201.4 %all-gather.12.cloned.1.call-start = ((), (), s32[]{:S(2)}) async-start(), calls=%async_computation.8 | async-start | bytes 3932160 | tf_op jit(solution)/shard_map/all_gather | solution.py:762
  191.7 231.3 %all-gather.14.cloned.1.call-start = ((), (), s32[]{:S(2)}) async-start(), calls=%async_computation.9 | async-start | bytes 3932160 | tf_op jit(solution)/shard_map/all_gather | solution.py:762
  193.1 78.4 %collective-permute-start.19 = (bf16[512,2048]{1,0:T(8,128)(2,1)}, bf16[512,2048]{1,0:T(8,128)(2,1)}, u32[]{:S(2)}, u32[]{:S(2)}) collective-permute-start(bf16[512,2048]{1,0:T(8,128)(2,1)} %tie.22), channel_id=1, source_target_pairs={{0,4},{2,6},{4,0},{6,2},{1,5},{3,7},{5,1},{7,3},{8,12},{10,14},{12... | collective-permute-start | bytes 6291464 | tf_op jit(solution)/shard_map/ppermute | solution.py:653
  194.5 125.7 %collective-permute-start.29 = (bf16[512,2048]{1,0:T(8,128)(2,1)S(1)}, bf16[512,2048]{1,0:T(8,128)(2,1)}, u32[]{:S(2)}, u32[]{:S(2)}) collective-permute-start(bf16[512,2048]{1,0:T(8,128)(2,1)S(1)} %copy-done.16), channel_id=1, source_target_pairs={{0,2},{2,0},{4,6},{6,4},{1,3},{3,1},{5,7},{7,5},{8,10},{10,8},{12,... | collective-permute-start | bytes 6291464 | tf_op jit(solution)/shard_map/ppermute | solution.py:653
  202.8 65.4 %collective-permute-start.20 = (bf16[128,704]{1,0:T(8,128)(2,1)}, bf16[128,704]{1,0:T(8,128)(2,1)S(1)}, u32[]{:S(2)}, u32[]{:S(2)}) collective-permute-start(bf16[128,704]{1,0:T(8,128)(2,1)} %get-tuple-element.135), channel_id=1, source_target_pairs={{0,2},{2,0},{4,6},{6,4},{1,3},{3,1},{5,7},{7,5},{8,10},{10,8},{12,... | collective-permute-start | bytes 540680 | tf_op jit(solution)/shard_map/ppermute | solution.py:653
  202.8 65.4 %collective-permute-start.21 = (bf16[128,704]{1,0:T(8,128)(2,1)}, bf16[128,704]{1,0:T(8,128)(2,1)S(1)}, u32[]{:S(2)}, u32[]{:S(2)}) collective-permute-start(bf16[128,704]{1,0:T(8,128)(2,1)} %get-tuple-element.136), channel_id=1, source_target_pairs={{0,4},{2,6},{4,0},{6,2},{1,5},{3,7},{5,1},{7,3},{8,12},{10,14},{12... | collective-permute-start | bytes 540680 | tf_op jit(solution)/shard_map/ppermute | solution.py:653
  203.6 64.5 %collective-permute-start.22 = (bf16[128,704]{1,0:T(8,128)(2,1)}, bf16[128,704]{1,0:T(8,128)(2,1)S(1)}, u32[]{:S(2)}, u32[]{:S(2)}) collective-permute-start(bf16[128,704]{1,0:T(8,128)(2,1)} %get-tuple-element.137), channel_id=1, source_target_pairs={{0,6},{2,4},{4,2},{6,0},{1,7},{3,5},{5,3},{7,1},{8,14},{10,12},{12... | collective-permute-start | bytes 540680 | tf_op jit(solution)/shard_map/ppermute | solution.py:653
  271.2 269.0 %reduce-scatter.6.cloned.1.call-start = ((), (), s32[]{:S(2)}) async-start(), calls=%async_computation.10 | async-start | bytes 3932160 | tf_op jit(solution)/shard_map/reduce_scatter | solution.py:765
  271.4 55.1 %collective-permute-start.30 = (bf16[512,2048]{1,0:T(8,128)(2,1)}, bf16[512,2048]{1,0:T(8,128)(2,1)}, u32[]{:S(2)}, u32[]{:S(2)}) collective-permute-start(bf16[512,2048]{1,0:T(8,128)(2,1)} %collective-permute-done.19.refs_1_), channel_id=1, source_target_pairs={{0,2},{2,0},{4,6},{6,4},{1,3},{3,1},{5,7},{7,5},{8,10},{10,8},{12,... | collective-permute-start | bytes 6291464 | tf_op jit(solution)/shard_map/ppermute | solution.py:653
  315.5 13.0 %collective-permute-start.25 = (bf16[512,2048]{1,0:T(8,128)(2,1)S(1)}, bf16[512,2048]{1,0:T(8,128)(2,1)S(1)}, u32[]{:S(2)}, u32[]{:S(2)}) collective-permute-start(bf16[512,2048]{1,0:T(8,128)(2,1)S(1)} %convolution_convert_fusion.15), channel_id=1, source_target_pairs={{0,2},{2,0},{4,6},{6,4},{1,3},{3,1},{5,7},{7,5},{8,10},{10,8},{12,... | collective-permute-start | bytes 6291464 | tf_op jit(solution)/shard_map/ppermute | solution.py:653
  317.9 12.5 %collective-permute-start.23 = (bf16[512,2048]{1,0:T(8,128)(2,1)S(1)}, bf16[512,2048]{1,0:T(8,128)(2,1)S(1)}, u32[]{:S(2)}, u32[]{:S(2)}) collective-permute-start(bf16[512,2048]{1,0:T(8,128)(2,1)S(1)} %convolution_convert_fusion.17), channel_id=1, source_target_pairs={{0,2},{2,0},{4,6},{6,4},{1,3},{3,1},{5,7},{7,5},{8,10},{10,8},{12,... | collective-permute-start | bytes 6291464 | tf_op jit(solution)/shard_map/ppermute | solution.py:653
  328.9 25.3 %collective-permute-start.26 = (bf16[256,2048]{1,0:T(8,128)(2,1)S(1)}, bf16[256,2048]{1,0:T(8,128)(2,1)S(1)}, u32[]{:S(2)}, u32[]{:S(2)}) collective-permute-start(bf16[256,2048]{1,0:T(8,128)(2,1)S(1)} %add_convert_fusion.7), channel_id=1, source_target_pairs={{0,1},{1,0},{2,3},{3,2},{4,5},{5,4},{6,7},{7,6},{8,9},{9,8},{10,11... | collective-permute-start | bytes 3145736 | tf_op jit(solution)/shard_map/ppermute | solution.py:653
  330.9 25.1 %collective-permute-start.24 = (bf16[256,2048]{1,0:T(8,128)(2,1)S(1)}, bf16[256,2048]{1,0:T(8,128)(2,1)S(1)}, u32[]{:S(2)}, u32[]{:S(2)}) collective-permute-start(bf16[256,2048]{1,0:T(8,128)(2,1)S(1)} %add_convert_fusion.8), channel_id=1, source_target_pairs={{0,4},{2,6},{4,0},{6,2},{1,5},{3,7},{5,1},{7,3},{8,12},{10,14},{12... | collective-permute-start | bytes 3145736 | tf_op jit(solution)/shard_map/ppermute | solution.py:653
  357.4 14.7 %collective-permute-start.27 = (bf16[128,2048]{1,0:T(8,128)(2,1)}, bf16[128,2048]{1,0:T(8,128)(2,1)S(1)}, u32[]{:S(2)}, u32[]{:S(2)}) collective-permute-start(bf16[128,2048]{1,0:T(8,128)(2,1)} %slice.560), channel_id=1, source_target_pairs={{0,1},{1,0},{2,3},{3,2},{4,5},{5,4},{6,7},{7,6},{8,9},{9,8},{10,11... | collective-permute-start | bytes 1572872 | tf_op jit(solution)/shard_map/ppermute | solution.py:653
  359.2 13.0 %collective-permute-start.28 = (bf16[128,2048]{1,0:T(8,128)(2,1)}, bf16[128,2048]{1,0:T(8,128)(2,1)}, u32[]{:S(2)}, u32[]{:S(2)}) collective-permute-start(bf16[128,2048]{1,0:T(8,128)(2,1)} %slice.559), channel_id=1, source_target_pairs={{0,4},{2,6},{4,0},{6,2},{1,5},{3,7},{5,1},{7,3},{8,12},{10,14},{12... | collective-permute-start | bytes 1572872 | tf_op jit(solution)/shard_map/ppermute | solution.py:653
  377.8 12.3 %collective-permute-start.31 = (bf16[128,2048]{1,0:T(8,128)(2,1)S(1)}, bf16[128,2048]{1,0:T(8,128)(2,1)S(1)}, u32[]{:S(2)}, u32[]{:S(2)}) collective-permute-start(bf16[128,2048]{1,0:T(8,128)(2,1)S(1)} %get-tuple-element.273), channel_id=1, source_target_pairs={{0,1},{1,0},{2,3},{3,2},{4,5},{5,4},{6,7},{7,6},{8,9},{9,8},{10,11... | collective-permute-start | bytes 1572872 | tf_op jit(solution)/shard_map/ppermute | solution.py:653
  379.4 11.9 %collective-permute-start.32 = (bf16[128,2048]{1,0:T(8,128)(2,1)S(1)}, bf16[128,2048]{1,0:T(8,128)(2,1)S(1)}, u32[]{:S(2)}, u32[]{:S(2)}) collective-permute-start(bf16[128,2048]{1,0:T(8,128)(2,1)S(1)} %get-tuple-element.271), channel_id=1, source_target_pairs={{0,4},{2,6},{4,0},{6,2},{1,5},{3,7},{5,1},{7,3},{8,12},{10,14},{12... | collective-permute-start | bytes 1572872 | tf_op jit(solution)/shard_map/ppermute | solution.py:653
  391.4 22.3 %collective-permute-start.34 = (bf16[256,2048]{1,0:T(8,128)(2,1)S(1)}, bf16[256,2048]{1,0:T(8,128)(2,1)S(1)}, u32[]{:S(2)}, u32[]{:S(2)}) collective-permute-start(bf16[256,2048]{1,0:T(8,128)(2,1)S(1)} %pad_maximum_fusion.5), channel_id=1, source_target_pairs={{0,1},{1,0},{2,3},{3,2},{4,5},{5,4},{6,7},{7,6},{8,9},{9,8},{10,11... | collective-permute-start | bytes 3145736 | tf_op jit(solution)/shard_map/ppermute | solution.py:653
  392.1 22.3 %collective-permute-start.33 = (bf16[256,2048]{1,0:T(8,128)(2,1)S(1)}, bf16[256,2048]{1,0:T(8,128)(2,1)S(1)}, u32[]{:S(2)}, u32[]{:S(2)}) collective-permute-start(bf16[256,2048]{1,0:T(8,128)(2,1)S(1)} %pad_maximum_fusion.4), channel_id=1, source_target_pairs={{0,4},{2,6},{4,0},{6,2},{1,5},{3,7},{5,1},{7,3},{8,12},{10,14},{12... | collective-permute-start | bytes 3145736 | tf_op jit(solution)/shard_map/ppermute | solution.py:653
  395.4 23.3 %collective-permute-start.35 = (bf16[256,2048]{1,0:T(8,128)(2,1)S(1)}, bf16[256,2048]{1,0:T(8,128)(2,1)S(1)}, u32[]{:S(2)}, u32[]{:S(2)}) collective-permute-start(bf16[256,2048]{1,0:T(8,128)(2,1)S(1)} %pad_maximum_fusion.4), channel_id=1, source_target_pairs={{0,2},{2,0},{4,6},{6,4},{1,3},{3,1},{5,7},{7,5},{8,10},{10,8},{12,... | collective-permute-start | bytes 3145736 | tf_op jit(solution)/shard_map/ppermute | solution.py:653
  395.4 25.5 %collective-permute-start.37 = (bf16[256,2048]{1,0:T(8,128)(2,1)S(1)}, bf16[256,2048]{1,0:T(8,128)(2,1)S(1)}, u32[]{:S(2)}, u32[]{:S(2)}) collective-permute-start(bf16[256,2048]{1,0:T(8,128)(2,1)S(1)} %pad_maximum_fusion.5), channel_id=1, source_target_pairs={{0,2},{2,0},{4,6},{6,4},{1,3},{3,1},{5,7},{7,5},{8,10},{10,8},{12,... | collective-permute-start | bytes 3145736 | tf_op jit(solution)/shard_map/ppermute | solution.py:653
  454.2 221.0 %reduce-scatter.8.cloned.1.call-start = ((), (), s32[]{:S(2)}) async-start(), calls=%async_computation.11 | async-start | bytes 7208960 | tf_op jit(solution)/shard_map/reduce_scatter | solution.py:765
  462.5 18.5 %collective-permute-start.41 = (bf16[512,2048]{1,0:T(8,128)(2,1)}, bf16[512,2048]{1,0:T(8,128)(2,1)}, u32[]{:S(2)}, u32[]{:S(2)}) collective-permute-start(bf16[512,2048]{1,0:T(8,128)(2,1)} %convolution_convert_fusion.19.refs_2_), channel_id=1, source_target_pairs={{0,2},{2,0},{4,6},{6,4},{1,3},{3,1},{5,7},{7,5},{8,10},{10,8},{12,... | collective-permute-start | bytes 6291464 | tf_op jit(solution)/shard_map/ppermute | solution.py:653
  467.6 17.9 %collective-permute-start.39 = (bf16[512,2048]{1,0:T(8,128)(2,1)}, bf16[512,2048]{1,0:T(8,128)(2,1)}, u32[]{:S(2)}, u32[]{:S(2)}) collective-permute-start(bf16[512,2048]{1,0:T(8,128)(2,1)} %convolution_convert_fusion.21.refs_1_), channel_id=1, source_target_pairs={{0,2},{2,0},{4,6},{6,4},{1,3},{3,1},{5,7},{7,5},{8,10},{10,8},{12,... | collective-permute-start | bytes 6291464 | tf_op jit(solution)/shard_map/ppermute | solution.py:653
  484.1 34.1 %collective-permute-start.42 = (bf16[256,2048]{1,0:T(8,128)(2,1)}, bf16[256,2048]{1,0:T(8,128)(2,1)S(1)}, u32[]{:S(2)}, u32[]{:S(2)}) collective-permute-start(bf16[256,2048]{1,0:T(8,128)(2,1)} %add_convert_fusion.5), channel_id=1, source_target_pairs={{0,1},{1,0},{2,3},{3,2},{4,5},{5,4},{6,7},{7,6},{8,9},{9,8},{10,11... | collective-permute-start | bytes 3145736 | tf_op jit(solution)/shard_map/ppermute | solution.py:653
  488.2 30.0 %collective-permute-start.40 = (bf16[256,2048]{1,0:T(8,128)(2,1)}, bf16[256,2048]{1,0:T(8,128)(2,1)}, u32[]{:S(2)}, u32[]{:S(2)}) collective-permute-start(bf16[256,2048]{1,0:T(8,128)(2,1)} %add_convert_fusion.6), channel_id=1, source_target_pairs={{0,4},{2,6},{4,0},{6,2},{1,5},{3,7},{5,1},{7,3},{8,12},{10,14},{12... | collective-permute-start | bytes 3145736 | tf_op jit(solution)/shard_map/ppermute | solution.py:653
  509.0 248.2 %reduce-scatter.10.cloned.1.call-start = ((), (), s32[]{:S(2)}) async-start(), calls=%async_computation.12 | async-start | bytes 2621440 | tf_op jit(solution)/shard_map/reduce_scatter | solution.py:765
  520.5 13.4 %collective-permute-start.43 = (bf16[128,2048]{1,0:T(8,128)(2,1)S(1)}, bf16[128,2048]{1,0:T(8,128)(2,1)S(1)}, u32[]{:S(2)}, u32[]{:S(2)}) collective-permute-start(bf16[128,2048]{1,0:T(8,128)(2,1)S(1)} %slice.558), channel_id=1, source_target_pairs={{0,1},{1,0},{2,3},{3,2},{4,5},{5,4},{6,7},{7,6},{8,9},{9,8},{10,11... | collective-permute-start | bytes 1572872 | tf_op jit(solution)/shard_map/ppermute | solution.py:653
  522.8 13.1 %collective-permute-start.44 = (bf16[128,2048]{1,0:T(8,128)(2,1)S(1)}, bf16[128,2048]{1,0:T(8,128)(2,1)S(1)}, u32[]{:S(2)}, u32[]{:S(2)}) collective-permute-start(bf16[128,2048]{1,0:T(8,128)(2,1)S(1)} %slice.557), channel_id=1, source_target_pairs={{0,4},{2,6},{4,0},{6,2},{1,5},{3,7},{5,1},{7,3},{8,12},{10,14},{12... | collective-permute-start | bytes 1572872 | tf_op jit(solution)/shard_map/ppermute | solution.py:653
  542.3 12.2 %collective-permute-start.45 = (bf16[128,2048]{1,0:T(8,128)(2,1)S(1)}, bf16[128,2048]{1,0:T(8,128)(2,1)S(1)}, u32[]{:S(2)}, u32[]{:S(2)}) collective-permute-start(bf16[128,2048]{1,0:T(8,128)(2,1)S(1)} %get-tuple-element.270), channel_id=1, source_target_pairs={{0,1},{1,0},{2,3},{3,2},{4,5},{5,4},{6,7},{7,6},{8,9},{9,8},{10,11... | collective-permute-start | bytes 1572872 | tf_op jit(solution)/shard_map/ppermute | solution.py:653
  543.8 11.9 %collective-permute-start.46 = (bf16[128,2048]{1,0:T(8,128)(2,1)S(1)}, bf16[128,2048]{1,0:T(8,128)(2,1)S(1)}, u32[]{:S(2)}, u32[]{:S(2)}) collective-permute-start(bf16[128,2048]{1,0:T(8,128)(2,1)S(1)} %get-tuple-element.268), channel_id=1, source_target_pairs={{0,4},{2,6},{4,0},{6,2},{1,5},{3,7},{5,1},{7,3},{8,12},{10,14},{12... | collective-permute-start | bytes 1572872 | tf_op jit(solution)/shard_map/ppermute | solution.py:653
  555.8 22.4 %collective-permute-start.48 = (bf16[256,2048]{1,0:T(8,128)(2,1)S(1)}, bf16[256,2048]{1,0:T(8,128)(2,1)S(1)}, u32[]{:S(2)}, u32[]{:S(2)}) collective-permute-start(bf16[256,2048]{1,0:T(8,128)(2,1)S(1)} %pad_maximum_fusion.7), channel_id=1, source_target_pairs={{0,1},{1,0},{2,3},{3,2},{4,5},{5,4},{6,7},{7,6},{8,9},{9,8},{10,11... | collective-permute-start | bytes 3145736 | tf_op jit(solution)/shard_map/ppermute | solution.py:653
  556.5 22.1 %collective-permute-start.47 = (bf16[256,2048]{1,0:T(8,128)(2,1)S(1)}, bf16[256,2048]{1,0:T(8,128)(2,1)S(1)}, u32[]{:S(2)}, u32[]{:S(2)}) collective-permute-start(bf16[256,2048]{1,0:T(8,128)(2,1)S(1)} %pad_maximum_fusion.6), channel_id=1, source_target_pairs={{0,4},{2,6},{4,0},{6,2},{1,5},{3,7},{5,1},{7,3},{8,12},{10,14},{12... | collective-permute-start | bytes 3145736 | tf_op jit(solution)/shard_map/ppermute | solution.py:653
  557.1 26.0 %collective-permute-start.49 = (bf16[256,2048]{1,0:T(8,128)(2,1)S(1)}, bf16[256,2048]{1,0:T(8,128)(2,1)S(1)}, u32[]{:S(2)}, u32[]{:S(2)}) collective-permute-start(bf16[256,2048]{1,0:T(8,128)(2,1)S(1)} %pad_maximum_fusion.6), channel_id=1, source_target_pairs={{0,2},{2,0},{4,6},{6,4},{1,3},{3,1},{5,7},{7,5},{8,10},{10,8},{12,... | collective-permute-start | bytes 3145736 | tf_op jit(solution)/shard_map/ppermute | solution.py:653
  557.1 28.2 %collective-permute-start.51 = (bf16[256,2048]{1,0:T(8,128)(2,1)S(1)}, bf16[256,2048]{1,0:T(8,128)(2,1)S(1)}, u32[]{:S(2)}, u32[]{:S(2)}) collective-permute-start(bf16[256,2048]{1,0:T(8,128)(2,1)S(1)} %pad_maximum_fusion.7), channel_id=1, source_target_pairs={{0,2},{2,0},{4,6},{6,4},{1,3},{3,1},{5,7},{7,5},{8,10},{10,8},{12,... | collective-permute-start | bytes 3145736 | tf_op jit(solution)/shard_map/ppermute | solution.py:653
  587.4 13.1 %collective-permute-start.53 = (bf16[512,2048]{1,0:T(8,128)(2,1)}, bf16[512,2048]{1,0:T(8,128)(2,1)S(1)}, u32[]{:S(2)}, u32[]{:S(2)}) collective-permute-start(bf16[512,2048]{1,0:T(8,128)(2,1)} %tie.28), channel_id=1, source_target_pairs={{0,2},{2,0},{4,6},{6,4},{1,3},{3,1},{5,7},{7,5},{8,10},{10,8},{12,... | collective-permute-start | bytes 6291464 | tf_op jit(solution)/shard_map/ppermute | solution.py:653
  639.9 258.0 %reduce-scatter.14.cloned.1.call-start = ((), (), s32[]{:S(2)}) async-start(), calls=%async_computation.14 | async-start | bytes 2621440 | tf_op jit(solution)/shard_map/reduce_scatter | solution.py:765
  640.0 25.2 %collective-permute-start.56 = (bf16[256,2048]{1,0:T(8,128)(2,1)S(1)}, bf16[256,2048]{1,0:T(8,128)(2,1)}, u32[]{:S(2)}, u32[]{:S(2)}) collective-permute-start(bf16[256,2048]{1,0:T(8,128)(2,1)S(1)} %copy-done.47), channel_id=1, source_target_pairs={{0,1},{1,0},{2,3},{3,2},{4,5},{5,4},{6,7},{7,6},{8,9},{9,8},{10,11... | collective-permute-start | bytes 3145736 | tf_op jit(solution)/shard_map/ppermute | solution.py:653
  641.5 25.1 %collective-permute-start.54 = (bf16[256,2048]{1,0:T(8,128)(2,1)}, bf16[256,2048]{1,0:T(8,128)(2,1)}, u32[]{:S(2)}, u32[]{:S(2)}) collective-permute-start(bf16[256,2048]{1,0:T(8,128)(2,1)} %add_convert_fusion.4.refs_1_), channel_id=1, source_target_pairs={{0,4},{2,6},{4,0},{6,2},{1,5},{3,7},{5,1},{7,3},{8,12},{10,14},{12... | collective-permute-start | bytes 3145736 | tf_op jit(solution)/shard_map/ppermute | solution.py:653
  651.3 246.7 %reduce-scatter.12.cloned.1.call-start = ((), (), s32[]{:S(2)}) async-start(), calls=%async_computation.13 | async-start | bytes 5242880 | tf_op jit(solution)/shard_map/reduce_scatter | solution.py:765
  674.1 52.7 %collective-permute-start.57 = (bf16[128,2048]{1,0:T(8,128)(2,1)S(1)}, bf16[128,2048]{1,0:T(8,128)(2,1)}, u32[]{:S(2)}, u32[]{:S(2)}) collective-permute-start(bf16[128,2048]{1,0:T(8,128)(2,1)S(1)} %slice.556.refs_1_), channel_id=1, source_target_pairs={{0,1},{1,0},{2,3},{3,2},{4,5},{5,4},{6,7},{7,6},{8,9},{9,8},{10,11... | collective-permute-start | bytes 1572872 | tf_op jit(solution)/shard_map/ppermute | solution.py:653
  674.7 52.0 %collective-permute-start.58 = (bf16[128,2048]{1,0:T(8,128)(2,1)S(1)}, bf16[128,2048]{1,0:T(8,128)(2,1)}, u32[]{:S(2)}, u32[]{:S(2)}) collective-permute-start(bf16[128,2048]{1,0:T(8,128)(2,1)S(1)} %slice.555.refs_2_), channel_id=1, source_target_pairs={{0,4},{2,6},{4,0},{6,2},{1,5},{3,7},{5,1},{7,3},{8,12},{10,14},{12... | collective-permute-start | bytes 1572872 | tf_op jit(solution)/shard_map/ppermute | solution.py:653
  731.2 23.7 %collective-permute-start.59 = (bf16[256,2048]{1,0:T(8,128)(2,1)S(1)}, bf16[256,2048]{1,0:T(8,128)(2,1)S(1)}, u32[]{:S(2)}, u32[]{:S(2)}) collective-permute-start(bf16[256,2048]{1,0:T(8,128)(2,1)S(1)} %get-tuple-element.267), channel_id=1, source_target_pairs={{0,1},{1,0},{2,3},{3,2},{4,5},{5,4},{6,7},{7,6},{8,9},{9,8},{10,11... | collective-permute-start | bytes 3145736 | tf_op jit(solution)/shard_map/ppermute | solution.py:653
  792.6 12.1 %collective-permute-start.71 = (f32[100,128]{1,0:T(8,128)S(1)}, f32[100,128]{1,0:T(8,128)S(1)}, u32[]{:S(2)}, u32[]{:S(2)}) collective-permute-start(f32[100,128]{1,0:T(8,128)S(1)} %fusion.92), channel_id=1, source_target_pairs={{0,16},{8,24},{16,0},{24,8},{1,17},{9,25},{17,1},{25,9},{2,18},{10... | collective-permute-start | bytes 153608 | tf_op jit(solution)/shard_map/ppermute | solution.py:653
  804.7 29.9 %collective-permute-start.62 = (bf16[512,2048]{1,0:T(8,128)(2,1)}, bf16[512,2048]{1,0:T(8,128)(2,1)}, u32[]{:S(2)}, u32[]{:S(2)}) collective-permute-start(bf16[512,2048]{1,0:T(8,128)(2,1)} %convolution_convert_fusion.4), channel_id=1, source_target_pairs={{0,2},{2,0},{4,6},{6,4},{1,3},{3,1},{5,7},{7,5},{8,10},{10,8},{12,... | collective-permute-start | bytes 6291464 | tf_op jit(solution)/shard_map/ppermute | solution.py:653
  812.7 25.0 %collective-permute-start.60 = (bf16[512,2048]{1,0:T(8,128)(2,1)}, bf16[512,2048]{1,0:T(8,128)(2,1)}, u32[]{:S(2)}, u32[]{:S(2)}) collective-permute-start(bf16[512,2048]{1,0:T(8,128)(2,1)} %convolution_convert_fusion.6), channel_id=1, source_target_pairs={{0,2},{2,0},{4,6},{6,4},{1,3},{3,1},{5,7},{7,5},{8,10},{10,8},{12,... | collective-permute-start | bytes 6291464 | tf_op jit(solution)/shard_map/ppermute | solution.py:653
  820.1 59.6 %collective-permute-start.75 = (bf16[128,2112]{0,1:T(8,128)(2,1)}, bf16[128,2112]{0,1:T(8,128)(2,1)}, u32[]{:S(2)}, u32[]{:S(2)}) collective-permute-start(bf16[128,2112]{0,1:T(8,128)(2,1)} %copy.104), channel_id=1, source_target_pairs={{0,2},{2,0},{4,6},{6,4},{1,3},{3,1},{5,7},{7,5},{8,10},{10,8},{12,... | collective-permute-start | bytes 1622024 | tf_op jit(solution)/shard_map/ppermute | solution.py:653
  821.1 59.9 %collective-permute-start.76 = (bf16[128,2112]{0,1:T(8,128)(2,1)}, bf16[128,2112]{0,1:T(8,128)(2,1)S(1)}, u32[]{:S(2)}, u32[]{:S(2)}) collective-permute-start(bf16[128,2112]{0,1:T(8,128)(2,1)} %copy.105), channel_id=1, source_target_pairs={{0,4},{2,6},{4,0},{6,2},{1,5},{3,7},{5,1},{7,3},{8,12},{10,14},{12... | collective-permute-start | bytes 1622024 | tf_op jit(solution)/shard_map/ppermute | solution.py:653
  832.3 49.1 %collective-permute-start.77 = (bf16[128,2112]{0,1:T(8,128)(2,1)}, bf16[128,2112]{0,1:T(8,128)(2,1)}, u32[]{:S(2)}, u32[]{:S(2)}) collective-permute-start(bf16[128,2112]{0,1:T(8,128)(2,1)} %copy.106), channel_id=1, source_target_pairs={{0,6},{2,4},{4,2},{6,0},{1,7},{3,5},{5,3},{7,1},{8,14},{10,12},{12... | collective-permute-start | bytes 1622024 | tf_op jit(solution)/shard_map/ppermute | solution.py:653
  837.3 25.6 %collective-permute-start.63 = (bf16[256,2048]{1,0:T(8,128)(2,1)}, bf16[256,2048]{1,0:T(8,128)(2,1)}, u32[]{:S(2)}, u32[]{:S(2)}) collective-permute-start(bf16[256,2048]{1,0:T(8,128)(2,1)} %add_convert_fusion), channel_id=1, source_target_pairs={{0,1},{1,0},{2,3},{3,2},{4,5},{5,4},{6,7},{7,6},{8,9},{9,8},{10,11... | collective-permute-start | bytes 3145736 | tf_op jit(solution)/shard_map/ppermute | solution.py:653
  840.3 29.9 %collective-permute-start.61 = (bf16[256,2048]{1,0:T(8,128)(2,1)}, bf16[256,2048]{1,0:T(8,128)(2,1)}, u32[]{:S(2)}, u32[]{:S(2)}) collective-permute-start(bf16[256,2048]{1,0:T(8,128)(2,1)} %add_convert_fusion.1), channel_id=1, source_target_pairs={{0,4},{2,6},{4,0},{6,2},{1,5},{3,7},{5,1},{7,3},{8,12},{10,14},{12... | collective-permute-start | bytes 3145736 | tf_op jit(solution)/shard_map/ppermute | solution.py:653
  874.1 13.9 %collective-permute-start.64 = (bf16[128,2048]{1,0:T(8,128)(2,1)}, bf16[128,2048]{1,0:T(8,128)(2,1)}, u32[]{:S(2)}, u32[]{:S(2)}) collective-permute-start(bf16[128,2048]{1,0:T(8,128)(2,1)} %slice.554), channel_id=1, source_target_pairs={{0,1},{1,0},{2,3},{3,2},{4,5},{5,4},{6,7},{7,6},{8,9},{9,8},{10,11... | collective-permute-start | bytes 1572872 | tf_op jit(solution)/shard_map/ppermute | solution.py:653
  877.5 13.7 %collective-permute-start.65 = (bf16[128,2048]{1,0:T(8,128)(2,1)}, bf16[128,2048]{1,0:T(8,128)(2,1)}, u32[]{:S(2)}, u32[]{:S(2)}) collective-permute-start(bf16[128,2048]{1,0:T(8,128)(2,1)} %slice.553), channel_id=1, source_target_pairs={{0,4},{2,6},{4,0},{6,2},{1,5},{3,7},{5,1},{7,3},{8,12},{10,14},{12... | collective-permute-start | bytes 1572872 | tf_op jit(solution)/shard_map/ppermute | solution.py:653
  903.2 14.7 %collective-permute-start.68 = (bf16[128,2048]{1,0:T(8,128)(2,1)S(1)}, bf16[128,2048]{1,0:T(8,128)(2,1)S(1)}, u32[]{:S(2)}, u32[]{:S(2)}) collective-permute-start(bf16[128,2048]{1,0:T(8,128)(2,1)S(1)} %get-tuple-element.180), channel_id=1, source_target_pairs={{0,4},{2,6},{4,0},{6,2},{1,5},{3,7},{5,1},{7,3},{8,12},{10,14},{12... | collective-permute-start | bytes 1572872 | tf_op jit(solution)/shard_map/ppermute | solution.py:653
  904.4 24.2 %collective-permute-start.69 = (bf16[128,2048]{1,0:T(8,128)(2,1)S(1)}, bf16[128,2048]{1,0:T(8,128)(2,1)}, u32[]{:S(2)}, u32[]{:S(2)}) collective-permute-start(bf16[128,2048]{1,0:T(8,128)(2,1)S(1)} %get-tuple-element.181), channel_id=1, source_target_pairs={{0,6},{2,4},{4,2},{6,0},{1,7},{3,5},{5,3},{7,1},{8,14},{10,12},{12... | collective-permute-start | bytes 1572872 | tf_op jit(solution)/shard_map/ppermute | solution.py:653
  908.8 28.8 %collective-permute-start.66 = (bf16[256,2048]{1,0:T(8,128)(2,1)S(1)}, bf16[256,2048]{1,0:T(8,128)(2,1)S(1)}, u32[]{:S(2)}, u32[]{:S(2)}) collective-permute-start(bf16[256,2048]{1,0:T(8,128)(2,1)S(1)} %copy-done.46), channel_id=1, source_target_pairs={{0,1},{1,0},{2,3},{3,2},{4,5},{5,4},{6,7},{7,6},{8,9},{9,8},{10,11... | collective-permute-start | bytes 3145736 | tf_op jit(solution)/shard_map/ppermute | solution.py:653
  (126 other events, 943.3 us)
Sparse Core Ops, SparseCore 0:
  28.4 82.6 all-gather.5
  113.3 82.5 all-gather.7
  197.5 62.0 all-gather.9
  261.0 62.4 all-gather.11
  324.9 62.1 all-gather.13
  454.3 66.2 reduce-scatter.5
  522.9 102.3 reduce-scatter.7
  640.1 48.7 reduce-scatter.9
  691.3 43.1 reduce-scatter.13
  790.6 77.8 reduce-scatter.11

commit v3 on v2

--- a/solution.py
+++ b/solution.py
@@ -570,8 +570,8 @@
     )(at, *blocks)
 
 
-def collect_kernel(count, at, *refs):
-    blocks, outs = refs[:count], refs[count:]
+def collect_kernel(count, n_wait, at, *refs):
+    blocks, outs = refs[:count], refs[count + n_wait :]
     for d, block in enumerate(blocks):
         for c in range(count):
 
@@ -584,17 +584,18 @@
                     begin += width
 
 
-def collect(at, blocks, widths):
+def collect(at, blocks, widths, wait=()):
     rows, count = blocks[0].shape[0], len(blocks)
     return pl.pallas_call(
-        functools.partial(collect_kernel, count),
-        in_specs=[pl.BlockSpec(memory_space=pltpu.SMEM)] + in_vmem(count),
+        functools.partial(collect_kernel, count, len(wait)),
+        in_specs=[pl.BlockSpec(memory_space=pltpu.SMEM)] + in_vmem(count)
+        + [pl.BlockSpec(memory_space=pl.ANY)] * len(wait),
         out_specs=in_vmem(len(widths)),
         out_shape=[jax.ShapeDtypeStruct((rows, w * count), F32) for w in widths],
         compiler_params=pltpu.CompilerParams(vmem_limit_bytes=32 * 2**20),
         cost_estimate=cost(2),
         name="collect",
-    )(at, *blocks)
+    )(at, *blocks, *wait)
 
 
 def tie_kernel(*refs):
@@ -744,10 +745,12 @@
         return a.astype(F32) + b.astype(F32)
 
     def pair_tokens(block):
-        other = across_y(block)
-        whole = jnp.concatenate([block, other], axis=0)
-        swapped = jnp.concatenate([other, block], axis=0)
-        return jnp.where(at_tp == 0, whole, swapped)
+        return order_pair(block, across_y(block))
+
+    def order_pair(block, other):
+        return jnp.where(
+            at_tp == 0, jnp.concatenate([block, other], axis=0), jnp.concatenate([other, block], axis=0)
+        )
 
     at_here = jnp.reshape(at_ctx, (1,)).astype(jnp.int32)
 
@@ -870,21 +873,27 @@
         wait=(g_gates, *ffn_near[2:], g_hidden),
     )
     g_gates = reduce(g_gates)
-    output = pair_tokens((middle + ffn_out).astype(BF16))
+    output = (middle + ffn_out).astype(BF16)
+    output_other = across_y(output)
+    output = order_pair(output, output_other)
+    gw_gate, gw_up, gw_down = collect(
+        at_here, exchange(divide(at_here, (g_hidden, g_last), n_ctx)), (units, units, units), wait=(output_other,)
+    )
     g_first = dense_t(normed1, tie(dx, ffn_out)).astype(BF16)
-    inverse = tie(inverse, g_first, g_out)
+    inverse = tie(inverse, g_first, g_out, g_gates)
     g_first = reduce(g_first)
-    grad_parts = product((tie(dx_all[inverse], output), w_all))
-    later = tie(at_here, grad_parts[3])
-    g_taps = tie(g_taps, grad_parts[3])
-    grad_normed1 = sum_tokens(*grad_parts)
+    grad_parts = product((tie(dx_all[inverse], output, gw_gate), w_all))
+    grad_near = sum_near(*sum_cores(*grad_parts))
+    grad_near = (*grad_near[:2], tie(grad_near[2], g_first), grad_near[3])
+    grad_normed1 = sum_far(*grad_near)
     scale1 = lax.rsqrt(jnp.mean(source * source, axis=-1, keepdims=True) + EPS)
     grad_input = (grad_mid + norm_back(source, scale1, n_mix, grad_normed1)).astype(BF16)
-    grad_input = pair_tokens(grad_input)
-
-    gw_gate, gw_up, gw_down = own(later, (g_hidden, g_last), units, units, units)
-    gw_query, gw_key, gw_value, gw_output, gw_outgate = own(
-        tie(at_here, grad_normed1), (g_first, g_out, g_gates), hk, hk, hv, hv, hv
+    g_taps = tie(g_taps, *grad_parts)
+    later, other = tie(at_here, grad_normed1), across_y(grad_input)
+    grad_input = order_pair(grad_input, other)
+
+    gw_query, gw_key, gw_value, gw_output, gw_outgate = collect(
+        at_here, exchange(divide(later, (g_first, g_out, g_gates), n_ctx)), (hk, hk, hv, hv, hv), wait=(other,)
     )
     gw_output, gw_down = gw_output.T, gw_down.T
 

time: 958 us -> 945 us (0.986)
    unnamed x248 -> x242, local copies, waits for them, and re-layouts: 70.3 us -> 65.6 us
  transfers between devices with their start and end apart: 89 -> 89, of which waited for: 36 -> 39; matrix products, arithmetic and copies ran while one was open for 39% -> 38% of each run, Pallas kernels for 22% -> 22%
where the time goes in v3:
time: 945 us; the launch traced here: 936 us
  Pallas kernels  231 us (24%)
  waiting for transfers between devices  228 us (24%)
  matrix products  173 us (18%)
  local copies, waits for them, and re-layouts  146 us (15%)
  other arithmetic  71.6 us (8%)
  starting transfers between devices  71.3 us (8%)
  between operations  15.9 us (2%)
    ppermute x79, waiting for transfers between devices, flip(): lax.ppermute(a, axis, [(i, i ^ distance) for i in range(size)])  228 us
    ppermute x79, starting transfers between devices, flip(): lax.ppermute(a, axis, [(i, i ^ distance) for i in range(size)])  69.7 us
    dot_general x6, matrix products, dense_t(): lax.dot_general(a, b, (((0,), (0,)), ((), ())), preferred_element_type=F32)  69.1 us
    dot_general x16, matrix products, dense_bt(): lax.dot_general(a, b, (((1,), (1,)), ((), ())), preferred_element_type=F32)  68.6 us
    unnamed x242, local copies, waits for them, and re-layouts  65.6 us
    pallas_call x1, Pallas kernels, prepare(): pl.pallas_call(functools.partial(prepare_kernel, heads, key, val, len(wai...  62.2 us
    pallas_call x1, Pallas kernels, finish(): pl.pallas_call(functools.partial(finish_kernel, heads, key, val, len(wait...  46 us
    dot_general x3, matrix products, dense(): return jnp.dot(a, b, preferred_element_type=F32)  34.9 us
  transfers between devices with their start and end apart: 89, of which 39 were waited for; matrix products, arithmetic and copies ran while one was open for 38% of the time, Pallas kernels for 22%

profile of v3, /device:TPU:0, one launch (start us, length us, event | category | flops | bytes accessed | tf_op | source)
XLA Modules:
  0.0 935.9 jit_solution(3551744342541217163)
XLA Ops:
  12.7 7.2 collective-permute-done.5.refs_2_
  19.9 5.2 collective-permute-done.6.refs_3_
  43.3 5.2 collective-permute-start.7
  51.1 6.5 fusion.23
  57.6 8.6 scatter_custom_fusion.refs_3_.refs_0_
  66.3 21.3 %collective-permute-done.7.refs_1_ = bf16[512,2048]{1,0:T(8,128)(2,1)} collective-permute-done((bf16[512,2048]{1,0:T(8,128)(2,1)}, bf16[512,2048]{1,0:T(8,128)(2,1)}, u32[]{:S(2)}, u32[]{:S(2)}) %collective-permute-start.7) | collective-permute-done | bytes 2097184 | tf_op jit(solution)/shard_map/ppermute | solution.py:654
  89.0 3.1 deal.6
  95.2 6.7 collective-permute-done.11.refs_2_
  101.9 3.8 collective-permute-done.12.refs_3_
  111.1 31.5 %packed_rows.1 = (bf16[2048,2048]{1,0:T(8,128)(2,1)}, bf16[2048,128]{1,0:T(8,128)(2,1)}) custom-call(s32[2048,1]{1,0:T(8,128)} %get-tuple-element.274.order_ref, f32[1,2048]{1,0:T(1,128)} %bitcast.148, bf16[128,2048]{1,0:T(8,128)(2,1)} %pad.9.clone.thin_ref, bf16[512,2048]{1,0:T(8,128)(2,1)} %tie.19.refs_0_, ...), custom_call_target="tpu_custom_call" | custom-call | flops 29899999232 | bytes 26000000 | tf_op jit(solution)/shard_map/packed_rows/pallas_call | solution.py:479
  142.6 13.8 %convolution_convert_fusion.1.raw_ref.before_ref.refs_1_ = bf16[2048,1024]{1,0:T(8,128)(2,1)} fusion(bf16[2048,2048]{1,0:T(8,128)(2,1)} %get-tuple-element.113.normed_ref, bf16[2048,1024]{1,0:T(8,128)(2,1)} %all-gather.6.cloned.1.call-done), kind=kOutput, calls=%fused_computation.7 | convolution fusion | flops 8592031744 | bytes 16777216 | tf_op jit(solution)/shard_map/dot_general | solution.py:642
  156.8 3.0 deal.7
  162.4 6.5 collective-permute-done.14.refs_2_
  174.2 3.0 deal.8
  179.7 6.5 collective-permute-done.17.refs_2_
  199.7 3.0 deal.9
  205.8 62.2 %prepare.1 = (f32[2048,1024]{1,0:T(8,128)}, bf16[2048,256]{1,0:T(8,128)(2,1)}, bf16[2048,256]{1,0:T(8,128)(2,1)}, bf16[2048,256]{1,0:T(8,128)(2,1)}, f32[2048,51...) custom-call(s32[1,4]{1,0:T(1,128)} %lengths.3, ...), custom_call_target="tpu_custom_call" | custom-call | flops 115000000 | bytes 100000 | tf_op jit(solution)/shard_map/prepare/pallas_call | solution.py:361
  279.0 22.1 %forward.1 = (bf16[2048,512]{1,0:T(8,128)(2,1)}, f32[2048,512]{1,0:T(8,128)}, bf16[2048,512]{1,0:T(8,128)(2,1)}, bf16[2048,512]{1,0:T(8,128)(2,1)}, bf16[16,2,128,256]{3,2,1,0:T(8,128)(2,1)}) custom-call(bf16[2048,256]{1,0:T(8,128)(2,1)} %get-tuple-element.119.qe_ref, bf16[2048,256]{1,0:T(8,128)(2,1)} %get-tuple-element.120.w_ref, ...), custom_call_target="tpu_custom_call" | custom-call | flops 115000000 | bytes 100000 | tf_op jit(solution)/shard_map/forward/pallas_call | solution.py:387
  301.1 11.1 %gather_fusion = bf16[2048,512]{1,0:T(8,128)(2,1)} fusion(bf16[2048,512]{1,0:T(8,128)(2,1)} %get-tuple-element.133, s32[2048]{0:T(1024)S(1)} %fusion.70), kind=kCustom, calls=%fused_computation | custom fusion | bytes 4202496 | tf_op jit(solution)/shard_map/gather | solution.py:835
  312.2 3.2 convolution_convert_fusion.15
  341.2 13.0 %collective-permute-done.26 = bf16[256,2048]{1,0:T(8,128)(2,1)S(1)} collective-permute-done((bf16[256,2048]{1,0:T(8,128)(2,1)S(1)}, bf16[256,2048]{1,0:T(8,128)(2,1)S(1)}, u32[]{:S(2)}, u32[]{:S(2)}) %collective-permute-start.26) | collective-permute-done | bytes 1048608 | tf_op jit(solution)/shard_map/ppermute | solution.py:654
  359.8 12.2 %fusion.99.refs_1_.grad_ref = f32[2048,704]{1,0:T(8,128)} fusion(bf16[2048,2048]{1,0:T(8,128)(2,1)} %dynamic-slice_dynamic-update-slice_fusion, bf16[2048,704]{1,0:T(8,128)(2,1)} %all-gather.10.cloned.1.call-done), kind=kOutput, calls=%fused_computation.335 | convolution fusion | flops 5905580032 | bytes 17039360 | tf_op jit(solution)/shard_map/dot_general | solution.py:642
  380.6 9.3 collective-permute-done.31
  396.7 17.0 %collective-permute-done.34 = bf16[256,2048]{1,0:T(8,128)(2,1)S(1)} collective-permute-done((bf16[256,2048]{1,0:T(8,128)(2,1)S(1)}, bf16[256,2048]{1,0:T(8,128)(2,1)S(1)}, u32[]{:S(2)}, u32[]{:S(2)}) %collective-permute-start.34) | collective-permute-done | bytes 1048608 | tf_op jit(solution)/shard_map/ppermute | solution.py:654
  422.8 19.8 %hidden_units.1 = (bf16[2048,704]{1,0:T(8,128)(2,1)}, bf16[2048,1408]{1,0:T(8,128)(2,1)}) custom-call(bf16[2048,2048]{1,0:T(8,128)(2,1)} %constant_dynamic-update-slice_fusion.rows_ref.refs_0_, bf16[2048,704]{1,0:T(8,128)(2,1)} %all-gather.12.cloned.1.call-done.refs_2_.gate_ref, bf16[2048,704]{1,0:T(8,128)(2,1)} %all-gather.14.cloned.1.call-done.up_ref, ...), custom_call_target="tpu_custom_call" | custom-call | flops 115000000 | bytes 100000 | tf_op jit(solution)/shard_map/hidden_units/pallas_call | solution.py:509
  442.5 11.3 %convolution_convert_fusion.3.refs_1_ = bf16[2048,704]{1,0:T(8,128)(2,1)} fusion(bf16[2048,2048]{1,0:T(8,128)(2,1)} %dynamic-slice_dynamic-update-slice_fusion, bf16[2048,704]{1,0:T(8,128)(2,1)} %get-tuple-element.146), kind=kOutput, calls=%fused_computation.13 | convolution fusion | flops 5907021824 | bytes 14155776 | tf_op jit(solution)/shard_map/dot_general | solution.py:646
  454.0 8.2 convolution_convert_fusion.19.refs_2_
  462.2 5.1 convolution_convert_fusion.21.refs_1_
  467.8 3.3 pad_maximum_fusion.refs_7_
  471.0 4.9 convolution_convert_fusion.20.refs_4_
  475.9 4.9 convolution_convert_fusion.22.refs_3_
  480.8 3.1 add_convert_fusion.5
  489.7 19.1 %convolution_convert_fusion.refs_5_ = bf16[2048,1408]{1,0:T(8,128)(2,1)} fusion(bf16[2048,2048]{1,0:T(8,128)(2,1)} %tie.26, bf16[2048,1408]{1,0:T(8,128)(2,1)} %tie.25), kind=kOutput, calls=%fused_computation.4 | convolution fusion | flops 11814043648 | bytes 19922944 | tf_op jit(solution)/shard_map/dot_general | solution.py:646
  509.3 5.4 convolution_convert_fusion.11.refs_4_
  514.8 3.3 convolution_convert_fusion.12.refs_2_.refs_0_
  523.1 3.2 convolution_convert_fusion.14.refs_3_
  526.3 3.2 convolution_convert_fusion.13.refs_1_.refs_0_
  529.5 4.2 collective-permute-done.43
  544.0 10.4 %collective-permute-done.45 = bf16[128,2048]{1,0:T(8,128)(2,1)S(1)} collective-permute-done((bf16[128,2048]{1,0:T(8,128)(2,1)S(1)}, bf16[128,2048]{1,0:T(8,128)(2,1)S(1)}, u32[]{:S(2)}, u32[]{:S(2)}) %collective-permute-start.45) | collective-permute-done | bytes 524320 | tf_op jit(solution)/shard_map/ppermute | solution.py:654
  558.3 19.7 %collective-permute-done.48 = bf16[256,2048]{1,0:T(8,128)(2,1)S(1)} collective-permute-done((bf16[256,2048]{1,0:T(8,128)(2,1)S(1)}, bf16[256,2048]{1,0:T(8,128)(2,1)S(1)}, u32[]{:S(2)}, u32[]{:S(2)}) %collective-permute-start.48) | collective-permute-done | bytes 1048608 | tf_op jit(solution)/shard_map/ppermute | solution.py:654
  588.5 9.0 convolution_convert_fusion.10
  603.7 9.2 gather_fusion.1
  612.9 16.7 %backward.1 = (bf16[2048,512]{1,0:T(8,128)(2,1)}, f32[1,256]{1,0:T(1,128)}, bf16[2048,512]{1,0:T(8,128)(2,1)}, bf16[2048,512]{1,0:T(8,128)(2,1)}, bf16[16,2,128,256]{3,2,1,0:T(8,128)(2,1)}) custom-call(bf16[2048,512]{1,0:T(8,128)(2,1)} %gather_fusion.1, f32[2048,512]{1,0:T(8,128)} %get-tuple-element.165.mixed_ref, ...), custom_call_target="tpu_custom_call" | custom-call | flops 115000000 | bytes 100000 | tf_op jit(solution)/shard_map/backward/pallas_call | solution.py:412
  629.7 10.0 %convolution_convert_fusion.8 = bf16[2048,512]{1,0:T(8,128)(2,1)} fusion(bf16[2048,2048]{1,0:T(8,128)(2,1)} %constant_dynamic-update-slice_fusion.10.refs_1_, bf16[2048,512]{1,0:T(8,128)(2,1)} %tie.32), kind=kOutput, calls=%fused_computation.19 | convolution fusion | flops 4296015872 | bytes 12582912 | tf_op jit(solution)/shard_map/dot_general | solution.py:646
  641.7 9.5 %convolution_convert_fusion.9.refs_0_ = bf16[2048,512]{1,0:T(8,128)(2,1)} fusion(bf16[2048,2048]{1,0:T(8,128)(2,1)} %get-tuple-element.113.normed_ref, bf16[2048,512]{1,0:T(8,128)(2,1)S(1)} %copy-done.26), kind=kOutput, calls=%fused_computation.20 | convolution fusion | flops 4296015872 | bytes 12582912 | tf_op jit(solution)/shard_map/dot_general | solution.py:646
  659.6 5.3 collective-permute-done.56
  673.9 46.0 %finish.1 = (bf16[2048,1024]{1,0:T(8,128)(2,1)}, bf16[2048,128]{1,0:T(8,128)(2,1)}, bf16[2048,1664]{1,0:T(8,128)(2,1)}, f32[8,1024]{1,0:T(8,128)}, f32[8,128]{1,0:T(8,128)}) custom-call(s32[1,4]{1,0:T(1,128)} %lengths.3, bf16[2048,1024]{1,0:T(8,128)(2,1)} %convolution_convert_fusion.1.raw_ref.before_ref.refs_1_, ...), custom_call_target="tpu_custom_call" | custom-call | flops 115000000 | bytes 100000 | tf_op jit(solution)/shard_map/finish/pallas_call | solution.py:441
  719.9 4.9 fusion.54
  731.9 14.1 %convolution_convert_fusion.2.refs_1_ = bf16[2048,1024]{1,0:T(8,128)(2,1)} fusion(bf16[2048,2048]{1,0:T(8,128)(2,1)} %get-tuple-element.113.normed_ref, bf16[2048,1024]{1,0:T(8,128)(2,1)} %tie.31), kind=kOutput, calls=%fused_computation.8 | convolution fusion | flops 8592031744 | bytes 16777216 | tf_op jit(solution)/shard_map/dot_general | solution.py:646
  758.6 17.7 %gather_fusion.2 = bf16[2048,1664]{1,0:T(8,128)(2,1)} fusion(bf16[2048,1664]{1,0:T(8,128)(2,1)} %get-tuple-element.172, s32[2048]{0:T(1024)S(1)} %fusion.72), kind=kCustom, calls=%fused_computation.2 | custom fusion | bytes 13639680 | tf_op jit(solution)/shard_map/gather | solution.py:885
  777.9 7.5 convolution_convert_fusion.4.refs_2_
  785.4 5.3 convolution_convert_fusion.6.refs_1_
  791.2 5.2 convolution_convert_fusion.5.refs_4_
  796.4 5.4 convolution_convert_fusion.7.refs_3_
  802.8 5.1 collective-permute-start.73
  807.9 3.9 collective-permute-done.73
  811.8 5.6 collective-permute-start.74
  817.3 6.9 collective-permute-done.74
  829.9 3.3 collective-permute-done.76
  839.9 20.7 %collective-permute-done.66 = bf16[256,2048]{1,0:T(8,128)(2,1)S(1)} collective-permute-done((bf16[256,2048]{1,0:T(8,128)(2,1)S(1)}, bf16[256,2048]{1,0:T(8,128)(2,1)S(1)}, u32[]{:S(2)}, u32[]{:S(2)}) %collective-permute-start.66) | collective-permute-done | bytes 1048608 | tf_op jit(solution)/shard_map/ppermute | solution.py:654
  874.4 7.0 collective-permute-done.68
  895.5 12.3 %collective-permute-done.71.refs_2_ = bf16[128,2048]{1,0:T(8,128)(2,1)S(1)} collective-permute-done((bf16[128,2048]{1,0:T(8,128)(2,1)S(1)}, bf16[128,2048]{1,0:T(8,128)(2,1)S(1)}, u32[]{:S(2)}, u32[]{:S(2)}) %collective-permute-start.71) | collective-permute-done | bytes 524320 | tf_op jit(solution)/shard_map/ppermute | solution.py:654
  907.8 10.3 %collective-permute-done.72.refs_3_ = bf16[128,2048]{1,0:T(8,128)(2,1)S(1)} collective-permute-done((bf16[128,2048]{1,0:T(8,128)(2,1)S(1)}, bf16[128,2048]{1,0:T(8,128)(2,1)S(1)}, u32[]{:S(2)}, u32[]{:S(2)}) %collective-permute-start.72) | collective-permute-done | bytes 524320 | tf_op jit(solution)/shard_map/ppermute | solution.py:654
  923.2 3.8 maximum_select_fusion.1
  (561 shorter events, 261.4 us)
Async XLA Ops:
  7.2 135.4 %all-gather.6.cloned.1.call-start = ((), (), s32[]{:S(2)}) async-start(), calls=%async_computation.5 | async-start | bytes 5242880 | tf_op jit(solution)/shard_map/all_gather | solution.py:765
  12.5 12.6 %collective-permute-start.6 = (bf16[128,1024]{1,0:T(8,128)(2,1)}, bf16[128,1024]{1,0:T(8,128)(2,1)S(1)}, u32[]{:S(2)}, u32[]{:S(2)}) collective-permute-start(bf16[128,1024]{1,0:T(8,128)(2,1)} %get-tuple-element.112), channel_id=1, source_target_pairs={{0,6},{2,4},{4,2},{6,0},{1,7},{3,5},{5,3},{7,1},{8,14},{10,12},{12... | collective-permute-start | bytes 786440 | tf_op jit(solution)/shard_map/ppermute | solution.py:654
  28.3 250.7 %all-gather.8.cloned.1.call-start = ((), (), s32[]{:S(2)}) async-start(), calls=%async_computation.6 | async-start | bytes 5242880 | tf_op jit(solution)/shard_map/all_gather | solution.py:765
  43.3 44.3 %collective-permute-start.7 = (bf16[512,2048]{1,0:T(8,128)(2,1)}, bf16[512,2048]{1,0:T(8,128)(2,1)}, u32[]{:S(2)}, u32[]{:S(2)}) collective-permute-start(bf16[512,2048]{1,0:T(8,128)(2,1)} %tie.19.refs_0_), channel_id=1, source_target_pairs={{0,4},{2,6},{4,0},{6,2},{1,5},{3,7},{5,1},{7,3},{8,12},{10,14},{12... | collective-permute-start | bytes 6291464 | tf_op jit(solution)/shard_map/ppermute | solution.py:654
  66.2 44.8 %collective-permute-start.8 = (bf16[512,2048]{1,0:T(8,128)(2,1)S(1)}, bf16[512,2048]{1,0:T(8,128)(2,1)}, u32[]{:S(2)}, u32[]{:S(2)}) collective-permute-start(bf16[512,2048]{1,0:T(8,128)(2,1)S(1)} %copy-done.34), channel_id=1, source_target_pairs={{0,2},{2,0},{4,6},{6,4},{1,3},{3,1},{5,7},{7,5},{8,10},{10,8},{12,... | collective-permute-start | bytes 6291464 | tf_op jit(solution)/shard_map/ppermute | solution.py:654
  87.6 23.4 %collective-permute-start.9 = (bf16[512,2048]{1,0:T(8,128)(2,1)}, bf16[512,2048]{1,0:T(8,128)(2,1)}, u32[]{:S(2)}, u32[]{:S(2)}) collective-permute-start(bf16[512,2048]{1,0:T(8,128)(2,1)} %collective-permute-done.7.refs_1_), channel_id=1, source_target_pairs={{0,2},{2,0},{4,6},{6,4},{1,3},{3,1},{5,7},{7,5},{8,10},{10,8},{12,... | collective-permute-start | bytes 6291464 | tf_op jit(solution)/shard_map/ppermute | solution.py:654
  94.0 11.7 %collective-permute-start.12 = (bf16[128,1024]{1,0:T(8,128)(2,1)}, bf16[128,1024]{1,0:T(8,128)(2,1)}, u32[]{:S(2)}, u32[]{:S(2)}) collective-permute-start(bf16[128,1024]{1,0:T(8,128)(2,1)} %get-tuple-element.118), channel_id=1, source_target_pairs={{0,6},{2,4},{4,2},{6,0},{1,7},{3,5},{5,3},{7,1},{8,14},{10,12},{12... | collective-permute-start | bytes 786440 | tf_op jit(solution)/shard_map/ppermute | solution.py:654
  108.0 251.8 %all-gather.10.cloned.1.call-start = ((), (), s32[]{:S(2)}) async-start(), calls=%async_computation.7 | async-start | bytes 3932160 | tf_op jit(solution)/shard_map/all_gather | solution.py:765
  174.1 201.4 %all-gather.12.cloned.1.call-start = ((), (), s32[]{:S(2)}) async-start(), calls=%async_computation.8 | async-start | bytes 3932160 | tf_op jit(solution)/shard_map/all_gather | solution.py:765
  191.6 231.2 %all-gather.14.cloned.1.call-start = ((), (), s32[]{:S(2)}) async-start(), calls=%async_computation.9 | async-start | bytes 3932160 | tf_op jit(solution)/shard_map/all_gather | solution.py:765
  193.0 78.4 %collective-permute-start.19 = (bf16[512,2048]{1,0:T(8,128)(2,1)}, bf16[512,2048]{1,0:T(8,128)(2,1)}, u32[]{:S(2)}, u32[]{:S(2)}) collective-permute-start(bf16[512,2048]{1,0:T(8,128)(2,1)} %tie.22), channel_id=1, source_target_pairs={{0,4},{2,6},{4,0},{6,2},{1,5},{3,7},{5,1},{7,3},{8,12},{10,14},{12... | collective-permute-start | bytes 6291464 | tf_op jit(solution)/shard_map/ppermute | solution.py:654
  194.5 125.6 %collective-permute-start.29 = (bf16[512,2048]{1,0:T(8,128)(2,1)S(1)}, bf16[512,2048]{1,0:T(8,128)(2,1)}, u32[]{:S(2)}, u32[]{:S(2)}) collective-permute-start(bf16[512,2048]{1,0:T(8,128)(2,1)S(1)} %copy-done.15), channel_id=1, source_target_pairs={{0,2},{2,0},{4,6},{6,4},{1,3},{3,1},{5,7},{7,5},{8,10},{10,8},{12,... | collective-permute-start | bytes 6291464 | tf_op jit(solution)/shard_map/ppermute | solution.py:654
  202.7 65.3 %collective-permute-start.20 = (bf16[128,704]{1,0:T(8,128)(2,1)}, bf16[128,704]{1,0:T(8,128)(2,1)S(1)}, u32[]{:S(2)}, u32[]{:S(2)}) collective-permute-start(bf16[128,704]{1,0:T(8,128)(2,1)} %get-tuple-element.135), channel_id=1, source_target_pairs={{0,2},{2,0},{4,6},{6,4},{1,3},{3,1},{5,7},{7,5},{8,10},{10,8},{12,... | collective-permute-start | bytes 540680 | tf_op jit(solution)/shard_map/ppermute | solution.py:654
  202.7 65.4 %collective-permute-start.21 = (bf16[128,704]{1,0:T(8,128)(2,1)}, bf16[128,704]{1,0:T(8,128)(2,1)S(1)}, u32[]{:S(2)}, u32[]{:S(2)}) collective-permute-start(bf16[128,704]{1,0:T(8,128)(2,1)} %get-tuple-element.136), channel_id=1, source_target_pairs={{0,4},{2,6},{4,0},{6,2},{1,5},{3,7},{5,1},{7,3},{8,12},{10,14},{12... | collective-permute-start | bytes 540680 | tf_op jit(solution)/shard_map/ppermute | solution.py:654
  203.5 64.5 %collective-permute-start.22 = (bf16[128,704]{1,0:T(8,128)(2,1)}, bf16[128,704]{1,0:T(8,128)(2,1)S(1)}, u32[]{:S(2)}, u32[]{:S(2)}) collective-permute-start(bf16[128,704]{1,0:T(8,128)(2,1)} %get-tuple-element.137), channel_id=1, source_target_pairs={{0,6},{2,4},{4,2},{6,0},{1,7},{3,5},{5,3},{7,1},{8,14},{10,12},{12... | collective-permute-start | bytes 540680 | tf_op jit(solution)/shard_map/ppermute | solution.py:654
  271.1 268.9 %reduce-scatter.6.cloned.1.call-start = ((), (), s32[]{:S(2)}) async-start(), calls=%async_computation.10 | async-start | bytes 3932160 | tf_op jit(solution)/shard_map/reduce_scatter | solution.py:768
  271.4 55.1 %collective-permute-start.30 = (bf16[512,2048]{1,0:T(8,128)(2,1)}, bf16[512,2048]{1,0:T(8,128)(2,1)}, u32[]{:S(2)}, u32[]{:S(2)}) collective-permute-start(bf16[512,2048]{1,0:T(8,128)(2,1)} %collective-permute-done.19.refs_1_), channel_id=1, source_target_pairs={{0,2},{2,0},{4,6},{6,4},{1,3},{3,1},{5,7},{7,5},{8,10},{10,8},{12,... | collective-permute-start | bytes 6291464 | tf_op jit(solution)/shard_map/ppermute | solution.py:654
  315.4 13.0 %collective-permute-start.25 = (bf16[512,2048]{1,0:T(8,128)(2,1)S(1)}, bf16[512,2048]{1,0:T(8,128)(2,1)S(1)}, u32[]{:S(2)}, u32[]{:S(2)}) collective-permute-start(bf16[512,2048]{1,0:T(8,128)(2,1)S(1)} %convolution_convert_fusion.15), channel_id=1, source_target_pairs={{0,2},{2,0},{4,6},{6,4},{1,3},{3,1},{5,7},{7,5},{8,10},{10,8},{12,... | collective-permute-start | bytes 6291464 | tf_op jit(solution)/shard_map/ppermute | solution.py:654
  317.8 12.5 %collective-permute-start.23 = (bf16[512,2048]{1,0:T(8,128)(2,1)S(1)}, bf16[512,2048]{1,0:T(8,128)(2,1)S(1)}, u32[]{:S(2)}, u32[]{:S(2)}) collective-permute-start(bf16[512,2048]{1,0:T(8,128)(2,1)S(1)} %convolution_convert_fusion.17), channel_id=1, source_target_pairs={{0,2},{2,0},{4,6},{6,4},{1,3},{3,1},{5,7},{7,5},{8,10},{10,8},{12,... | collective-permute-start | bytes 6291464 | tf_op jit(solution)/shard_map/ppermute | solution.py:654
  328.8 25.3 %collective-permute-start.26 = (bf16[256,2048]{1,0:T(8,128)(2,1)S(1)}, bf16[256,2048]{1,0:T(8,128)(2,1)S(1)}, u32[]{:S(2)}, u32[]{:S(2)}) collective-permute-start(bf16[256,2048]{1,0:T(8,128)(2,1)S(1)} %add_convert_fusion.7), channel_id=1, source_target_pairs={{0,1},{1,0},{2,3},{3,2},{4,5},{5,4},{6,7},{7,6},{8,9},{9,8},{10,11... | collective-permute-start | bytes 3145736 | tf_op jit(solution)/shard_map/ppermute | solution.py:654
  330.8 25.1 %collective-permute-start.24 = (bf16[256,2048]{1,0:T(8,128)(2,1)S(1)}, bf16[256,2048]{1,0:T(8,128)(2,1)S(1)}, u32[]{:S(2)}, u32[]{:S(2)}) collective-permute-start(bf16[256,2048]{1,0:T(8,128)(2,1)S(1)} %add_convert_fusion.8), channel_id=1, source_target_pairs={{0,4},{2,6},{4,0},{6,2},{1,5},{3,7},{5,1},{7,3},{8,12},{10,14},{12... | collective-permute-start | bytes 3145736 | tf_op jit(solution)/shard_map/ppermute | solution.py:654
  357.3 14.7 %collective-permute-start.27 = (bf16[128,2048]{1,0:T(8,128)(2,1)}, bf16[128,2048]{1,0:T(8,128)(2,1)S(1)}, u32[]{:S(2)}, u32[]{:S(2)}) collective-permute-start(bf16[128,2048]{1,0:T(8,128)(2,1)} %slice.560), channel_id=1, source_target_pairs={{0,1},{1,0},{2,3},{3,2},{4,5},{5,4},{6,7},{7,6},{8,9},{9,8},{10,11... | collective-permute-start | bytes 1572872 | tf_op jit(solution)/shard_map/ppermute | solution.py:654
  359.2 13.0 %collective-permute-start.28 = (bf16[128,2048]{1,0:T(8,128)(2,1)}, bf16[128,2048]{1,0:T(8,128)(2,1)}, u32[]{:S(2)}, u32[]{:S(2)}) collective-permute-start(bf16[128,2048]{1,0:T(8,128)(2,1)} %slice.559), channel_id=1, source_target_pairs={{0,4},{2,6},{4,0},{6,2},{1,5},{3,7},{5,1},{7,3},{8,12},{10,14},{12... | collective-permute-start | bytes 1572872 | tf_op jit(solution)/shard_map/ppermute | solution.py:654
  377.7 12.3 %collective-permute-start.31 = (bf16[128,2048]{1,0:T(8,128)(2,1)S(1)}, bf16[128,2048]{1,0:T(8,128)(2,1)S(1)}, u32[]{:S(2)}, u32[]{:S(2)}) collective-permute-start(bf16[128,2048]{1,0:T(8,128)(2,1)S(1)} %get-tuple-element.273), channel_id=1, source_target_pairs={{0,1},{1,0},{2,3},{3,2},{4,5},{5,4},{6,7},{7,6},{8,9},{9,8},{10,11... | collective-permute-start | bytes 1572872 | tf_op jit(solution)/shard_map/ppermute | solution.py:654
  379.2 12.0 %collective-permute-start.32 = (bf16[128,2048]{1,0:T(8,128)(2,1)S(1)}, bf16[128,2048]{1,0:T(8,128)(2,1)S(1)}, u32[]{:S(2)}, u32[]{:S(2)}) collective-permute-start(bf16[128,2048]{1,0:T(8,128)(2,1)S(1)} %get-tuple-element.271), channel_id=1, source_target_pairs={{0,4},{2,6},{4,0},{6,2},{1,5},{3,7},{5,1},{7,3},{8,12},{10,14},{12... | collective-permute-start | bytes 1572872 | tf_op jit(solution)/shard_map/ppermute | solution.py:654
  391.3 22.4 %collective-permute-start.34 = (bf16[256,2048]{1,0:T(8,128)(2,1)S(1)}, bf16[256,2048]{1,0:T(8,128)(2,1)S(1)}, u32[]{:S(2)}, u32[]{:S(2)}) collective-permute-start(bf16[256,2048]{1,0:T(8,128)(2,1)S(1)} %pad_maximum_fusion.5), channel_id=1, source_target_pairs={{0,1},{1,0},{2,3},{3,2},{4,5},{5,4},{6,7},{7,6},{8,9},{9,8},{10,11... | collective-permute-start | bytes 3145736 | tf_op jit(solution)/shard_map/ppermute | solution.py:654
  391.9 22.3 %collective-permute-start.33 = (bf16[256,2048]{1,0:T(8,128)(2,1)S(1)}, bf16[256,2048]{1,0:T(8,128)(2,1)S(1)}, u32[]{:S(2)}, u32[]{:S(2)}) collective-permute-start(bf16[256,2048]{1,0:T(8,128)(2,1)S(1)} %pad_maximum_fusion.4), channel_id=1, source_target_pairs={{0,4},{2,6},{4,0},{6,2},{1,5},{3,7},{5,1},{7,3},{8,12},{10,14},{12... | collective-permute-start | bytes 3145736 | tf_op jit(solution)/shard_map/ppermute | solution.py:654
  395.4 23.1 %collective-permute-start.35 = (bf16[256,2048]{1,0:T(8,128)(2,1)S(1)}, bf16[256,2048]{1,0:T(8,128)(2,1)S(1)}, u32[]{:S(2)}, u32[]{:S(2)}) collective-permute-start(bf16[256,2048]{1,0:T(8,128)(2,1)S(1)} %pad_maximum_fusion.4), channel_id=1, source_target_pairs={{0,2},{2,0},{4,6},{6,4},{1,3},{3,1},{5,7},{7,5},{8,10},{10,8},{12,... | collective-permute-start | bytes 3145736 | tf_op jit(solution)/shard_map/ppermute | solution.py:654
  395.4 25.3 %collective-permute-start.37 = (bf16[256,2048]{1,0:T(8,128)(2,1)S(1)}, bf16[256,2048]{1,0:T(8,128)(2,1)S(1)}, u32[]{:S(2)}, u32[]{:S(2)}) collective-permute-start(bf16[256,2048]{1,0:T(8,128)(2,1)S(1)} %pad_maximum_fusion.5), channel_id=1, source_target_pairs={{0,2},{2,0},{4,6},{6,4},{1,3},{3,1},{5,7},{7,5},{8,10},{10,8},{12,... | collective-permute-start | bytes 3145736 | tf_op jit(solution)/shard_map/ppermute | solution.py:654
  453.9 197.8 %reduce-scatter.8.cloned.1.call-start = ((), (), s32[]{:S(2)}) async-start(), calls=%async_computation.11 | async-start | bytes 7208960 | tf_op jit(solution)/shard_map/reduce_scatter | solution.py:768
  462.1 18.7 %collective-permute-start.41 = (bf16[512,2048]{1,0:T(8,128)(2,1)}, bf16[512,2048]{1,0:T(8,128)(2,1)}, u32[]{:S(2)}, u32[]{:S(2)}) collective-permute-start(bf16[512,2048]{1,0:T(8,128)(2,1)} %convolution_convert_fusion.19.refs_2_), channel_id=1, source_target_pairs={{0,2},{2,0},{4,6},{6,4},{1,3},{3,1},{5,7},{7,5},{8,10},{10,8},{12,... | collective-permute-start | bytes 6291464 | tf_op jit(solution)/shard_map/ppermute | solution.py:654
  467.3 18.1 %collective-permute-start.39 = (bf16[512,2048]{1,0:T(8,128)(2,1)}, bf16[512,2048]{1,0:T(8,128)(2,1)}, u32[]{:S(2)}, u32[]{:S(2)}) collective-permute-start(bf16[512,2048]{1,0:T(8,128)(2,1)} %convolution_convert_fusion.21.refs_1_), channel_id=1, source_target_pairs={{0,2},{2,0},{4,6},{6,4},{1,3},{3,1},{5,7},{7,5},{8,10},{10,8},{12,... | collective-permute-start | bytes 6291464 | tf_op jit(solution)/shard_map/ppermute | solution.py:654
  483.9 34.2 %collective-permute-start.42 = (bf16[256,2048]{1,0:T(8,128)(2,1)}, bf16[256,2048]{1,0:T(8,128)(2,1)S(1)}, u32[]{:S(2)}, u32[]{:S(2)}) collective-permute-start(bf16[256,2048]{1,0:T(8,128)(2,1)} %add_convert_fusion.5), channel_id=1, source_target_pairs={{0,1},{1,0},{2,3},{3,2},{4,5},{5,4},{6,7},{7,6},{8,9},{9,8},{10,11... | collective-permute-start | bytes 3145736 | tf_op jit(solution)/shard_map/ppermute | solution.py:654
  488.0 30.1 %collective-permute-start.40 = (bf16[256,2048]{1,0:T(8,128)(2,1)}, bf16[256,2048]{1,0:T(8,128)(2,1)}, u32[]{:S(2)}, u32[]{:S(2)}) collective-permute-start(bf16[256,2048]{1,0:T(8,128)(2,1)} %add_convert_fusion.6), channel_id=1, source_target_pairs={{0,4},{2,6},{4,0},{6,2},{1,5},{3,7},{5,1},{7,3},{8,12},{10,14},{12... | collective-permute-start | bytes 3145736 | tf_op jit(solution)/shard_map/ppermute | solution.py:654
  508.9 249.0 %reduce-scatter.10.cloned.1.call-start = ((), (), s32[]{:S(2)}) async-start(), calls=%async_computation.12 | async-start | bytes 2621440 | tf_op jit(solution)/shard_map/reduce_scatter | solution.py:768
  520.4 13.3 %collective-permute-start.43 = (bf16[128,2048]{1,0:T(8,128)(2,1)S(1)}, bf16[128,2048]{1,0:T(8,128)(2,1)S(1)}, u32[]{:S(2)}, u32[]{:S(2)}) collective-permute-start(bf16[128,2048]{1,0:T(8,128)(2,1)S(1)} %slice.558), channel_id=1, source_target_pairs={{0,1},{1,0},{2,3},{3,2},{4,5},{5,4},{6,7},{7,6},{8,9},{9,8},{10,11... | collective-permute-start | bytes 1572872 | tf_op jit(solution)/shard_map/ppermute | solution.py:654
  522.7 13.1 %collective-permute-start.44 = (bf16[128,2048]{1,0:T(8,128)(2,1)S(1)}, bf16[128,2048]{1,0:T(8,128)(2,1)S(1)}, u32[]{:S(2)}, u32[]{:S(2)}) collective-permute-start(bf16[128,2048]{1,0:T(8,128)(2,1)S(1)} %slice.557), channel_id=1, source_target_pairs={{0,4},{2,6},{4,0},{6,2},{1,5},{3,7},{5,1},{7,3},{8,12},{10,14},{12... | collective-permute-start | bytes 1572872 | tf_op jit(solution)/shard_map/ppermute | solution.py:654
  542.2 12.2 %collective-permute-start.45 = (bf16[128,2048]{1,0:T(8,128)(2,1)S(1)}, bf16[128,2048]{1,0:T(8,128)(2,1)S(1)}, u32[]{:S(2)}, u32[]{:S(2)}) collective-permute-start(bf16[128,2048]{1,0:T(8,128)(2,1)S(1)} %get-tuple-element.270), channel_id=1, source_target_pairs={{0,1},{1,0},{2,3},{3,2},{4,5},{5,4},{6,7},{7,6},{8,9},{9,8},{10,11... | collective-permute-start | bytes 1572872 | tf_op jit(solution)/shard_map/ppermute | solution.py:654
  543.7 11.9 %collective-permute-start.46 = (bf16[128,2048]{1,0:T(8,128)(2,1)S(1)}, bf16[128,2048]{1,0:T(8,128)(2,1)S(1)}, u32[]{:S(2)}, u32[]{:S(2)}) collective-permute-start(bf16[128,2048]{1,0:T(8,128)(2,1)S(1)} %get-tuple-element.268), channel_id=1, source_target_pairs={{0,4},{2,6},{4,0},{6,2},{1,5},{3,7},{5,1},{7,3},{8,12},{10,14},{12... | collective-permute-start | bytes 1572872 | tf_op jit(solution)/shard_map/ppermute | solution.py:654
  555.7 22.4 %collective-permute-start.48 = (bf16[256,2048]{1,0:T(8,128)(2,1)S(1)}, bf16[256,2048]{1,0:T(8,128)(2,1)S(1)}, u32[]{:S(2)}, u32[]{:S(2)}) collective-permute-start(bf16[256,2048]{1,0:T(8,128)(2,1)S(1)} %pad_maximum_fusion.7), channel_id=1, source_target_pairs={{0,1},{1,0},{2,3},{3,2},{4,5},{5,4},{6,7},{7,6},{8,9},{9,8},{10,11... | collective-permute-start | bytes 3145736 | tf_op jit(solution)/shard_map/ppermute | solution.py:654
  556.4 22.1 %collective-permute-start.47 = (bf16[256,2048]{1,0:T(8,128)(2,1)S(1)}, bf16[256,2048]{1,0:T(8,128)(2,1)S(1)}, u32[]{:S(2)}, u32[]{:S(2)}) collective-permute-start(bf16[256,2048]{1,0:T(8,128)(2,1)S(1)} %pad_maximum_fusion.6), channel_id=1, source_target_pairs={{0,4},{2,6},{4,0},{6,2},{1,5},{3,7},{5,1},{7,3},{8,12},{10,14},{12... | collective-permute-start | bytes 3145736 | tf_op jit(solution)/shard_map/ppermute | solution.py:654
  556.9 25.9 %collective-permute-start.49 = (bf16[256,2048]{1,0:T(8,128)(2,1)S(1)}, bf16[256,2048]{1,0:T(8,128)(2,1)S(1)}, u32[]{:S(2)}, u32[]{:S(2)}) collective-permute-start(bf16[256,2048]{1,0:T(8,128)(2,1)S(1)} %pad_maximum_fusion.6), channel_id=1, source_target_pairs={{0,2},{2,0},{4,6},{6,4},{1,3},{3,1},{5,7},{7,5},{8,10},{10,8},{12,... | collective-permute-start | bytes 3145736 | tf_op jit(solution)/shard_map/ppermute | solution.py:654
  556.9 28.2 %collective-permute-start.51 = (bf16[256,2048]{1,0:T(8,128)(2,1)S(1)}, bf16[256,2048]{1,0:T(8,128)(2,1)S(1)}, u32[]{:S(2)}, u32[]{:S(2)}) collective-permute-start(bf16[256,2048]{1,0:T(8,128)(2,1)S(1)} %pad_maximum_fusion.7), channel_id=1, source_target_pairs={{0,2},{2,0},{4,6},{6,4},{1,3},{3,1},{5,7},{7,5},{8,10},{10,8},{12,... | collective-permute-start | bytes 3145736 | tf_op jit(solution)/shard_map/ppermute | solution.py:654
  587.2 13.1 %collective-permute-start.53 = (bf16[512,2048]{1,0:T(8,128)(2,1)}, bf16[512,2048]{1,0:T(8,128)(2,1)S(1)}, u32[]{:S(2)}, u32[]{:S(2)}) collective-permute-start(bf16[512,2048]{1,0:T(8,128)(2,1)} %tie.28), channel_id=1, source_target_pairs={{0,2},{2,0},{4,6},{6,4},{1,3},{3,1},{5,7},{7,5},{8,10},{10,8},{12,... | collective-permute-start | bytes 6291464 | tf_op jit(solution)/shard_map/ppermute | solution.py:654
  639.7 118.2 %reduce-scatter.12.cloned.1.call-start = ((), (), s32[]{:S(2)}) async-start(), calls=%async_computation.13 | async-start | bytes 2621440 | tf_op jit(solution)/shard_map/reduce_scatter | solution.py:768
  639.8 25.2 %collective-permute-start.56 = (bf16[256,2048]{1,0:T(8,128)(2,1)S(1)}, bf16[256,2048]{1,0:T(8,128)(2,1)}, u32[]{:S(2)}, u32[]{:S(2)}) collective-permute-start(bf16[256,2048]{1,0:T(8,128)(2,1)S(1)} %copy-done.42), channel_id=1, source_target_pairs={{0,1},{1,0},{2,3},{3,2},{4,5},{5,4},{6,7},{7,6},{8,9},{9,8},{10,11... | collective-permute-start | bytes 3145736 | tf_op jit(solution)/shard_map/ppermute | solution.py:654
  641.3 26.4 %collective-permute-start.54 = (bf16[256,2048]{1,0:T(8,128)(2,1)}, bf16[256,2048]{1,0:T(8,128)(2,1)}, u32[]{:S(2)}, u32[]{:S(2)}) collective-permute-start(bf16[256,2048]{1,0:T(8,128)(2,1)} %add_convert_fusion.4.refs_1_), channel_id=1, source_target_pairs={{0,4},{2,6},{4,0},{6,2},{1,5},{3,7},{5,1},{7,3},{8,12},{10,14},{12... | collective-permute-start | bytes 3145736 | tf_op jit(solution)/shard_map/ppermute | solution.py:654
  651.3 217.1 %reduce-scatter.14.cloned.1.call-start = ((), (), s32[]{:S(2)}) async-start(), calls=%async_computation.14 | async-start | bytes 5242880 | tf_op jit(solution)/shard_map/reduce_scatter | solution.py:768
  655.7 90.3 %collective-permute-start.60 = (bf16[128,2112]{0,1:T(8,128)(2,1)}, bf16[128,2112]{0,1:T(8,128)(2,1)}, u32[]{:S(2)}, u32[]{:S(2)}) collective-permute-start(bf16[128,2112]{0,1:T(8,128)(2,1)} %copy.102), channel_id=1, source_target_pairs={{0,2},{2,0},{4,6},{6,4},{1,3},{3,1},{5,7},{7,5},{8,10},{10,8},{12,... | collective-permute-start | bytes 1622024 | tf_op jit(solution)/shard_map/ppermute | solution.py:654
  656.8 90.7 %collective-permute-start.61 = (bf16[128,2112]{0,1:T(8,128)(2,1)}, bf16[128,2112]{0,1:T(8,128)(2,1)}, u32[]{:S(2)}, u32[]{:S(2)}) collective-permute-start(bf16[128,2112]{0,1:T(8,128)(2,1)} %copy.103), channel_id=1, source_target_pairs={{0,4},{2,6},{4,0},{6,2},{1,5},{3,7},{5,1},{7,3},{8,12},{10,14},{12... | collective-permute-start | bytes 1622024 | tf_op jit(solution)/shard_map/ppermute | solution.py:654
  659.4 90.1 %collective-permute-start.62 = (bf16[128,2112]{0,1:T(8,128)(2,1)}, bf16[128,2112]{0,1:T(8,128)(2,1)}, u32[]{:S(2)}, u32[]{:S(2)}) collective-permute-start(bf16[128,2112]{0,1:T(8,128)(2,1)} %copy.104), channel_id=1, source_target_pairs={{0,6},{2,4},{4,2},{6,0},{1,7},{3,5},{5,3},{7,1},{8,14},{10,12},{12... | collective-permute-start | bytes 1622024 | tf_op jit(solution)/shard_map/ppermute | solution.py:654
  670.2 56.0 %collective-permute-start.57 = (bf16[128,2048]{1,0:T(8,128)(2,1)S(1)}, bf16[128,2048]{1,0:T(8,128)(2,1)}, u32[]{:S(2)}, u32[]{:S(2)}) collective-permute-start(bf16[128,2048]{1,0:T(8,128)(2,1)S(1)} %slice.556.refs_1_), channel_id=1, source_target_pairs={{0,1},{1,0},{2,3},{3,2},{4,5},{5,4},{6,7},{7,6},{8,9},{9,8},{10,11... | collective-permute-start | bytes 1572872 | tf_op jit(solution)/shard_map/ppermute | solution.py:654
  673.2 53.0 %collective-permute-start.58 = (bf16[128,2048]{1,0:T(8,128)(2,1)S(1)}, bf16[128,2048]{1,0:T(8,128)(2,1)}, u32[]{:S(2)}, u32[]{:S(2)}) collective-permute-start(bf16[128,2048]{1,0:T(8,128)(2,1)S(1)} %slice.555.refs_2_), channel_id=1, source_target_pairs={{0,4},{2,6},{4,0},{6,2},{1,5},{3,7},{5,1},{7,3},{8,12},{10,14},{12... | collective-permute-start | bytes 1572872 | tf_op jit(solution)/shard_map/ppermute | solution.py:654
  730.6 22.6 %collective-permute-start.59 = (bf16[256,2048]{1,0:T(8,128)(2,1)S(1)}, bf16[256,2048]{1,0:T(8,128)(2,1)S(1)}, u32[]{:S(2)}, u32[]{:S(2)}) collective-permute-start(bf16[256,2048]{1,0:T(8,128)(2,1)S(1)} %get-tuple-element.267), channel_id=1, source_target_pairs={{0,1},{1,0},{2,3},{3,2},{4,5},{5,4},{6,7},{7,6},{8,9},{9,8},{10,11... | collective-permute-start | bytes 3145736 | tf_op jit(solution)/shard_map/ppermute | solution.py:654
  785.4 47.9 %collective-permute-start.65 = (bf16[512,2048]{1,0:T(8,128)(2,1)}, bf16[512,2048]{1,0:T(8,128)(2,1)}, u32[]{:S(2)}, u32[]{:S(2)}) collective-permute-start(bf16[512,2048]{1,0:T(8,128)(2,1)} %convolution_convert_fusion.4.refs_2_), channel_id=1, source_target_pairs={{0,2},{2,0},{4,6},{6,4},{1,3},{3,1},{5,7},{7,5},{8,10},{10,8},{12,... | collective-permute-start | bytes 6291464 | tf_op jit(solution)/shard_map/ppermute | solution.py:654
  790.7 45.1 %collective-permute-start.63 = (bf16[512,2048]{1,0:T(8,128)(2,1)}, bf16[512,2048]{1,0:T(8,128)(2,1)}, u32[]{:S(2)}, u32[]{:S(2)}) collective-permute-start(bf16[512,2048]{1,0:T(8,128)(2,1)} %convolution_convert_fusion.6.refs_1_), channel_id=1, source_target_pairs={{0,2},{2,0},{4,6},{6,4},{1,3},{3,1},{5,7},{7,5},{8,10},{10,8},{12,... | collective-permute-start | bytes 6291464 | tf_op jit(solution)/shard_map/ppermute | solution.py:654
  811.8 12.4 %collective-permute-start.74 = (f32[100,128]{1,0:T(8,128)S(1)}, f32[100,128]{1,0:T(8,128)S(1)}, u32[]{:S(2)}, u32[]{:S(2)}) collective-permute-start(f32[100,128]{1,0:T(8,128)S(1)} %fusion.92), channel_id=1, source_target_pairs={{0,16},{8,24},{16,0},{24,8},{1,17},{9,25},{17,1},{25,9},{2,18},{10... | collective-permute-start | bytes 153608 | tf_op jit(solution)/shard_map/ppermute | solution.py:654
  835.0 25.6 %collective-permute-start.66 = (bf16[256,2048]{1,0:T(8,128)(2,1)S(1)}, bf16[256,2048]{1,0:T(8,128)(2,1)S(1)}, u32[]{:S(2)}, u32[]{:S(2)}) collective-permute-start(bf16[256,2048]{1,0:T(8,128)(2,1)S(1)} %add_convert_fusion), channel_id=1, source_target_pairs={{0,1},{1,0},{2,3},{3,2},{4,5},{5,4},{6,7},{7,6},{8,9},{9,8},{10,11... | collective-permute-start | bytes 3145736 | tf_op jit(solution)/shard_map/ppermute | solution.py:654
  837.4 25.3 %collective-permute-start.64 = (bf16[256,2048]{1,0:T(8,128)(2,1)S(1)}, bf16[256,2048]{1,0:T(8,128)(2,1)S(1)}, u32[]{:S(2)}, u32[]{:S(2)}) collective-permute-start(bf16[256,2048]{1,0:T(8,128)(2,1)S(1)} %add_convert_fusion.1), channel_id=1, source_target_pairs={{0,4},{2,6},{4,0},{6,2},{1,5},{3,7},{5,1},{7,3},{8,12},{10,14},{12... | collective-permute-start | bytes 3145736 | tf_op jit(solution)/shard_map/ppermute | solution.py:654
  868.0 13.4 %collective-permute-start.68 = (bf16[128,2048]{1,0:T(8,128)(2,1)}, bf16[128,2048]{1,0:T(8,128)(2,1)S(1)}, u32[]{:S(2)}, u32[]{:S(2)}) collective-permute-start(bf16[128,2048]{1,0:T(8,128)(2,1)} %slice.553), channel_id=1, source_target_pairs={{0,4},{2,6},{4,0},{6,2},{1,5},{3,7},{5,1},{7,3},{8,12},{10,14},{12... | collective-permute-start | bytes 1572872 | tf_op jit(solution)/shard_map/ppermute | solution.py:654
  868.3 13.5 %collective-permute-start.67 = (bf16[128,2048]{1,0:T(8,128)(2,1)}, bf16[128,2048]{1,0:T(8,128)(2,1)S(1)}, u32[]{:S(2)}, u32[]{:S(2)}) collective-permute-start(bf16[128,2048]{1,0:T(8,128)(2,1)} %tie.35), channel_id=1, source_target_pairs={{0,1},{1,0},{2,3},{3,2},{4,5},{5,4},{6,7},{7,6},{8,9},{9,8},{10,11... | collective-permute-start | bytes 1572872 | tf_op jit(solution)/shard_map/ppermute | solution.py:654
  887.1 31.0 %collective-permute-start.69 = (bf16[256,2048]{1,0:T(8,128)(2,1)}, bf16[256,2048]{1,0:T(8,128)(2,1)S(1)}, u32[]{:S(2)}, u32[]{:S(2)}) collective-permute-start(bf16[256,2048]{1,0:T(8,128)(2,1)} %get-tuple-element.265), channel_id=1, source_target_pairs={{0,1},{1,0},{2,3},{3,2},{4,5},{5,4},{6,7},{7,6},{8,9},{9,8},{10,11... | collective-permute-start | bytes 3145736 | tf_op jit(solution)/shard_map/ppermute | solution.py:654
  893.0 14.8 %collective-permute-start.71 = (bf16[128,2048]{1,0:T(8,128)(2,1)S(1)}, bf16[128,2048]{1,0:T(8,128)(2,1)S(1)}, u32[]{:S(2)}, u32[]{:S(2)}) collective-permute-start(bf16[128,2048]{1,0:T(8,128)(2,1)S(1)} %get-tuple-element.185), channel_id=1, source_target_pairs={{0,4},{2,6},{4,0},{6,2},{1,5},{3,7},{5,1},{7,3},{8,12},{10,14},{12... | collective-permute-start | bytes 1572872 | tf_op jit(solution)/shard_map/ppermute | solution.py:654
  894.5 23.6 %collective-permute-start.72 = (bf16[128,2048]{1,0:T(8,128)(2,1)S(1)}, bf16[128,2048]{1,0:T(8,128)(2,1)S(1)}, u32[]{:S(2)}, u32[]{:S(2)}) collective-permute-start(bf16[128,2048]{1,0:T(8,128)(2,1)S(1)} %get-tuple-element.186), channel_id=1, source_target_pairs={{0,6},{2,4},{4,2},{6,0},{1,7},{3,5},{5,3},{7,1},{8,14},{10,12},{12... | collective-permute-start | bytes 1572872 | tf_op jit(solution)/shard_map/ppermute | solution.py:654
  (123 other events, 891.7 us)
Sparse Core Ops, SparseCore 0:
  28.4 82.6 all-gather.5
  113.3 82.5 all-gather.7
  197.5 62.0 all-gather.9
  261.0 62.3 all-gather.11
  324.8 62.1 all-gather.13
  454.0 66.2 reduce-scatter.5
  522.6 102.3 reduce-scatter.7
  639.8 48.8 reduce-scatter.9
  691.1 43.0 reduce-scatter.11
  746.2 83.7 reduce-scatter.13
